TPU v7x, 32 devices: a whole 2x2x4 slice. The times are simulated.
32 devices in a mesh: batch: 8 (over z, y), span: 4 (over x, core).
Axes of the slice: x: 2, y: 2, z: 4, core: 2. Of those that a mesh axis runs over, the one named last changes fastest.
Arguments:
- image_embeds: float32 [4096, 768], P(('batch', 'span')), may hold values from -1.2 to 1.2
- text_embeds: float32 [4096, 768], P(('batch', 'span')), may hold values from -1.2 to 1.2
Outputs:
- image_lse: float32 [4096], P(('batch', 'span'))
- text_lse: float32 [4096], P(('batch', 'span'))
- image_grad: float32 [4096, 768], P(('batch', 'span'))
- text_grad: float32 [4096, 768], P(('batch', 'span'))
All inputs are finite; a program needn't handle non-finite values.
Results may differ from a plain program's by a relative error of at most 0.0051.
Values may be sent and summed in bfloat16 or wider, within the bound.
No kernel may reach another device: no remote copies, remote signals or barrier semaphores. Data moves between devices by JAX's collectives and lax.ppermute only.
A program may use at most 64 MiB of HBM per device.

v0:
```python
import jax
import jax.numpy as jnp
from jax import lax
from jax.sharding import PartitionSpec as P

STEPS = 4


LOGIT_SCALE = 5.0
FLOOR_VALUE = -1e30


def passed_along(value, axis, steps):
    count = lax.axis_size(axis)
    pairs = [(source, (source + steps) % count) for source in range(count)]
    return lax.ppermute(value, axis, pairs)


def combined_all(part, axis, combine):
    gathered = jax.tree.map(lambda a: lax.all_gather(a, axis), part)

    def take(source):
        return jax.tree.map(lambda a: lax.dynamic_index_in_dim(a, source, 0, False), gathered)

    return lax.fori_loop(
        1, lax.axis_size(axis), lambda source, state: combine(state, take(source)), take(0)
    )


def tile_scores(images, block):
    return (
        lax.dot_general(images, block, (((1,), (1,)), ((), ())), preferred_element_type=jnp.float32)
        * LOGIT_SCALE
    )


def merge_parts(first, second):
    top = jnp.maximum(first[0], second[0])
    return (top, first[1] * jnp.exp(first[0] - top) + second[1] * jnp.exp(second[0] - top))


def body(image_embeds, text_embeds):
    images = image_embeds.astype(jnp.bfloat16)
    own_text = text_embeds.astype(jnp.bfloat16)
    rows = images.shape[0]
    width = rows * lax.axis_size("span")
    span_pos = lax.axis_index("span")
    row_max = jnp.full((rows,), FLOOR_VALUE, jnp.float32)
    row_total = jnp.zeros((rows,), jnp.float32)
    col_max = jnp.full((width,), FLOOR_VALUE, jnp.float32)
    col_total = jnp.zeros((width,), jnp.float32)
    moving = lax.all_gather(own_text, "span", axis=0, tiled=True)
    kept = []
    for step in range(STEPS):
        if step > 0:
            moving, col_max, col_total = (
                passed_along(moving.astype(jnp.float32), "batch", 1).astype(moving.dtype),
                passed_along(col_max, "batch", 1),
                passed_along(col_total, "batch", 1),
            )
        block = moving
        kept.append(block)
        scores = tile_scores(images, block)
        new_rows = jnp.maximum(row_max, jnp.max(scores, axis=1))
        row_total = row_total * jnp.exp(row_max - new_rows) + jnp.sum(
            jnp.exp(scores - new_rows[:, None]), axis=1
        )
        row_max = new_rows
        tile_max = jnp.max(scores, axis=0)
        tile_total = jnp.sum(jnp.exp(scores - tile_max[None, :]), axis=0)
        col_max, col_total = merge_parts((col_max, col_total), (tile_max, tile_total))
    col_max, col_total = combined_all((col_max, col_total), "span", merge_parts)
    image_lse = row_max + jnp.log(row_total)
    lse_cols = col_max + jnp.log(col_total)
    accum = jnp.zeros((width, images.shape[1]), jnp.float32)
    grad_rows = jnp.zeros((rows, images.shape[1]), jnp.float32)
    carried = moving
    for turn in range(STEPS):
        if turn > 0:
            accum, lse_cols, carried = (
                passed_along(accum, "batch", -1),
                passed_along(lse_cols, "batch", -1),
                passed_along(carried.astype(jnp.float32), "batch", -1).astype(carried.dtype),
            )
        block = carried
        scores = tile_scores(images, block)
        weights = 0.5 * jnp.exp(scores - image_lse[:, None]) + 0.5 * jnp.exp(
            scores - lse_cols[None, :]
        )
        if turn == STEPS - 1:
            columns = lax.broadcasted_iota(jnp.int32, (rows, width), 1)
            row_ids = lax.broadcasted_iota(jnp.int32, (rows, width), 0)
            weights = weights - (columns == row_ids + span_pos * rows).astype(jnp.float32)
        rounded = weights.astype(jnp.bfloat16)
        grad_rows = grad_rows + LOGIT_SCALE * jnp.dot(
            rounded, block, preferred_element_type=jnp.float32
        )
        accum = accum + LOGIT_SCALE * lax.dot_general(
            rounded, images, (((0,), (0,)), ((), ())), preferred_element_type=jnp.float32
        )
    text_grad = lax.psum_scatter(accum, "span", scatter_dimension=0, tiled=True)
    text_lse = lax.dynamic_slice_in_dim(lse_cols, span_pos * rows, rows)
    return (image_lse, text_lse, grad_rows, text_grad)


def solution(mesh):
    in_specs = (P(("batch", "span"), None), P(("batch", "span"), None))
    out_specs = (
        P(("batch", "span")),
        P(("batch", "span")),
        P(("batch", "span"), None),
        P(("batch", "span"), None),
    )
    return jax.shard_map(body, mesh=mesh, in_specs=in_specs, out_specs=out_specs, check_vma=False)
```

profile of v0, /device:TPU:0, one launch (start us, length us, event | category | flops | bytes accessed | tf_op | source)
XLA Modules:
  0.0 321.1 jit_solution(13955451443217144110)
XLA Ops:
  7.2 1.1 convert_element_type.58
  8.3 10.0 %all_gather.15 = bf16[512,768]{1,0:T(8,128)(2,1)S(1)} all-gather(bf16[128,768]{1,0:T(8,128)(2,1)S(1)} %convert_element_type.58), channel_id=1, replica_groups=mesh['batch'=8,'span'=4] {'span'}, dimensions={0}, use_global_device_ids=true | all-gather | bytes 983040 | tf_op jit(solution)/shard_map/all_gather | solution.py:52
  18.3 1.5 collective-permute-start
  19.8 21.1 %collective-permute-done = bf16[512,768]{1,0:T(8,128)(2,1)S(1)} collective-permute-done((bf16[512,768]{1,0:T(8,128)(2,1)S(1)}, bf16[512,768]{1,0:T(8,128)(2,1)S(1)}, u32[]{:S(2)}, u32[]{:S(2)}) %collective-permute-start) | collective-permute-done | bytes 786464 | tf_op jit(solution)/shard_map/ppermute | solution.py:16
  40.9 21.9 %collective-permute-done.1 = bf16[512,768]{1,0:T(8,128)(2,1)} collective-permute-done((bf16[512,768]{1,0:T(8,128)(2,1)S(1)}, bf16[512,768]{1,0:T(8,128)(2,1)}, u32[]{:S(2)}, u32[]{:S(2)}) %collective-permute-start.1) | collective-permute-done | bytes 786464 | tf_op jit(solution)/shard_map/ppermute | solution.py:16
  63.9 1.6 fusion.32
  65.5 18.6 %collective-permute-done.2 = bf16[512,768]{1,0:T(8,128)(2,1)S(1)} collective-permute-done((bf16[512,768]{1,0:T(8,128)(2,1)}, bf16[512,768]{1,0:T(8,128)(2,1)S(1)}, u32[]{:S(2)}, u32[]{:S(2)}) %collective-permute-start.2) | collective-permute-done | bytes 786464 | tf_op jit(solution)/shard_map/ppermute | solution.py:16
  85.2 5.8 %collective-permute-done.3 = f32[512]{0:T(512)S(1)} collective-permute-done((f32[512]{0:T(512)S(1)}, f32[512]{0:T(512)S(1)}, u32[]{:S(2)}, u32[]{:S(2)}) %collective-permute-start.3) | collective-permute-done | bytes 2080 | tf_op jit(solution)/shard_map/ppermute | solution.py:16
  91.4 6.0 %collective-permute-done.7 = f32[512]{0:T(512)S(1)} collective-permute-done((f32[512]{0:T(512)S(1)}, f32[512]{0:T(512)S(1)}, u32[]{:S(2)}, u32[]{:S(2)}) %collective-permute-start.7) | collective-permute-done | bytes 2080 | tf_op jit(solution)/shard_map/ppermute | solution.py:16
  97.7 6.2 %collective-permute-done.8 = f32[512]{0:T(512)S(1)} collective-permute-done((f32[512]{0:T(512)S(1)}, f32[512]{0:T(512)S(1)}, u32[]{:S(2)}, u32[]{:S(2)}) %collective-permute-start.8) | collective-permute-done | bytes 2080 | tf_op jit(solution)/shard_map/ppermute | solution.py:16
  103.9 5.2 %all-gather.2 = f32[4,1,512]{2,1,0:T(1,128)S(1)} all-gather(f32[1,1,512]{2,1,0:T(1,128)S(1)} %bitcast.47), channel_id=2, replica_groups=mesh['batch'=8,'span'=4] {'span'}, dimensions={0}, use_global_device_ids=true | all-gather | bytes 10240 | tf_op jit(solution)/shard_map/all_gather | solution.py:20
  109.1 5.1 %all-gather.3 = f32[4,1,512]{2,1,0:T(1,128)S(1)} all-gather(f32[1,1,512]{2,1,0:T(1,128)S(1)} %bitcast.46), channel_id=3, replica_groups=mesh['batch'=8,'span'=4] {'span'}, dimensions={0}, use_global_device_ids=true | all-gather | bytes 10240 | tf_op jit(solution)/shard_map/all_gather | solution.py:20
  114.9 2.0 collective-permute-start.15
  117.3 51.2 %collective-permute-done.9 = f32[512]{0:T(512)S(1)} collective-permute-done((f32[512]{0:T(512)S(1)}, f32[512]{0:T(512)S(1)}, u32[]{:S(2)}, u32[]{:S(2)}) %collective-permute-start.9) | collective-permute-done | bytes 2080 | tf_op jit(solution)/shard_map/ppermute | solution.py:16
  169.3 4.7 %collective-permute-start.16 = (f32[512,768]{1,0:T(8,128)S(1)}, f32[512,768]{1,0:T(8,128)S(1)}, u32[]{:S(2)}, u32[]{:S(2)}) collective-permute-start(f32[512,768]{1,0:T(8,128)S(1)} %multiply_add_fusion.3), channel_id=1, source_target_pairs={{0,28},{4,0},{8,4},{12,8},{16,12},{20,16},{24,20},{28,24},{1,29},{... | collective-permute-start | bytes 4718600 | tf_op jit(solution)/shard_map/ppermute | solution.py:16
  174.2 50.0 %collective-permute-done.13 = bf16[512,768]{1,0:T(8,128)(2,1)S(1)} collective-permute-done((bf16[512,768]{1,0:T(8,128)(2,1)S(1)}, bf16[512,768]{1,0:T(8,128)(2,1)S(1)}, u32[]{:S(2)}, u32[]{:S(2)}) %collective-permute-start.13) | collective-permute-done | bytes 786464 | tf_op jit(solution)/shard_map/ppermute | solution.py:16
  224.7 1.6 multiply_add_fusion.2
  226.3 5.2 %collective-permute-start.17 = (f32[512,768]{1,0:T(8,128)}, f32[512,768]{1,0:T(8,128)}, u32[]{:S(2)}, u32[]{:S(2)}) collective-permute-start(f32[512,768]{1,0:T(8,128)} %multiply_add_fusion.2), channel_id=1, source_target_pairs={{0,28},{4,0},{8,4},{12,8},{16,12},{20,16},{24,20},{28,24},{1,29},{... | collective-permute-start | bytes 4718600 | tf_op jit(solution)/shard_map/ppermute | solution.py:16
  231.5 49.4 %collective-permute-done.14 = bf16[512,768]{1,0:T(8,128)(2,1)S(1)} collective-permute-done((bf16[512,768]{1,0:T(8,128)(2,1)S(1)}, bf16[512,768]{1,0:T(8,128)(2,1)S(1)}, u32[]{:S(2)}, u32[]{:S(2)}) %collective-permute-start.14) | collective-permute-done | bytes 786464 | tf_op jit(solution)/shard_map/ppermute | solution.py:16
  281.3 3.1 multiply_add_fusion.1
  284.4 0.6 dynamic_slice.32
  285.0 1.4 fusion.37
  287.1 1.1 fusion.2
  288.2 26.1 %reduce-scatter.2.cloned.1.call-done = f32[128,768]{1,0:T(8,128)} async-done(((f32[512,768]{1,0:T(8,128)}), f32[128,768]{1,0:T(8,128)}) %reduce-scatter.2.cloned.1.call-update) | async-done | bytes 393232 | tf_op jit(solution)/shard_map/reduce_scatter | solution.py:101
  (65 shorter events, 6.5 us)
Async XLA Ops:
  7.2 55.7 %copy-start.1 = (f32[128,768]{1,0:T(8,128)S(1)}, f32[128,768]{1,0:T(8,128)}, u32[]{:S(2)}) copy-start(f32[128,768]{1,0:T(8,128)} %param.4) | copy-start | bytes 1179652
  7.2 307.1 %reduce-scatter.2.cloned.1.call-start = ((), (), s32[]{:S(2)}) async-start(), calls=%async_computation.1 | async-start | bytes 1966080 | tf_op jit(solution)/shard_map/reduce_scatter | solution.py:101
  18.3 22.6 %collective-permute-start = (bf16[512,768]{1,0:T(8,128)(2,1)S(1)}, bf16[512,768]{1,0:T(8,128)(2,1)S(1)}, u32[]{:S(2)}, u32[]{:S(2)}) collective-permute-start(bf16[512,768]{1,0:T(8,128)(2,1)S(1)} %all_gather.15), channel_id=1, source_target_pairs={{0,4},{4,8},{8,12},{12,16},{16,20},{20,24},{24,28},{28,0},{1,5},{5... | collective-permute-start | bytes 2359304 | tf_op jit(solution)/shard_map/ppermute | solution.py:16
  40.9 21.9 %collective-permute-start.1 = (bf16[512,768]{1,0:T(8,128)(2,1)S(1)}, bf16[512,768]{1,0:T(8,128)(2,1)}, u32[]{:S(2)}, u32[]{:S(2)}) collective-permute-start(bf16[512,768]{1,0:T(8,128)(2,1)S(1)} %collective-permute-done), channel_id=1, source_target_pairs={{0,4},{4,8},{8,12},{12,16},{16,20},{20,24},{24,28},{28,0},{1,5},{5... | collective-permute-start | bytes 2359304 | tf_op jit(solution)/shard_map/ppermute | solution.py:16
  62.9 21.1 %collective-permute-start.2 = (bf16[512,768]{1,0:T(8,128)(2,1)}, bf16[512,768]{1,0:T(8,128)(2,1)S(1)}, u32[]{:S(2)}, u32[]{:S(2)}) collective-permute-start(bf16[512,768]{1,0:T(8,128)(2,1)} %collective-permute-done.1), channel_id=1, source_target_pairs={{0,4},{4,8},{8,12},{12,16},{16,20},{20,24},{24,28},{28,0},{1,5},{5... | collective-permute-start | bytes 2359304 | tf_op jit(solution)/shard_map/ppermute | solution.py:16
  84.7 6.3 %collective-permute-start.3 = (f32[512]{0:T(512)S(1)}, f32[512]{0:T(512)S(1)}, u32[]{:S(2)}, u32[]{:S(2)}) collective-permute-start(f32[512]{0:T(512)S(1)} %get-tuple-element.178), channel_id=1, source_target_pairs={{0,4},{4,8},{8,12},{12,16},{16,20},{20,24},{24,28},{28,0},{1,5},{5... | collective-permute-start | bytes 6152 | tf_op jit(solution)/shard_map/ppermute | solution.py:16
  84.8 6.3 %collective-permute-start.6 = (f32[512]{0:T(512)S(1)}, f32[512]{0:T(512)S(1)}, u32[]{:S(2)}, u32[]{:S(2)}) collective-permute-start(f32[512]{0:T(512)S(1)} %get-tuple-element.179), channel_id=1, source_target_pairs={{0,4},{4,8},{8,12},{12,16},{16,20},{20,24},{24,28},{28,0},{1,5},{5... | collective-permute-start | bytes 6152 | tf_op jit(solution)/shard_map/ppermute | solution.py:16
  91.1 6.3 %collective-permute-start.7 = (f32[512]{0:T(512)S(1)}, f32[512]{0:T(512)S(1)}, u32[]{:S(2)}, u32[]{:S(2)}) collective-permute-start(f32[512]{0:T(512)S(1)} %get-tuple-element.171), channel_id=1, source_target_pairs={{0,4},{4,8},{8,12},{12,16},{16,20},{20,24},{24,28},{28,0},{1,5},{5... | collective-permute-start | bytes 6152 | tf_op jit(solution)/shard_map/ppermute | solution.py:16
  91.2 6.3 %collective-permute-start.4 = (f32[512]{0:T(512)S(1)}, f32[512]{0:T(512)S(1)}, u32[]{:S(2)}, u32[]{:S(2)}) collective-permute-start(f32[512]{0:T(512)S(1)} %get-tuple-element.172), channel_id=1, source_target_pairs={{0,4},{4,8},{8,12},{12,16},{16,20},{20,24},{24,28},{28,0},{1,5},{5... | collective-permute-start | bytes 6152 | tf_op jit(solution)/shard_map/ppermute | solution.py:16
  97.5 6.3 %collective-permute-start.8 = (f32[512]{0:T(512)S(1)}, f32[512]{0:T(512)S(1)}, u32[]{:S(2)}, u32[]{:S(2)}) collective-permute-start(f32[512]{0:T(512)S(1)} %get-tuple-element.169), channel_id=1, source_target_pairs={{0,4},{4,8},{8,12},{12,16},{16,20},{20,24},{24,28},{28,0},{1,5},{5... | collective-permute-start | bytes 6152 | tf_op jit(solution)/shard_map/ppermute | solution.py:16
  97.6 6.3 %collective-permute-start.5 = (f32[512]{0:T(512)S(1)}, f32[512]{0:T(512)S(1)}, u32[]{:S(2)}, u32[]{:S(2)}) collective-permute-start(f32[512]{0:T(512)S(1)} %get-tuple-element.170), channel_id=1, source_target_pairs={{0,4},{4,8},{8,12},{12,16},{16,20},{20,24},{24,28},{28,0},{1,5},{5... | collective-permute-start | bytes 6152 | tf_op jit(solution)/shard_map/ppermute | solution.py:16
  97.7 189.4 %copy-start.2 = (f32[128]{0:T(128)}, f32[128]{0:T(128)S(1)}, u32[]{:S(2)}) copy-start(f32[128]{0:T(128)S(1)} %log_add_fusion.1) | copy-start | bytes 1540
  114.9 54.0 %collective-permute-start.15 = (f32[512,768]{1,0:T(8,128)S(1)}, f32[512,768]{1,0:T(8,128)S(1)}, u32[]{:S(2)}, u32[]{:S(2)}) collective-permute-start(f32[512,768]{1,0:T(8,128)S(1)} %convolution_multiply_fusion), channel_id=1, source_target_pairs={{0,28},{4,0},{8,4},{12,8},{16,12},{20,16},{24,20},{28,24},{1,29},{... | collective-permute-start | bytes 4718600 | tf_op jit(solution)/shard_map/ppermute | solution.py:16
  117.0 51.5 %collective-permute-start.12 = (bf16[512,768]{1,0:T(8,128)(2,1)S(1)}, bf16[512,768]{1,0:T(8,128)(2,1)S(1)}, u32[]{:S(2)}, u32[]{:S(2)}) collective-permute-start(bf16[512,768]{1,0:T(8,128)(2,1)S(1)} %collective-permute-done.2), channel_id=1, source_target_pairs={{0,28},{4,0},{8,4},{12,8},{16,12},{20,16},{24,20},{28,24},{1,29},{... | collective-permute-start | bytes 2359304 | tf_op jit(solution)/shard_map/ppermute | solution.py:16
  117.1 51.4 %collective-permute-start.9 = (f32[512]{0:T(512)S(1)}, f32[512]{0:T(512)S(1)}, u32[]{:S(2)}, u32[]{:S(2)}) collective-permute-start(f32[512]{0:T(512)S(1)} %log_add_fusion), channel_id=1, source_target_pairs={{0,28},{4,0},{8,4},{12,8},{16,12},{20,16},{24,20},{28,24},{1,29},{... | collective-permute-start | bytes 6152 | tf_op jit(solution)/shard_map/ppermute | solution.py:16
  168.5 5.6 %copy-start = (bf16[512,768]{1,0:T(8,128)(2,1)}, bf16[512,768]{1,0:T(8,128)(2,1)S(1)}, u32[]{:S(2)}) copy-start(bf16[512,768]{1,0:T(8,128)(2,1)S(1)} %collective-permute-done.12) | copy-start | bytes 2359300
  169.3 55.3 %collective-permute-start.16 = (f32[512,768]{1,0:T(8,128)S(1)}, f32[512,768]{1,0:T(8,128)S(1)}, u32[]{:S(2)}, u32[]{:S(2)}) collective-permute-start(f32[512,768]{1,0:T(8,128)S(1)} %multiply_add_fusion.3), channel_id=1, source_target_pairs={{0,28},{4,0},{8,4},{12,8},{16,12},{20,16},{24,20},{28,24},{1,29},{... | collective-permute-start | bytes 4718600 | tf_op jit(solution)/shard_map/ppermute | solution.py:16
  174.1 50.2 %collective-permute-start.13 = (bf16[512,768]{1,0:T(8,128)(2,1)S(1)}, bf16[512,768]{1,0:T(8,128)(2,1)S(1)}, u32[]{:S(2)}, u32[]{:S(2)}) collective-permute-start(bf16[512,768]{1,0:T(8,128)(2,1)S(1)} %collective-permute-done.12), channel_id=1, source_target_pairs={{0,28},{4,0},{8,4},{12,8},{16,12},{20,16},{24,20},{28,24},{1,29},{... | collective-permute-start | bytes 2359304 | tf_op jit(solution)/shard_map/ppermute | solution.py:16
  174.1 50.5 %collective-permute-start.10 = (f32[512]{0:T(512)S(1)}, f32[512]{0:T(512)S(1)}, u32[]{:S(2)}, u32[]{:S(2)}) collective-permute-start(f32[512]{0:T(512)S(1)} %collective-permute-done.9), channel_id=1, source_target_pairs={{0,28},{4,0},{8,4},{12,8},{16,12},{20,16},{24,20},{28,24},{1,29},{... | collective-permute-start | bytes 6152 | tf_op jit(solution)/shard_map/ppermute | solution.py:16
  226.3 55.0 %collective-permute-start.17 = (f32[512,768]{1,0:T(8,128)}, f32[512,768]{1,0:T(8,128)}, u32[]{:S(2)}, u32[]{:S(2)}) collective-permute-start(f32[512,768]{1,0:T(8,128)} %multiply_add_fusion.2), channel_id=1, source_target_pairs={{0,28},{4,0},{8,4},{12,8},{16,12},{20,16},{24,20},{28,24},{1,29},{... | collective-permute-start | bytes 4718600 | tf_op jit(solution)/shard_map/ppermute | solution.py:16
  231.5 49.4 %collective-permute-start.14 = (bf16[512,768]{1,0:T(8,128)(2,1)S(1)}, bf16[512,768]{1,0:T(8,128)(2,1)S(1)}, u32[]{:S(2)}, u32[]{:S(2)}) collective-permute-start(bf16[512,768]{1,0:T(8,128)(2,1)S(1)} %collective-permute-done.13), channel_id=1, source_target_pairs={{0,28},{4,0},{8,4},{12,8},{16,12},{20,16},{24,20},{28,24},{1,29},{... | collective-permute-start | bytes 2359304 | tf_op jit(solution)/shard_map/ppermute | solution.py:16
  231.5 49.8 %collective-permute-start.11 = (f32[512]{0:T(512)S(1)}, f32[512]{0:T(512)S(1)}, u32[]{:S(2)}, u32[]{:S(2)}) collective-permute-start(f32[512]{0:T(512)S(1)} %collective-permute-done.10), channel_id=1, source_target_pairs={{0,28},{4,0},{8,4},{12,8},{16,12},{20,16},{24,20},{28,24},{1,29},{... | collective-permute-start | bytes 6152 | tf_op jit(solution)/shard_map/ppermute | solution.py:16
Sparse Core Ops, SparseCore 0:
  284.5 29.6 reduce-scatter.1
where the time goes:
time: 321 us
  waiting for transfers between devices  256 us (80%)
  blocking collectives  20.4 us (6%)
  starting transfers between devices  14.4 us (4%)
  between operations  14.3 us (4%)
  matrix products  12.9 us (4%)
    ppermute x18, waiting for transfers between devices, passed_along(): return lax.ppermute(value, axis, pairs)  230 us
    reduce_scatter x1, waiting for transfers between devices, body(): text_grad = lax.psum_scatter(accum, 'span', scatter_dimension=0, tiled=True)  26.1 us
    ppermute x18, starting transfers between devices, passed_along(): return lax.ppermute(value, axis, pairs)  14.3 us
    all_gather x2, blocking collectives, combined_all(): gathered = jax.tree.map(lambda a: lax.all_gather(a, axis), part)  10.3 us
    all_gather x1, blocking collectives, body(): moving = lax.all_gather(own_text, 'span', axis=0, tiled=True)  10 us
  transfers between devices with their start and end apart: 19, of which 13 were waited for; matrix products, arithmetic and copies ran while one was open for 3% of the time, Pallas kernels for 0%

commit v1 on v0

v1 whole, which is shorter than its diff:
```python
import jax
import jax.numpy as jnp
from jax import lax
from jax.sharding import PartitionSpec as P

STEPS = 4
LOGIT_SCALE = 5.0
AXES = ("batch", "span")


def moved(value, target):
    count, spans = lax.axis_size("batch"), lax.axis_size("span")
    pairs = []
    for b in range(count):
        for s in range(spans):
            to_b, to_s = target(b, s)
            pairs.append((b * spans + s, (to_b % count) * spans + to_s))
    return lax.ppermute(value, AXES, pairs)


def over_core(value):
    return moved(value, lambda b, s: (b, s ^ 1))


def over_x(value):
    return moved(value, lambda b, s: (b, s ^ 2))


def along(value, steps):
    return moved(value, lambda b, s: (b + steps, s))


def scores_of(rows, cols):
    return (
        lax.dot_general(rows, cols, (((1,), (1,)), ((), ())), preferred_element_type=jnp.float32)
        * LOGIT_SCALE
    )


def partial_lse(rows, cols):
    scores = [scores_of(rows, col) for col in cols]
    top = scores[0].max(axis=1)
    for s in scores[1:]:
        top = jnp.maximum(top, s.max(axis=1))
    total = 0.0
    for s in scores:
        total = total + jnp.sum(jnp.exp(s - top[:, None]), axis=1)
    return top + jnp.log(total)


def relative(pieces, span_pos):
    shape = pieces.shape
    p = pieces.reshape(shape[:-2] + (2, 2) + shape[-1:])
    p = jnp.where(span_pos // 2 == 1, jnp.flip(p, -3), p)
    p = jnp.where(span_pos % 2 == 1, jnp.flip(p, -2), p)
    return p.reshape(shape)


def gradient(rows, cols, row_lse, col_lse):
    total = 0.0
    for k, (col, lse) in enumerate(zip(cols, col_lse)):
        s = scores_of(rows, col)
        w = 0.5 * jnp.exp(s - row_lse[:, None]) + 0.5 * jnp.exp(s - lse[None, :])
        if k == 0:
            n = rows.shape[0] // 2
            i = lax.broadcasted_iota(jnp.int32, s.shape, 0)
            j = lax.broadcasted_iota(jnp.int32, s.shape, 1)
            w = w - ((i == j) & (i < n)).astype(jnp.float32)
        w = w.astype(jnp.bfloat16)
        total = total + LOGIT_SCALE * jnp.dot(w, col, preferred_element_type=jnp.float32)
    return total


def all_lse(part):
    count, spans = lax.axis_size("batch"), lax.axis_size("span")
    n = part.shape[-1]
    send = jnp.broadcast_to(part[None], (count * spans,) + part.shape)
    got = lax.all_to_all(send, AXES, 0, 0, tiled=True).reshape((count, spans) + part.shape)
    out = []
    for piece in range(4):
        terms = [got[:, s, :, piece ^ s] for s in range(4)]
        top = jnp.maximum(jnp.maximum(terms[0], terms[1]), jnp.maximum(terms[2], terms[3]))
        out.append(top + jnp.log(sum(jnp.exp(t - top) for t in terms)))
    return jnp.stack(out, 2)


def body(image_embeds, text_embeds):
    i0 = image_embeds.astype(jnp.bfloat16)
    t0 = text_embeds.astype(jnp.bfloat16)
    rows = i0.shape[0]
    pos = lax.axis_index("span")
    b = lax.axis_index("batch")
    texts = [t0] + [along(t0, k) for k in range(1, STEPS)]
    images = [i0] + [along(i0, -k) for k in range(1, STEPS)]
    texts_x = [over_x(v) for v in texts]
    images_x = [over_x(v) for v in images]
    ct0, ci0 = over_core(t0), over_core(i0)
    cxt0, cxi0 = over_core(texts_x[0]), over_core(images_x[0])
    image_rows = jnp.concatenate([i0, ci0, images_x[0], cxi0])
    text_rows = jnp.concatenate([t0, ct0, texts_x[0], cxt0])
    part = jnp.stack([partial_lse(image_rows, texts), partial_lse(text_rows, images)])
    lse = relative(all_lse(part.reshape(2, 4, rows)), pos)
    count = lse.shape[0]
    around = jnp.concatenate([lse, lse])
    image_lses = lax.dynamic_slice_in_dim(around[:, 0], b, STEPS)
    text_lses = lax.dynamic_slice_in_dim(around[:, 1], b + count - (STEPS - 1), STEPS)[::-1]
    own_image = image_lses[0, :2].reshape(2 * rows)
    own_text = text_lses[0, :2].reshape(2 * rows)

    def cols(a, ax):
        return [jnp.concatenate([v, w]) for v, w in zip(a, ax)]

    def col_lse(l):
        return [jnp.concatenate([l[k, 0], l[k, 2]]) for k in range(STEPS)]

    grad_i = gradient(image_rows[: 2 * rows], cols(texts, texts_x), own_image, col_lse(text_lses))
    grad_t = gradient(text_rows[: 2 * rows], cols(images, images_x), own_text, col_lse(image_lses))
    image_grad = grad_i[:rows] + over_core(grad_i[rows:])
    text_grad = grad_t[:rows] + over_core(grad_t[rows:])
    return (own_image[:rows], own_text[:rows], image_grad, text_grad)


def solution(mesh):
    in_specs = (P(("batch", "span"), None), P(("batch", "span"), None))
    out_specs = (
        P(("batch", "span")),
        P(("batch", "span")),
        P(("batch", "span"), None),
        P(("batch", "span"), None),
    )
    return jax.shard_map(body, mesh=mesh, in_specs=in_specs, out_specs=out_specs, check_vma=False)
```

time: 321 us -> 88.7 us (0.28)
  waiting for transfers between devices: 256 us -> 16.6 us
  blocking collectives: 20.4 us -> 0 us
  starting transfers between devices: 14.4 us -> 30.9 us
  between operations: 14.3 us -> 1.34 us
  local copies, waits for them, and re-layouts: 0.64 us -> 13.6 us
  matrix products: 12.9 us -> 21.3 us
    ppermute x18 -> x20, waiting for transfers between devices: 230 us -> 16.6 us  [moved(): return lax.ppermute(value, AXES, pairs)]
    reduce_scatter x1 -> x0, waiting for transfers between devices: 26.1 us -> none  [body(): text_grad = lax.psum_scatter(accum, 'span', scatter_dimension=0, tiled=True)]
    all_gather x3 -> x0, blocking collectives: 20.4 us -> none  [the longest x2 10.3 us: combined_all(): gathered = jax.tree.map(lambda a: lax.all_gather(a, axis), part)]
    ppermute x18 -> x20, starting transfers between devices: 14.3 us -> 27.6 us  [moved(): return lax.ppermute(value, AXES, pairs)]
    dot_general x15 -> x16, matrix products: 12.9 us -> 21.3 us  [the longest x8 12.5 us: gradient(): jnp.dot(w, col, preferred_element_type=jnp.float32)]
    unnamed x8 -> x49, local copies, waits for them, and re-layouts: 0.02 us -> 6.62 us
    concatenate x0 -> x7, local copies, waits for them, and re-layouts: none -> 4.74 us  [the longest x6 4.72 us: cols(): return [jnp.concatenate([v, w]) for v, w in zip(a, ax)]]
    all_to_all x0 -> x1, starting transfers between devices: none -> 3.3 us  [all_lse(): lax.all_to_all(send, AXES, 0, 0, tiled=True)]
  transfers between devices with their start and end apart: 19 -> 21, of which waited for: 13 -> 5; matrix products, arithmetic and copies ran while one was open for 3% -> 32% of each run, Pallas kernels for 0% -> 0%
where the time goes in v1:
time: 88.7 us; the launch traced here: 87.9 us
  starting transfers between devices  30.9 us (35%)
  matrix products  21.3 us (24%)
  waiting for transfers between devices  16.6 us (19%)
  local copies, waits for them, and re-layouts  13.6 us (15%)
  other arithmetic  4.23 us (5%)
  between operations  1.34 us (2%)
    ppermute x20, starting transfers between devices, moved(): return lax.ppermute(value, AXES, pairs)  27.6 us
    ppermute x20, waiting for transfers between devices, moved(): return lax.ppermute(value, AXES, pairs)  16.6 us
    dot_general x8, matrix products, gradient(): jnp.dot(w, col, preferred_element_type=jnp.float32)  12.5 us
    dot_general x8, matrix products, scores_of(): lax.dot_general(rows, cols, (((1,), (1,)), ((), ())), preferred_element_t...  8.81 us
    unnamed x49, local copies, waits for them, and re-layouts  6.62 us
    concatenate x6, local copies, waits for them, and re-layouts, cols(): return [jnp.concatenate([v, w]) for v, w in zip(a, ax)]  4.72 us
    all_to_all x1, starting transfers between devices, all_lse(): lax.all_to_all(send, AXES, 0, 0, tiled=True)  3.3 us
    add x1, other arithmetic, body(): text_grad = grad_t[:rows] + over_core(grad_t[rows:])  1.78 us
  transfers between devices with their start and end apart: 21, of which 5 were waited for; matrix products, arithmetic and copies ran while one was open for 32% of the time, Pallas kernels for 0%

profile of v1, /device:TPU:0, one launch (start us, length us, event | category | flops | bytes accessed | tf_op | source)
XLA Modules:
  0.0 87.9 jit_solution(14570395349778847322)
XLA Ops:
  1.7 6.1 %collective-permute-start.9 = (bf16[128,768]{1,0:T(8,128)(2,1)S(1)}, bf16[128,768]{1,0:T(8,128)(2,1)}, u32[]{:S(2)}, u32[]{:S(2)}) collective-permute-start(bf16[128,768]{1,0:T(8,128)(2,1)S(1)} %convert_element_type.36), channel_id=1, source_target_pairs={{0,28},{1,29},{2,30},{3,31},{4,0},{5,1},{6,2},{7,3},{8,4},{9,5},{1... | collective-permute-start | bytes 589832 | tf_op jit(solution)/shard_map/ppermute | solution.py:18
  7.8 1.5 %collective-permute-start.1 = (bf16[128,768]{1,0:T(8,128)(2,1)S(1)}, bf16[128,768]{1,0:T(8,128)(2,1)S(1)}, u32[]{:S(2)}, u32[]{:S(2)}) collective-permute-start(bf16[128,768]{1,0:T(8,128)(2,1)S(1)} %convert_element_type.36), channel_id=1, source_target_pairs={{0,2},{1,3},{2,0},{3,1},{4,6},{5,7},{6,4},{7,5},{8,10},{9,11},{10,... | collective-permute-start | bytes 589832 | tf_op jit(solution)/shard_map/ppermute | solution.py:18
  9.8 3.3 %collective-permute-done.9 = bf16[128,768]{1,0:T(8,128)(2,1)} collective-permute-done((bf16[128,768]{1,0:T(8,128)(2,1)S(1)}, bf16[128,768]{1,0:T(8,128)(2,1)}, u32[]{:S(2)}, u32[]{:S(2)}) %collective-permute-start.9) | collective-permute-done | bytes 196640 | tf_op jit(solution)/shard_map/ppermute | solution.py:18
  13.1 1.4 %collective-permute-start.5 = (bf16[128,768]{1,0:T(8,128)(2,1)S(1)}, bf16[128,768]{1,0:T(8,128)(2,1)}, u32[]{:S(2)}, u32[]{:S(2)}) collective-permute-start(bf16[128,768]{1,0:T(8,128)(2,1)S(1)} %convert_element_type.37), channel_id=1, source_target_pairs={{0,12},{1,13},{2,14},{3,15},{4,16},{5,17},{6,18},{7,19},{8,20},{9,... | collective-permute-start | bytes 589832 | tf_op jit(solution)/shard_map/ppermute | solution.py:18
  15.5 6.1 %collective-permute-done.11 = bf16[128,768]{1,0:T(8,128)(2,1)} collective-permute-done((bf16[128,768]{1,0:T(8,128)(2,1)S(1)}, bf16[128,768]{1,0:T(8,128)(2,1)}, u32[]{:S(2)}, u32[]{:S(2)}) %collective-permute-start.11) | collective-permute-done | bytes 196640 | tf_op jit(solution)/shard_map/ppermute | solution.py:18
  21.5 8.7 %collective-permute-start.3 = (bf16[128,768]{1,0:T(8,128)(2,1)S(1)}, bf16[128,768]{1,0:T(8,128)(2,1)}, u32[]{:S(2)}, u32[]{:S(2)}) collective-permute-start(bf16[128,768]{1,0:T(8,128)(2,1)S(1)} %convert_element_type.37), channel_id=1, source_target_pairs={{0,4},{1,5},{2,6},{3,7},{4,8},{5,9},{6,10},{7,11},{8,12},{9,13},{1... | collective-permute-start | bytes 589832 | tf_op jit(solution)/shard_map/ppermute | solution.py:18
  30.2 1.6 %constant_dynamic-update-slice_fusion.13 = bf16[256,768]{1,0:T(8,128)(2,1)} fusion(bf16[128,768]{1,0:T(8,128)(2,1)} %collective-permute-done.11), kind=kLoop, calls=%fused_computation.106 | loop fusion | bytes 393216
  32.8 2.5 %collective-permute-done.3 = bf16[128,768]{1,0:T(8,128)(2,1)} collective-permute-done((bf16[128,768]{1,0:T(8,128)(2,1)S(1)}, bf16[128,768]{1,0:T(8,128)(2,1)}, u32[]{:S(2)}, u32[]{:S(2)}) %collective-permute-start.3) | collective-permute-done | bytes 196640 | tf_op jit(solution)/shard_map/ppermute | solution.py:18
  35.4 1.5 %collective-permute-start.7 = (bf16[128,768]{1,0:T(8,128)(2,1)S(1)}, bf16[128,768]{1,0:T(8,128)(2,1)S(1)}, u32[]{:S(2)}, u32[]{:S(2)}) collective-permute-start(bf16[128,768]{1,0:T(8,128)(2,1)S(1)} %convert_element_type.37), channel_id=1, source_target_pairs={{0,2},{1,3},{2,0},{3,1},{4,6},{5,7},{6,4},{7,5},{8,10},{9,11},{10,... | collective-permute-start | bytes 589832 | tf_op jit(solution)/shard_map/ppermute | solution.py:18
  38.4 1.6 %constant_dynamic-update-slice_fusion.7 = bf16[256,768]{1,0:T(8,128)(2,1)} fusion(bf16[128,768]{1,0:T(8,128)(2,1)} %collective-permute-done.5), kind=kLoop, calls=%fused_computation.100 | loop fusion | bytes 393216
  46.1 1.3 %fusion.87 = (f32[512]{0:T(512)S(1)}, f32[512,128]{0,1:T(8,128)S(1)}) fusion(bf16[128,768]{1,0:T(8,128)(2,1)S(1)} %convert_element_type.37, bf16[128,768]{1,0:T(8,128)(2,1)S(1)} %collective-permute-done.2, bf16[128,768]{1,0:T(8,128)(2,1)} %copy-done.16, bf16[128,768]{1,0:T(8,128)(2,1)S(1)} %collective-permute-done, ...), kind=kOutput, calls=%fused_computation.191 | convolution fusion | flops 103939584 | bytes 1247232 | tf_op jit(solution)/shard_map/dot_general | solution.py:35
  50.8 1.3 %fusion.82 = (f32[512]{0:T(512)S(1)}, f32[512,128]{0,1:T(8,128)S(1)}) fusion(bf16[128,768]{1,0:T(8,128)(2,1)} %collective-permute-done.10, bf16[128,768]{1,0:T(8,128)(2,1)S(1)} %collective-permute-done.8, bf16[128,768]{1,0:T(8,128)(2,1)S(1)} %collective-permute-done.7, bf16[128,768]{1,0:T(8,128)(2,1)S(1)} %collective-permute-done.6, ...), kind=kOutput, calls=%fused_computation.186 | convolution fusion | flops 103939584 | bytes 1247232 | tf_op jit(solution)/shard_map/dot_general | solution.py:35
  55.0 3.3 %all-to-all-start = ((f32[32,2,4,128]{3,2,1,0:T(4,128)}), f32[32,2,4,128]{3,2,1,0:T(4,128)S(1)}, u32[]{:S(2)}, u32[]{:S(2)}) async-start(f32[32,2,4,128]{3,2,1,0:T(4,128)} %broadcast_in_dim.5), calls=%async_computation | async-start | bytes 262144 | tf_op jit(solution)/shard_map/all_to_all | solution.py:78
  58.4 1.8 %collective-permute-start.13 = (bf16[128,768]{1,0:T(8,128)(2,1)S(1)}, bf16[128,768]{1,0:T(8,128)(2,1)S(1)}, u32[]{:S(2)}, u32[]{:S(2)}) collective-permute-start(bf16[128,768]{1,0:T(8,128)(2,1)S(1)} %copy-done.2), channel_id=1, source_target_pairs={{0,2},{1,3},{2,0},{3,1},{4,6},{5,7},{6,4},{7,5},{8,10},{9,11},{10,... | collective-permute-start | bytes 589832 | tf_op jit(solution)/shard_map/ppermute | solution.py:18
  64.0 2.0 %collective-permute-done.14 = bf16[128,768]{1,0:T(8,128)(2,1)} collective-permute-done((bf16[128,768]{1,0:T(8,128)(2,1)}, bf16[128,768]{1,0:T(8,128)(2,1)}, u32[]{:S(2)}, u32[]{:S(2)}) %collective-permute-start.14) | collective-permute-done | bytes 196640 | tf_op jit(solution)/shard_map/ppermute | solution.py:18
  67.0 2.6 %collective-permute-done.13 = bf16[128,768]{1,0:T(8,128)(2,1)S(1)} collective-permute-done((bf16[128,768]{1,0:T(8,128)(2,1)S(1)}, bf16[128,768]{1,0:T(8,128)(2,1)S(1)}, u32[]{:S(2)}, u32[]{:S(2)}) %collective-permute-start.13) | collective-permute-done | bytes 196640 | tf_op jit(solution)/shard_map/ppermute | solution.py:18
  71.2 1.6 %fusion.7 = f32[256,768]{1,0:T(8,128)} fusion(bf16[128,768]{1,0:T(8,128)(2,1)S(1)} %convert_element_type.36, bf16[128,768]{1,0:T(8,128)(2,1)S(1)} %copy-done.17, f32[256]{0:T(256)S(1)} %pad_maximum_fusion.15, f32[256]{0:T(256)S(1)} %slice_bitcast_fusion, pred[256]{0:T(512)(128)(4,1)S(1)} %iota_compare_fusion.1, ...), kind=kOutput, calls=%fused_computation.40 | convolution fusion | flops 204341248 | bytes 1575168 | tf_op jit(solution)/shard_map/dot_general | solution.py:70
  72.8 1.5 %fusion.6 = f32[256,768]{1,0:T(8,128)} fusion(bf16[256,768]{1,0:T(8,128)(2,1)S(1)} %constant_dynamic-update-slice_fusion.12, f32[256]{0:T(256)S(1)} %pad_maximum_fusion.18, f32[256]{0:T(256)S(1)} %slice_bitcast_fusion, bf16[128,768]{1,0:T(8,128)(2,1)S(1)} %convert_element_type.37, bf16[128,768]{1,0:T(8,128)(2,1)S(1)} %collective-permute-done.6), kind=kOutput, calls=%fused_computation.37 | convolution fusion | flops 202506240 | bytes 1574912 | tf_op jit(solution)/shard_map/dot_general | solution.py:70
  74.3 1.8 %convolution_add_fusion.1 = f32[256,768]{1,0:T(8,128)S(1)} fusion(f32[256,768]{1,0:T(8,128)} %fusion.7, bf16[256,768]{1,0:T(8,128)(2,1)S(1)} %constant_dynamic-update-slice_fusion.8, f32[256]{0:T(256)S(1)} %pad_maximum_fusion.16, f32[256]{0:T(256)S(1)} %slice_bitcast_fusion, bf16[128,768]{1,0:T(8,128)(2,1)S(1)} %convert_element_type.37, ...), kind=kOutput, calls=%fused_computation.3 | convolution fusion | flops 202702848 | bytes 2361344 | tf_op jit(solution)/shard_map/dot_general | solution.py:70
  76.1 1.8 %fusion.1 = f32[256,768]{1,0:T(8,128)S(1)} fusion(f32[256,768]{1,0:T(8,128)} %fusion.6, f32[256,768]{1,0:T(8,128)S(1)} %convolution_add_fusion.1, bf16[256,768]{1,0:T(8,128)(2,1)S(1)} %constant_dynamic-update-slice_fusion.10, f32[256]{0:T(256)S(1)} %pad_maximum_fusion.17, f32[256]{0:T(256)S(1)} %slice_bitcast_fusion, ...), kind=kOutput, calls=%fused_computation.2 | convolution fusion | flops 203096064 | bytes 3147776 | tf_op jit(solution)/shard_map/dot_general | solution.py:70
  78.9 1.7 %fusion.9 = f32[256,768]{1,0:T(8,128)S(1)} fusion(bf16[128,768]{1,0:T(8,128)(2,1)S(1)} %convert_element_type.37, bf16[128,768]{1,0:T(8,128)(2,1)} %copy-done.18, f32[256]{0:T(256)S(1)} %pad_maximum_fusion.11, f32[256]{0:T(256)S(1)} %slice_bitcast_fusion.1, pred[256]{0:T(512)(128)(4,1)S(1)} %copy-done.20, bf16[128,768]{1,0:T(8,128)(2,1)S(1)} %convert_element_type.36, ...), kind=kOutput, calls=%fused_computation.46 | convolution fusion | flops 204341248 | bytes 1575168 | tf_op jit(solution)/shard_map/dot_general | solution.py:70
  80.7 1.5 %fusion.8 = f32[256,768]{1,0:T(8,128)} fusion(bf16[256,768]{1,0:T(8,128)(2,1)S(1)} %copy-done.6, f32[256]{0:T(256)S(1)} %pad_maximum_fusion.14, f32[256]{0:T(256)S(1)} %slice_bitcast_fusion.1, bf16[128,768]{1,0:T(8,128)(2,1)S(1)} %convert_element_type.36, bf16[128,768]{1,0:T(8,128)(2,1)S(1)} %collective-permute-done), kind=kOutput, calls=%fused_computation.42 | convolution fusion | flops 202506240 | bytes 1574912 | tf_op jit(solution)/shard_map/dot_general | solution.py:70
  82.9 1.8 %fusion.3 = f32[256,768]{1,0:T(8,128)S(1)} fusion(f32[256,768]{1,0:T(8,128)} %fusion.8, f32[256,768]{1,0:T(8,128)S(1)} %convolution_add_fusion.3, bf16[256,768]{1,0:T(8,128)(2,1)S(1)} %constant_dynamic-update-slice_fusion.4, f32[256]{0:T(256)S(1)} %pad_maximum_fusion.13, f32[256]{0:T(256)S(1)} %slice_bitcast_fusion.1, ...), kind=kOutput, calls=%fused_computation.6 | convolution fusion | flops 203096064 | bytes 3147776 | tf_op jit(solution)/shard_map/dot_general | solution.py:70
  85.3 1.8 %slice_add_fusion = f32[128,768]{1,0:T(8,128)} fusion(f32[128,768]{1,0:T(8,128)} %collective-permute-done.19, f32[256,768]{1,0:T(8,128)S(1)} %fusion.1), kind=kLoop, calls=%fused_computation.30 | loop fusion | flops 98304 | bytes 1179648 | tf_op jit(solution)/shard_map/add | solution.py:119
  (128 shorter events, 26.2 us)
Async XLA Ops:
  0.6 9.1 %copy-start = (f32[128,768]{1,0:T(8,128)S(1)}, f32[128,768]{1,0:T(8,128)}, u32[]{:S(2)}) copy-start(f32[128,768]{1,0:T(8,128)} %param.3) | copy-start | bytes 1179652
  1.7 11.4 %collective-permute-start.9 = (bf16[128,768]{1,0:T(8,128)(2,1)S(1)}, bf16[128,768]{1,0:T(8,128)(2,1)}, u32[]{:S(2)}, u32[]{:S(2)}) collective-permute-start(bf16[128,768]{1,0:T(8,128)(2,1)S(1)} %convert_element_type.36), channel_id=1, source_target_pairs={{0,28},{1,29},{2,30},{3,31},{4,0},{5,1},{6,2},{7,3},{8,4},{9,5},{1... | collective-permute-start | bytes 589832 | tf_op jit(solution)/shard_map/ppermute | solution.py:18
  7.8 30.0 %collective-permute-start.1 = (bf16[128,768]{1,0:T(8,128)(2,1)S(1)}, bf16[128,768]{1,0:T(8,128)(2,1)S(1)}, u32[]{:S(2)}, u32[]{:S(2)}) collective-permute-start(bf16[128,768]{1,0:T(8,128)(2,1)S(1)} %convert_element_type.36), channel_id=1, source_target_pairs={{0,2},{1,3},{2,0},{3,1},{4,6},{5,7},{6,4},{7,5},{8,10},{9,11},{10,... | collective-permute-start | bytes 589832 | tf_op jit(solution)/shard_map/ppermute | solution.py:18
  9.3 31.6 %collective-permute-start = (bf16[128,768]{1,0:T(8,128)(2,1)S(1)}, bf16[128,768]{1,0:T(8,128)(2,1)S(1)}, u32[]{:S(2)}, u32[]{:S(2)}) collective-permute-start(bf16[128,768]{1,0:T(8,128)(2,1)S(1)} %convert_element_type.36), channel_id=1, source_target_pairs={{0,1},{1,0},{2,3},{3,2},{4,5},{5,4},{6,7},{7,6},{8,9},{9,8},{10,11... | collective-permute-start | bytes 589832 | tf_op jit(solution)/shard_map/ppermute | solution.py:18
  9.3 22.6 %collective-permute-start.10 = (bf16[128,768]{1,0:T(8,128)(2,1)S(1)}, bf16[128,768]{1,0:T(8,128)(2,1)}, u32[]{:S(2)}, u32[]{:S(2)}) collective-permute-start(bf16[128,768]{1,0:T(8,128)(2,1)S(1)} %convert_element_type.36), channel_id=1, source_target_pairs={{0,24},{1,25},{2,26},{3,27},{4,28},{5,29},{6,30},{7,31},{8,0},{9,1... | collective-permute-start | bytes 589832 | tf_op jit(solution)/shard_map/ppermute | solution.py:18
  9.7 11.8 %collective-permute-start.11 = (bf16[128,768]{1,0:T(8,128)(2,1)S(1)}, bf16[128,768]{1,0:T(8,128)(2,1)}, u32[]{:S(2)}, u32[]{:S(2)}) collective-permute-start(bf16[128,768]{1,0:T(8,128)(2,1)S(1)} %convert_element_type.36), channel_id=1, source_target_pairs={{0,20},{1,21},{2,22},{3,23},{4,24},{5,25},{6,26},{7,27},{8,28},{9,... | collective-permute-start | bytes 589832 | tf_op jit(solution)/shard_map/ppermute | solution.py:18
  9.8 61.4 %copy-start.19 = (pred[256]{0:T(512)(128)(4,1)}, pred[256]{0:T(512)(128)(4,1)S(1)}, u32[]{:S(2)}) copy-start(pred[256]{0:T(512)(128)(4,1)S(1)} %iota_compare_fusion.1) | copy-start | bytes 772
  13.1 24.8 %collective-permute-start.5 = (bf16[128,768]{1,0:T(8,128)(2,1)S(1)}, bf16[128,768]{1,0:T(8,128)(2,1)}, u32[]{:S(2)}, u32[]{:S(2)}) collective-permute-start(bf16[128,768]{1,0:T(8,128)(2,1)S(1)} %convert_element_type.37), channel_id=1, source_target_pairs={{0,12},{1,13},{2,14},{3,15},{4,16},{5,17},{6,18},{7,19},{8,20},{9,... | collective-permute-start | bytes 589832 | tf_op jit(solution)/shard_map/ppermute | solution.py:18
  21.5 13.8 %collective-permute-start.3 = (bf16[128,768]{1,0:T(8,128)(2,1)S(1)}, bf16[128,768]{1,0:T(8,128)(2,1)}, u32[]{:S(2)}, u32[]{:S(2)}) collective-permute-start(bf16[128,768]{1,0:T(8,128)(2,1)S(1)} %convert_element_type.37), channel_id=1, source_target_pairs={{0,4},{1,5},{2,6},{3,7},{4,8},{5,9},{6,10},{7,11},{8,12},{9,13},{1... | collective-permute-start | bytes 589832 | tf_op jit(solution)/shard_map/ppermute | solution.py:18
  31.9 8.1 %collective-permute-start.4 = (bf16[128,768]{1,0:T(8,128)(2,1)S(1)}, bf16[128,768]{1,0:T(8,128)(2,1)S(1)}, u32[]{:S(2)}, u32[]{:S(2)}) collective-permute-start(bf16[128,768]{1,0:T(8,128)(2,1)S(1)} %convert_element_type.37), channel_id=1, source_target_pairs={{0,8},{1,9},{2,10},{3,11},{4,12},{5,13},{6,14},{7,15},{8,16},{9,17... | collective-permute-start | bytes 589832 | tf_op jit(solution)/shard_map/ppermute | solution.py:18
  35.4 6.8 %collective-permute-start.7 = (bf16[128,768]{1,0:T(8,128)(2,1)S(1)}, bf16[128,768]{1,0:T(8,128)(2,1)S(1)}, u32[]{:S(2)}, u32[]{:S(2)}) collective-permute-start(bf16[128,768]{1,0:T(8,128)(2,1)S(1)} %convert_element_type.37), channel_id=1, source_target_pairs={{0,2},{1,3},{2,0},{3,1},{4,6},{5,7},{6,4},{7,5},{8,10},{9,11},{10,... | collective-permute-start | bytes 589832 | tf_op jit(solution)/shard_map/ppermute | solution.py:18
  37.8 9.6 %collective-permute-start.6 = (bf16[128,768]{1,0:T(8,128)(2,1)S(1)}, bf16[128,768]{1,0:T(8,128)(2,1)S(1)}, u32[]{:S(2)}, u32[]{:S(2)}) collective-permute-start(bf16[128,768]{1,0:T(8,128)(2,1)S(1)} %convert_element_type.37), channel_id=1, source_target_pairs={{0,1},{1,0},{2,3},{3,2},{4,5},{5,4},{6,7},{7,6},{8,9},{9,8},{10,11... | collective-permute-start | bytes 589832 | tf_op jit(solution)/shard_map/ppermute | solution.py:18
  37.9 5.1 %collective-permute-start.2 = (bf16[128,768]{1,0:T(8,128)(2,1)S(1)}, bf16[128,768]{1,0:T(8,128)(2,1)S(1)}, u32[]{:S(2)}, u32[]{:S(2)}) collective-permute-start(bf16[128,768]{1,0:T(8,128)(2,1)S(1)} %collective-permute-done.1), channel_id=1, source_target_pairs={{0,1},{1,0},{2,3},{3,2},{4,5},{5,4},{6,7},{7,6},{8,9},{9,8},{10,11... | collective-permute-start | bytes 589832 | tf_op jit(solution)/shard_map/ppermute | solution.py:18
  40.0 18.3 %collective-permute-start.16 = (bf16[128,768]{1,0:T(8,128)(2,1)}, bf16[128,768]{1,0:T(8,128)(2,1)}, u32[]{:S(2)}, u32[]{:S(2)}) collective-permute-start(bf16[128,768]{1,0:T(8,128)(2,1)} %collective-permute-done.9), channel_id=1, source_target_pairs={{0,2},{1,3},{2,0},{3,1},{4,6},{5,7},{6,4},{7,5},{8,10},{9,11},{10,... | collective-permute-start | bytes 589832 | tf_op jit(solution)/shard_map/ppermute | solution.py:18
  40.9 20.3 %collective-permute-start.18 = (bf16[128,768]{1,0:T(8,128)(2,1)}, bf16[128,768]{1,0:T(8,128)(2,1)}, u32[]{:S(2)}, u32[]{:S(2)}) collective-permute-start(bf16[128,768]{1,0:T(8,128)(2,1)} %collective-permute-done.11), channel_id=1, source_target_pairs={{0,2},{1,3},{2,0},{3,1},{4,6},{5,7},{6,4},{7,5},{8,10},{9,11},{10,... | collective-permute-start | bytes 589832 | tf_op jit(solution)/shard_map/ppermute | solution.py:18
  42.1 11.4 %copy-start.18 = (bf16[128,768]{1,0:T(8,128)(2,1)}, bf16[128,768]{1,0:T(8,128)(2,1)S(1)}, u32[]{:S(2)}) copy-start(bf16[128,768]{1,0:T(8,128)(2,1)S(1)} %collective-permute-done.7) | copy-start | bytes 589828
  42.1 20.0 %collective-permute-start.17 = (bf16[128,768]{1,0:T(8,128)(2,1)}, bf16[128,768]{1,0:T(8,128)(2,1)}, u32[]{:S(2)}, u32[]{:S(2)}) collective-permute-start(bf16[128,768]{1,0:T(8,128)(2,1)} %collective-permute-done.10), channel_id=1, source_target_pairs={{0,2},{1,3},{2,0},{3,1},{4,6},{5,7},{6,4},{7,5},{8,10},{9,11},{10,... | collective-permute-start | bytes 589832 | tf_op jit(solution)/shard_map/ppermute | solution.py:18
  43.0 5.7 %collective-permute-start.8 = (bf16[128,768]{1,0:T(8,128)(2,1)S(1)}, bf16[128,768]{1,0:T(8,128)(2,1)S(1)}, u32[]{:S(2)}, u32[]{:S(2)}) collective-permute-start(bf16[128,768]{1,0:T(8,128)(2,1)S(1)} %collective-permute-done.7), channel_id=1, source_target_pairs={{0,1},{1,0},{2,3},{3,2},{4,5},{5,4},{6,7},{7,6},{8,9},{9,8},{10,11... | collective-permute-start | bytes 589832 | tf_op jit(solution)/shard_map/ppermute | solution.py:18
  47.4 15.7 %collective-permute-start.12 = (bf16[128,768]{1,0:T(8,128)(2,1)}, bf16[128,768]{1,0:T(8,128)(2,1)}, u32[]{:S(2)}, u32[]{:S(2)}) collective-permute-start(bf16[128,768]{1,0:T(8,128)(2,1)} %collective-permute-done.3), channel_id=1, source_target_pairs={{0,2},{1,3},{2,0},{3,1},{4,6},{5,7},{6,4},{7,5},{8,10},{9,11},{10,... | collective-permute-start | bytes 589832 | tf_op jit(solution)/shard_map/ppermute | solution.py:18
  48.7 17.3 %collective-permute-start.14 = (bf16[128,768]{1,0:T(8,128)(2,1)}, bf16[128,768]{1,0:T(8,128)(2,1)}, u32[]{:S(2)}, u32[]{:S(2)}) collective-permute-start(bf16[128,768]{1,0:T(8,128)(2,1)} %collective-permute-done.5), channel_id=1, source_target_pairs={{0,2},{1,3},{2,0},{3,1},{4,6},{5,7},{6,4},{7,5},{8,10},{9,11},{10,... | collective-permute-start | bytes 589832 | tf_op jit(solution)/shard_map/ppermute | solution.py:18
  55.0 14.6 %all-to-all-start = ((f32[32,2,4,128]{3,2,1,0:T(4,128)}), f32[32,2,4,128]{3,2,1,0:T(4,128)S(1)}, u32[]{:S(2)}, u32[]{:S(2)}) async-start(f32[32,2,4,128]{3,2,1,0:T(4,128)} %broadcast_in_dim.5), calls=%async_computation | async-start | bytes 262144 | tf_op jit(solution)/shard_map/all_to_all | solution.py:78
  58.4 11.2 %collective-permute-start.13 = (bf16[128,768]{1,0:T(8,128)(2,1)S(1)}, bf16[128,768]{1,0:T(8,128)(2,1)S(1)}, u32[]{:S(2)}, u32[]{:S(2)}) collective-permute-start(bf16[128,768]{1,0:T(8,128)(2,1)S(1)} %copy-done.2), channel_id=1, source_target_pairs={{0,2},{1,3},{2,0},{3,1},{4,6},{5,7},{6,4},{7,5},{8,10},{9,11},{10,... | collective-permute-start | bytes 589832 | tf_op jit(solution)/shard_map/ppermute | solution.py:18
  78.8 6.5 %collective-permute-start.19 = (f32[128,768]{1,0:T(8,128)}, f32[128,768]{1,0:T(8,128)}, u32[]{:S(2)}, u32[]{:S(2)}) collective-permute-start(f32[128,768]{1,0:T(8,128)} %slice.224), channel_id=1, source_target_pairs={{0,1},{1,0},{2,3},{3,2},{4,5},{5,4},{6,7},{7,6},{8,9},{9,8},{10,11... | collective-permute-start | bytes 1179656 | tf_op jit(solution)/shard_map/ppermute | solution.py:18
  84.7 2.4 %collective-permute-start.15 = (f32[128,768]{1,0:T(8,128)S(1)}, f32[128,768]{1,0:T(8,128)S(1)}, u32[]{:S(2)}, u32[]{:S(2)}) collective-permute-start(f32[128,768]{1,0:T(8,128)S(1)} %slice.214), channel_id=1, source_target_pairs={{0,1},{1,0},{2,3},{3,2},{4,5},{5,4},{6,7},{7,6},{8,9},{9,8},{10,11... | collective-permute-start | bytes 1179656 | tf_op jit(solution)/shard_map/ppermute | solution.py:18
  (18 other events, 54.5 us)

commit v2 on v1

v2 whole, which is shorter than its diff:
```python
import functools

import jax
import jax.numpy as jnp
from jax import lax
from jax.experimental import pallas as pl
from jax.experimental.pallas import tpu as pltpu
from jax.sharding import PartitionSpec as P

STEPS = 4
LOGIT_SCALE = 5.0
AXES = ("batch", "span")
SPANS = 4
F32, BF16 = jnp.float32, jnp.bfloat16
VMEM_LIMIT = 32 * 1024 * 1024


def moved(value, target):
    count, spans = lax.axis_size("batch"), lax.axis_size("span")
    pairs = []
    for b in range(count):
        for s in range(spans):
            to_b, to_s = target(b, s)
            pairs.append((b * spans + s, (to_b % count) * spans + to_s))
    return lax.ppermute(value, AXES, pairs)


def over_core(value):
    return moved(value, lambda b, s: (b, s ^ 1))


def over_x(value):
    return moved(value, lambda b, s: (b, s ^ 2))


def along(value, steps):
    return moved(value, lambda b, s: (b + steps, s))


def dot_t(a, b):
    return lax.dot_general(a, b, (((1,), (1,)), ((), ())), preferred_element_type=F32)


def call(kernel, out_shape, scratch, flops, *args):
    whole = pl.BlockSpec(memory_space=pltpu.VMEM)
    size = sum(a.size * a.dtype.itemsize for a in args)
    return pl.pallas_call(
        kernel,
        out_shape=out_shape,
        in_specs=[whole] * len(args),
        out_specs=jax.tree.map(lambda _: whole, out_shape),
        scratch_shapes=scratch,
        compiler_params=pltpu.CompilerParams(vmem_limit_bytes=VMEM_LIMIT),
        cost_estimate=pl.CostEstimate(flops=flops, bytes_accessed=size, transcendentals=0),
    )(*args)


def cast_kernel(image, text, i_out, t_out, own):
    i = image[...].astype(BF16)
    t = text[...].astype(BF16)
    n = i.shape[0]
    i_out[...] = i
    t_out[...] = t
    own[:n] = t
    own[n:] = i


def stats_kernel(count, *refs):
    own, core, x, corex, t1, t2, t3, i1, i2, i3, out, rows, cols = refs
    n = t1.shape[0]
    pos = lax.axis_index("span")
    near = (own, core, x, corex)
    part = []
    for side in range(2):
        for q, ref in enumerate(near):
            rows[side, q * n : (q + 1) * n] = ref[n:] if side == 0 else ref[:n]
        cols[side, :n] = own[:n] if side == 0 else own[n:]
        for q, ref in enumerate((t1, t2, t3) if side == 0 else (i1, i2, i3)):
            cols[side, (q + 1) * n : (q + 2) * n] = ref[...]
        s = dot_t(cols[side], rows[side]) * LOGIT_SCALE
        top = jnp.max(s, axis=0, keepdims=True)
        lse = top + jnp.log(jnp.sum(jnp.exp(s - top), axis=0, keepdims=True))
        part += [lse[:, q * n : (q + 1) * n] for q in range(SPANS)]
    for sigma in range(SPANS):
        v = jnp.concatenate([part[4 * (r // 4) + ((r % 4) ^ sigma)] for r in range(2 * SPANS)])
        to = pos ^ sigma

        def store(b, _):
            out[b * SPANS + to] = v
            return 0

        lax.fori_loop(0, count, store, 0)


def grad_kernel(count, *refs):
    got, own, core, x, t1, t2, t3, i1, i2, i3, tx1, tx2, tx3, ix1, ix2, ix3 = refs[:16]
    image_lse, text_lse, kept, sent, rows, cols = refs[16:]
    n = t1.shape[0]
    b = lax.axis_index("batch")

    def lse_of(block):
        at = lax.rem(block + count, count) * SPANS
        v = [got[at + s] for s in range(SPANS)]
        top = jnp.maximum(jnp.maximum(v[0], v[1]), jnp.maximum(v[2], v[3]))
        return top + jnp.log(sum(jnp.exp(a - top) for a in v))

    mine = lse_of(b)
    image_lse[...] = mine[0]
    text_lse[...] = mine[4]
    turned = mine.T
    for side in range(2):
        if side == 0:
            half = slice(n, 2 * n)
            pieces = [(own, x), (t1, tx1), (t2, tx2), (t3, tx3)]
        else:
            half = slice(0, n)
            pieces = [(own, x), (i1, ix1), (i2, ix2), (i3, ix3)]
        rows[side, :n] = own[half]
        rows[side, n:] = core[half]
        row_lse = jnp.concatenate([turned[:, 4 * side : 4 * side + 1], turned[:, 4 * side + 1 : 4 * side + 2]])
        total = jnp.zeros((2 * n, rows.shape[-1]), F32)
        for k, (near, far) in enumerate(pieces):
            if k == 0:
                other = slice(0, n) if side == 0 else slice(n, 2 * n)
                cols[side, k, :n] = near[other]
                cols[side, k, n:] = far[other]
                l = mine
            else:
                cols[side, k, :n] = near[...]
                cols[side, k, n:] = far[...]
                l = lse_of(b - k) if side == 0 else lse_of(b + k)
            at = 4 if side == 0 else 0
            col_lse = jnp.concatenate([l[at : at + 1], l[at + 2 : at + 3]], axis=1)
            c = cols[side, k]
            s = dot_t(rows[side], c) * LOGIT_SCALE
            w = 0.5 * jnp.exp(s - row_lse) + 0.5 * jnp.exp(s - col_lse)
            if k == 0:
                i = lax.broadcasted_iota(jnp.int32, s.shape, 0)
                j = lax.broadcasted_iota(jnp.int32, s.shape, 1)
                w = w - ((i == j) & (i < n)).astype(F32)
            total = total + jnp.dot(w.astype(BF16), c, preferred_element_type=F32)
        kept[side] = LOGIT_SCALE * total[:n]
        sent[side] = LOGIT_SCALE * total[n:]


def add_kernel(kept, got, image_grad, text_grad):
    image_grad[...] = kept[0] + got[0]
    text_grad[...] = kept[1] + got[1]


def body(image_embeds, text_embeds):
    n, width = image_embeds.shape
    count = lax.axis_size("batch")
    piece = jax.ShapeDtypeStruct((n, width), BF16)
    i0, t0, own = call(
        cast_kernel, (piece, piece, jax.ShapeDtypeStruct((2 * n, width), BF16)), [], 0, image_embeds, text_embeds
    )
    texts = [along(t0, k) for k in range(1, STEPS)]
    images = [along(i0, -k) for k in range(1, STEPS)]
    x = over_x(own)
    texts_x = [over_x(v) for v in texts]
    images_x = [over_x(v) for v in images]
    core = over_core(own)
    corex = over_core(x)
    send = call(
        functools.partial(stats_kernel, count),
        jax.ShapeDtypeStruct((count * SPANS, 2 * SPANS, n), F32),
        [pltpu.VMEM((2, SPANS * n, width), BF16), pltpu.VMEM((2, STEPS * n, width), BF16)],
        4 * SPANS * n * STEPS * n * width,
        own, core, x, corex, *texts, *images,
    )
    got = lax.all_to_all(send, AXES, 0, 0, tiled=True)
    row = jax.ShapeDtypeStruct((n,), F32)
    pair = jax.ShapeDtypeStruct((2, n, width), F32)
    image_lse, text_lse, kept, sent = call(
        functools.partial(grad_kernel, count),
        (row, row, pair, pair),
        [pltpu.VMEM((2, 2 * n, width), BF16), pltpu.VMEM((2, STEPS, 2 * n, width), BF16)],
        8 * 2 * n * STEPS * 2 * n * width,
        got, own, core, x, *texts, *images, *texts_x, *images_x,
    )
    grad = jax.ShapeDtypeStruct((n, width), F32)
    image_grad, text_grad = call(add_kernel, (grad, grad), [], 0, kept, over_core(sent))
    return (image_lse, text_lse, image_grad, text_grad)


def solution(mesh):
    in_specs = (P(("batch", "span"), None), P(("batch", "span"), None))
    out_specs = (
        P(("batch", "span")),
        P(("batch", "span")),
        P(("batch", "span"), None),
        P(("batch", "span"), None),
    )
    return jax.shard_map(body, mesh=mesh, in_specs=in_specs, out_specs=out_specs, check_vma=False)
```

time: 88.7 us -> 80.8 us (0.911)
  waiting for transfers between devices: 16.6 us -> 47.3 us
  matrix products: 21.3 us -> 0 us
  local copies, waits for them, and re-layouts: 13.6 us -> 3.59 us
  starting transfers between devices: 30.9 us -> 22.3 us
  Pallas kernels: 0 us -> 6.58 us
  other arithmetic: 4.23 us -> 0 us
    ppermute x20 -> x16, waiting for transfers between devices: 16.6 us -> 47.3 us  [moved(): return lax.ppermute(value, AXES, pairs)]
    dot_general x16 -> x0, matrix products: 21.3 us -> none  [the longest x8 12.5 us: gradient(): jnp.dot(w, col, preferred_element_type=jnp.float32)]
    ppermute x20 -> x16, starting transfers between devices: 27.6 us -> 16 us  [moved(): return lax.ppermute(value, AXES, pairs)]
    pallas_call x0 -> x4, Pallas kernels: none -> 6.58 us  [call(): pl.pallas_call(kernel, out_shape=out_shape, in_specs=[whole] * len(args),...]
    concatenate x7 -> x0, local copies, waits for them, and re-layouts: 4.74 us -> none  [the longest x6 4.72 us: cols(): return [jnp.concatenate([v, w]) for v, w in zip(a, ax)]]
    unnamed x49 -> x8, local copies, waits for them, and re-layouts: 6.62 us -> 3.59 us
    all_to_all x1, starting transfers between devices: 3.3 us -> 6.27 us  [body(): got = lax.all_to_all(send, AXES, 0, 0, tiled=True)]
    add x7 -> x0, other arithmetic: 2.7 us -> none  [the longest x1 1.78 us: body(): text_grad = grad_t[:rows] + over_core(grad_t[rows:])]
  transfers between devices with their start and end apart: 21 -> 17, of which waited for: 5 -> 11; matrix products, arithmetic and copies ran while one was open for 32% -> 0% of each run, Pallas kernels for 0% -> 3%
where the time goes in v2:
time: 80.8 us; the launch traced here: 80.5 us
  waiting for transfers between devices  47.3 us (59%)
  starting transfers between devices  22.3 us (28%)
  Pallas kernels  6.58 us (8%)
  local copies, waits for them, and re-layouts  3.59 us (4%)
    ppermute x16, waiting for transfers between devices, moved(): return lax.ppermute(value, AXES, pairs)  47.3 us
    ppermute x16, starting transfers between devices, moved(): return lax.ppermute(value, AXES, pairs)  16 us
    pallas_call x4, Pallas kernels, call(): pl.pallas_call(kernel, out_shape=out_shape, in_specs=[whole] * len(args),...  6.58 us
    all_to_all x1, starting transfers between devices, body(): got = lax.all_to_all(send, AXES, 0, 0, tiled=True)  6.27 us
    unnamed x8, local copies, waits for them, and re-layouts  3.59 us
  transfers between devices with their start and end apart: 17, of which 11 were waited for; matrix products, arithmetic and copies ran while one was open for 0% of the time, Pallas kernels for 3%

profile of v2, /device:TPU:0, one launch (start us, length us, event | category | flops | bytes accessed | tf_op | source)
XLA Modules:
  0.0 80.5 jit_solution(4413074749768433272)
XLA Ops:
  0.6 1.0 %copy-done = f32[128,768]{1,0:T(8,128)S(1)} copy-done((f32[128,768]{1,0:T(8,128)S(1)}, f32[128,768]{1,0:T(8,128)}, u32[]{:S(2)}) %copy-start) | copy-done | bytes 393240
  1.6 1.0 %copy-done.1 = f32[128,768]{1,0:T(8,128)S(1)} copy-done((f32[128,768]{1,0:T(8,128)S(1)}, f32[128,768]{1,0:T(8,128)}, u32[]{:S(2)}) %copy-start.1) | copy-done | bytes 393240
  2.7 3.0 %collective-permute-start.1 = (bf16[256,768]{1,0:T(8,128)(2,1)S(1)}, bf16[256,768]{1,0:T(8,128)(2,1)S(1)}, u32[]{:S(2)}, u32[]{:S(2)}) collective-permute-start(bf16[256,768]{1,0:T(8,128)(2,1)S(1)} %get-tuple-element.13.refs_0_.refs_1_), channel_id=1, source_target_pairs={{0,2},{1,3},{2,0},{3,1},{4,6},{5,7},{6,4},{7,5},{8,10},{9,11},{10,... | collective-permute-start | bytes 1179656 | tf_op jit(solution)/shard_map/ppermute | solution.py:25
  5.7 2.5 %collective-permute-start.5 = (bf16[128,768]{1,0:T(8,128)(2,1)S(1)}, bf16[128,768]{1,0:T(8,128)(2,1)S(1)}, u32[]{:S(2)}, u32[]{:S(2)}) collective-permute-start(bf16[128,768]{1,0:T(8,128)(2,1)S(1)} %get-tuple-element.14), channel_id=1, source_target_pairs={{0,12},{1,13},{2,14},{3,15},{4,16},{5,17},{6,18},{7,19},{8,20},{9,... | collective-permute-start | bytes 589832 | tf_op jit(solution)/shard_map/ppermute | solution.py:25
  8.2 1.6 %collective-permute-start.4 = (bf16[128,768]{1,0:T(8,128)(2,1)S(1)}, bf16[128,768]{1,0:T(8,128)(2,1)S(1)}, u32[]{:S(2)}, u32[]{:S(2)}) collective-permute-start(bf16[128,768]{1,0:T(8,128)(2,1)S(1)} %get-tuple-element.14), channel_id=1, source_target_pairs={{0,8},{1,9},{2,10},{3,11},{4,12},{5,13},{6,14},{7,15},{8,16},{9,17... | collective-permute-start | bytes 589832 | tf_op jit(solution)/shard_map/ppermute | solution.py:25
  9.8 1.5 %collective-permute-start.3 = (bf16[128,768]{1,0:T(8,128)(2,1)S(1)}, bf16[128,768]{1,0:T(8,128)(2,1)S(1)}, u32[]{:S(2)}, u32[]{:S(2)}) collective-permute-start(bf16[128,768]{1,0:T(8,128)(2,1)S(1)} %get-tuple-element.14), channel_id=1, source_target_pairs={{0,4},{1,5},{2,6},{3,7},{4,8},{5,9},{6,10},{7,11},{8,12},{9,13},{1... | collective-permute-start | bytes 589832 | tf_op jit(solution)/shard_map/ppermute | solution.py:25
  11.3 3.5 %collective-permute-done.1.refs_2_.refs_3_ = bf16[256,768]{1,0:T(8,128)(2,1)S(1)} collective-permute-done((bf16[256,768]{1,0:T(8,128)(2,1)S(1)}, bf16[256,768]{1,0:T(8,128)(2,1)S(1)}, u32[]{:S(2)}, u32[]{:S(2)}) %collective-permute-start.1) | collective-permute-done | bytes 393248 | tf_op jit(solution)/shard_map/ppermute | solution.py:25
  14.8 12.4 %collective-permute-done.5.refs_6_ = bf16[128,768]{1,0:T(8,128)(2,1)S(1)} collective-permute-done((bf16[128,768]{1,0:T(8,128)(2,1)S(1)}, bf16[128,768]{1,0:T(8,128)(2,1)S(1)}, u32[]{:S(2)}, u32[]{:S(2)}) %collective-permute-start.5) | collective-permute-done | bytes 196640 | tf_op jit(solution)/shard_map/ppermute | solution.py:25
  27.2 1.0 %collective-permute-start.6 = (bf16[128,768]{1,0:T(8,128)(2,1)S(1)}, bf16[128,768]{1,0:T(8,128)(2,1)S(1)}, u32[]{:S(2)}, u32[]{:S(2)}) collective-permute-start(bf16[128,768]{1,0:T(8,128)(2,1)S(1)} %get-tuple-element.15), channel_id=1, source_target_pairs={{0,28},{1,29},{2,30},{3,31},{4,0},{5,1},{6,2},{7,3},{8,4},{9,5},{1... | collective-permute-start | bytes 589832 | tf_op jit(solution)/shard_map/ppermute | solution.py:25
  28.2 7.2 %collective-permute-done.8.refs_9_ = bf16[128,768]{1,0:T(8,128)(2,1)S(1)} collective-permute-done((bf16[128,768]{1,0:T(8,128)(2,1)S(1)}, bf16[128,768]{1,0:T(8,128)(2,1)S(1)}, u32[]{:S(2)}, u32[]{:S(2)}) %collective-permute-start.8) | collective-permute-done | bytes 196640 | tf_op jit(solution)/shard_map/ppermute | solution.py:25
  36.4 2.1 %collective-permute-done.6.refs_7_ = bf16[128,768]{1,0:T(8,128)(2,1)S(1)} collective-permute-done((bf16[128,768]{1,0:T(8,128)(2,1)S(1)}, bf16[128,768]{1,0:T(8,128)(2,1)S(1)}, u32[]{:S(2)}, u32[]{:S(2)}) %collective-permute-start.6) | collective-permute-done | bytes 196640 | tf_op jit(solution)/shard_map/ppermute | solution.py:25
  38.5 2.2 %shard_map.58 = f32[32,8,128]{2,1,0:T(8,128)} custom-call(bf16[256,768]{1,0:T(8,128)(2,1)S(1)} %get-tuple-element.13.refs_0_.refs_1_, bf16[256,768]{1,0:T(8,128)(2,1)S(1)} %collective-permute-done.refs_1_.refs_2_, bf16[256,768]{1,0:T(8,128)(2,1)S(1)} %collective-permute-done.1.refs_2_.refs_3_, bf16[256,768]{1,0:T(8,128)(2,1)S(1)} %collective-permute-done.2.refs_3_, ...), custom_call_target="tpu_custom_call" | custom-call | flops 805306368 | bytes 2752512 | tf_op jit(solution)/shard_map/pallas_call | solution.py:47
  40.7 6.3 %all-to-all-start = ((f32[32,8,128]{2,1,0:T(8,128)}), f32[32,8,128]{2,1,0:T(8,128)S(1)}, u32[]{:S(2)}, u32[]{:S(2)}) async-start(f32[32,8,128]{2,1,0:T(8,128)} %shard_map.58), calls=%async_computation | async-start | bytes 262144 | tf_op jit(solution)/shard_map/all_to_all | solution.py:172
  46.9 1.8 %collective-permute-start.10 = (bf16[128,768]{1,0:T(8,128)(2,1)S(1)}, bf16[128,768]{1,0:T(8,128)(2,1)S(1)}, u32[]{:S(2)}, u32[]{:S(2)}) collective-permute-start(bf16[128,768]{1,0:T(8,128)(2,1)S(1)} %collective-permute-done.4.refs_5_), channel_id=1, source_target_pairs={{0,2},{1,3},{2,0},{3,1},{4,6},{5,7},{6,4},{7,5},{8,10},{9,11},{10,... | collective-permute-start | bytes 589832 | tf_op jit(solution)/shard_map/ppermute | solution.py:25
  49.0 1.8 %collective-permute-start.14 = (bf16[128,768]{1,0:T(8,128)(2,1)S(1)}, bf16[128,768]{1,0:T(8,128)(2,1)S(1)}, u32[]{:S(2)}, u32[]{:S(2)}) collective-permute-start(bf16[128,768]{1,0:T(8,128)(2,1)S(1)} %collective-permute-done.8.refs_9_), channel_id=1, source_target_pairs={{0,2},{1,3},{2,0},{3,1},{4,6},{5,7},{6,4},{7,5},{8,10},{9,11},{10,... | collective-permute-start | bytes 589832 | tf_op jit(solution)/shard_map/ppermute | solution.py:25
  51.1 1.8 %collective-permute-start.12 = (bf16[128,768]{1,0:T(8,128)(2,1)S(1)}, bf16[128,768]{1,0:T(8,128)(2,1)S(1)}, u32[]{:S(2)}, u32[]{:S(2)}) collective-permute-start(bf16[128,768]{1,0:T(8,128)(2,1)S(1)} %collective-permute-done.6.refs_7_), channel_id=1, source_target_pairs={{0,2},{1,3},{2,0},{3,1},{4,6},{5,7},{6,4},{7,5},{8,10},{9,11},{10,... | collective-permute-start | bytes 589832 | tf_op jit(solution)/shard_map/ppermute | solution.py:25
  52.8 3.1 %collective-permute-done.10.refs_11_ = bf16[128,768]{1,0:T(8,128)(2,1)S(1)} collective-permute-done((bf16[128,768]{1,0:T(8,128)(2,1)S(1)}, bf16[128,768]{1,0:T(8,128)(2,1)S(1)}, u32[]{:S(2)}, u32[]{:S(2)}) %collective-permute-start.10) | collective-permute-done | bytes 196640 | tf_op jit(solution)/shard_map/ppermute | solution.py:25
  55.9 4.2 %collective-permute-done.9.refs_10_ = bf16[128,768]{1,0:T(8,128)(2,1)S(1)} collective-permute-done((bf16[128,768]{1,0:T(8,128)(2,1)S(1)}, bf16[128,768]{1,0:T(8,128)(2,1)S(1)}, u32[]{:S(2)}, u32[]{:S(2)}) %collective-permute-start.9) | collective-permute-done | bytes 196640 | tf_op jit(solution)/shard_map/ppermute | solution.py:25
  60.1 4.2 %collective-permute-done.14.refs_15_ = bf16[128,768]{1,0:T(8,128)(2,1)S(1)} collective-permute-done((bf16[128,768]{1,0:T(8,128)(2,1)S(1)}, bf16[128,768]{1,0:T(8,128)(2,1)S(1)}, u32[]{:S(2)}, u32[]{:S(2)}) %collective-permute-start.14) | collective-permute-done | bytes 196640 | tf_op jit(solution)/shard_map/ppermute | solution.py:25
  64.3 4.2 %collective-permute-done.13.refs_14_ = bf16[128,768]{1,0:T(8,128)(2,1)S(1)} collective-permute-done((bf16[128,768]{1,0:T(8,128)(2,1)S(1)}, bf16[128,768]{1,0:T(8,128)(2,1)S(1)}, u32[]{:S(2)}, u32[]{:S(2)}) %collective-permute-start.13) | collective-permute-done | bytes 196640 | tf_op jit(solution)/shard_map/ppermute | solution.py:25
  68.5 3.7 %collective-permute-done.12.refs_13_ = bf16[128,768]{1,0:T(8,128)(2,1)S(1)} collective-permute-done((bf16[128,768]{1,0:T(8,128)(2,1)S(1)}, bf16[128,768]{1,0:T(8,128)(2,1)S(1)}, u32[]{:S(2)}, u32[]{:S(2)}) %collective-permute-start.12) | collective-permute-done | bytes 196640 | tf_op jit(solution)/shard_map/ppermute | solution.py:25
  73.9 3.4 %shard_map.59 = (f32[128]{0:T(128)}, f32[128]{0:T(128)}, f32[2,128,768]{2,1,0:T(8,128)S(1)}, f32[2,128,768]{2,1,0:T(8,128)S(1)}) custom-call(f32[32,8,128]{2,1,0:T(8,128)S(1)} %all-to-all-done.refs_0_, bf16[256,768]{1,0:T(8,128)(2,1)S(1)} %get-tuple-element.13.refs_0_.refs_1_, bf16[256,768]{1,0:T(8,128)(2,1)S(1)} %collective-permute-done.refs_1_.refs_2_, ...), custom_call_target="tpu_custom_call" | custom-call | flops 1610612736 | bytes 3670016 | tf_op jit(solution)/shard_map/pallas_call | solution.py:47
  77.3 2.3 %collective-permute-done.15.got = f32[2,128,768]{2,1,0:T(8,128)S(1)} collective-permute-done((f32[2,128,768]{2,1,0:T(8,128)S(1)}, f32[2,128,768]{2,1,0:T(8,128)S(1)}, u32[]{:S(2)}, u32[]{:S(2)}) %collective-permute-start.15) | collective-permute-done | bytes 786464 | tf_op jit(solution)/shard_map/ppermute | solution.py:25
  79.6 1.0 %shard_map.60 = (f32[128,768]{1,0:T(8,128)}, f32[128,768]{1,0:T(8,128)}) custom-call(f32[2,128,768]{2,1,0:T(8,128)S(1)} %get-tuple-element.18.kept, f32[2,128,768]{2,1,0:T(8,128)S(1)} %collective-permute-done.15.got), custom_call_target="tpu_custom_call" | custom-call | bytes 1572864 | tf_op jit(solution)/shard_map/pallas_call | solution.py:47
  (22 shorter events, 3.2 us)
Async XLA Ops:
  0.6 1.0 %copy-start = (f32[128,768]{1,0:T(8,128)S(1)}, f32[128,768]{1,0:T(8,128)}, u32[]{:S(2)}) copy-start(f32[128,768]{1,0:T(8,128)} %image.1) | copy-start | bytes 1179652
  1.6 1.0 %copy-start.1 = (f32[128,768]{1,0:T(8,128)S(1)}, f32[128,768]{1,0:T(8,128)}, u32[]{:S(2)}) copy-start(f32[128,768]{1,0:T(8,128)} %text.1) | copy-start | bytes 1179652
  2.7 12.1 %collective-permute-start.1 = (bf16[256,768]{1,0:T(8,128)(2,1)S(1)}, bf16[256,768]{1,0:T(8,128)(2,1)S(1)}, u32[]{:S(2)}, u32[]{:S(2)}) collective-permute-start(bf16[256,768]{1,0:T(8,128)(2,1)S(1)} %get-tuple-element.13.refs_0_.refs_1_), channel_id=1, source_target_pairs={{0,2},{1,3},{2,0},{3,1},{4,6},{5,7},{6,4},{7,5},{8,10},{9,11},{10,... | collective-permute-start | bytes 1179656 | tf_op jit(solution)/shard_map/ppermute | solution.py:25
  5.7 21.5 %collective-permute-start.5 = (bf16[128,768]{1,0:T(8,128)(2,1)S(1)}, bf16[128,768]{1,0:T(8,128)(2,1)S(1)}, u32[]{:S(2)}, u32[]{:S(2)}) collective-permute-start(bf16[128,768]{1,0:T(8,128)(2,1)S(1)} %get-tuple-element.14), channel_id=1, source_target_pairs={{0,12},{1,13},{2,14},{3,15},{4,16},{5,17},{6,18},{7,19},{8,20},{9,... | collective-permute-start | bytes 589832 | tf_op jit(solution)/shard_map/ppermute | solution.py:25
  8.2 19.0 %collective-permute-start.4 = (bf16[128,768]{1,0:T(8,128)(2,1)S(1)}, bf16[128,768]{1,0:T(8,128)(2,1)S(1)}, u32[]{:S(2)}, u32[]{:S(2)}) collective-permute-start(bf16[128,768]{1,0:T(8,128)(2,1)S(1)} %get-tuple-element.14), channel_id=1, source_target_pairs={{0,8},{1,9},{2,10},{3,11},{4,12},{5,13},{6,14},{7,15},{8,16},{9,17... | collective-permute-start | bytes 589832 | tf_op jit(solution)/shard_map/ppermute | solution.py:25
  9.8 17.4 %collective-permute-start.3 = (bf16[128,768]{1,0:T(8,128)(2,1)S(1)}, bf16[128,768]{1,0:T(8,128)(2,1)S(1)}, u32[]{:S(2)}, u32[]{:S(2)}) collective-permute-start(bf16[128,768]{1,0:T(8,128)(2,1)S(1)} %get-tuple-element.14), channel_id=1, source_target_pairs={{0,4},{1,5},{2,6},{3,7},{4,8},{5,9},{6,10},{7,11},{8,12},{9,13},{1... | collective-permute-start | bytes 589832 | tf_op jit(solution)/shard_map/ppermute | solution.py:25
  11.3 27.2 %collective-permute-start = (bf16[256,768]{1,0:T(8,128)(2,1)S(1)}, bf16[256,768]{1,0:T(8,128)(2,1)S(1)}, u32[]{:S(2)}, u32[]{:S(2)}) collective-permute-start(bf16[256,768]{1,0:T(8,128)(2,1)S(1)} %get-tuple-element.13.refs_0_.refs_1_), channel_id=1, source_target_pairs={{0,1},{1,0},{2,3},{3,2},{4,5},{5,4},{6,7},{7,6},{8,9},{9,8},{10,11... | collective-permute-start | bytes 1179656 | tf_op jit(solution)/shard_map/ppermute | solution.py:25
  14.8 23.7 %collective-permute-start.2 = (bf16[256,768]{1,0:T(8,128)(2,1)S(1)}, bf16[256,768]{1,0:T(8,128)(2,1)S(1)}, u32[]{:S(2)}, u32[]{:S(2)}) collective-permute-start(bf16[256,768]{1,0:T(8,128)(2,1)S(1)} %collective-permute-done.1.refs_2_.refs_3_), channel_id=1, source_target_pairs={{0,1},{1,0},{2,3},{3,2},{4,5},{5,4},{6,7},{7,6},{8,9},{9,8},{10,11... | collective-permute-start | bytes 1179656 | tf_op jit(solution)/shard_map/ppermute | solution.py:25
  27.2 8.2 %collective-permute-start.8 = (bf16[128,768]{1,0:T(8,128)(2,1)S(1)}, bf16[128,768]{1,0:T(8,128)(2,1)S(1)}, u32[]{:S(2)}, u32[]{:S(2)}) collective-permute-start(bf16[128,768]{1,0:T(8,128)(2,1)S(1)} %get-tuple-element.15), channel_id=1, source_target_pairs={{0,20},{1,21},{2,22},{3,23},{4,24},{5,25},{6,26},{7,27},{8,28},{9,... | collective-permute-start | bytes 589832 | tf_op jit(solution)/shard_map/ppermute | solution.py:25
  27.2 9.1 %collective-permute-start.7 = (bf16[128,768]{1,0:T(8,128)(2,1)S(1)}, bf16[128,768]{1,0:T(8,128)(2,1)S(1)}, u32[]{:S(2)}, u32[]{:S(2)}) collective-permute-start(bf16[128,768]{1,0:T(8,128)(2,1)S(1)} %get-tuple-element.15), channel_id=1, source_target_pairs={{0,24},{1,25},{2,26},{3,27},{4,28},{5,29},{6,30},{7,31},{8,0},{9,1... | collective-permute-start | bytes 589832 | tf_op jit(solution)/shard_map/ppermute | solution.py:25
  27.2 11.2 %collective-permute-start.6 = (bf16[128,768]{1,0:T(8,128)(2,1)S(1)}, bf16[128,768]{1,0:T(8,128)(2,1)S(1)}, u32[]{:S(2)}, u32[]{:S(2)}) collective-permute-start(bf16[128,768]{1,0:T(8,128)(2,1)S(1)} %get-tuple-element.15), channel_id=1, source_target_pairs={{0,28},{1,29},{2,30},{3,31},{4,0},{5,1},{6,2},{7,3},{8,4},{9,5},{1... | collective-permute-start | bytes 589832 | tf_op jit(solution)/shard_map/ppermute | solution.py:25
  35.4 15.7 %collective-permute-start.11 = (bf16[128,768]{1,0:T(8,128)(2,1)S(1)}, bf16[128,768]{1,0:T(8,128)(2,1)S(1)}, u32[]{:S(2)}, u32[]{:S(2)}) collective-permute-start(bf16[128,768]{1,0:T(8,128)(2,1)S(1)} %collective-permute-done.5.refs_6_), channel_id=1, source_target_pairs={{0,2},{1,3},{2,0},{3,1},{4,6},{5,7},{6,4},{7,5},{8,10},{9,11},{10,... | collective-permute-start | bytes 589832 | tf_op jit(solution)/shard_map/ppermute | solution.py:25
  40.7 32.3 %all-to-all-start = ((f32[32,8,128]{2,1,0:T(8,128)}), f32[32,8,128]{2,1,0:T(8,128)S(1)}, u32[]{:S(2)}, u32[]{:S(2)}) async-start(f32[32,8,128]{2,1,0:T(8,128)} %shard_map.58), calls=%async_computation | async-start | bytes 262144 | tf_op jit(solution)/shard_map/all_to_all | solution.py:172
  46.9 9.0 %collective-permute-start.10 = (bf16[128,768]{1,0:T(8,128)(2,1)S(1)}, bf16[128,768]{1,0:T(8,128)(2,1)S(1)}, u32[]{:S(2)}, u32[]{:S(2)}) collective-permute-start(bf16[128,768]{1,0:T(8,128)(2,1)S(1)} %collective-permute-done.4.refs_5_), channel_id=1, source_target_pairs={{0,2},{1,3},{2,0},{3,1},{4,6},{5,7},{6,4},{7,5},{8,10},{9,11},{10,... | collective-permute-start | bytes 589832 | tf_op jit(solution)/shard_map/ppermute | solution.py:25
  48.8 11.3 %collective-permute-start.9 = (bf16[128,768]{1,0:T(8,128)(2,1)S(1)}, bf16[128,768]{1,0:T(8,128)(2,1)S(1)}, u32[]{:S(2)}, u32[]{:S(2)}) collective-permute-start(bf16[128,768]{1,0:T(8,128)(2,1)S(1)} %collective-permute-done.3.refs_4_), channel_id=1, source_target_pairs={{0,2},{1,3},{2,0},{3,1},{4,6},{5,7},{6,4},{7,5},{8,10},{9,11},{10,... | collective-permute-start | bytes 589832 | tf_op jit(solution)/shard_map/ppermute | solution.py:25
  49.0 15.3 %collective-permute-start.14 = (bf16[128,768]{1,0:T(8,128)(2,1)S(1)}, bf16[128,768]{1,0:T(8,128)(2,1)S(1)}, u32[]{:S(2)}, u32[]{:S(2)}) collective-permute-start(bf16[128,768]{1,0:T(8,128)(2,1)S(1)} %collective-permute-done.8.refs_9_), channel_id=1, source_target_pairs={{0,2},{1,3},{2,0},{3,1},{4,6},{5,7},{6,4},{7,5},{8,10},{9,11},{10,... | collective-permute-start | bytes 589832 | tf_op jit(solution)/shard_map/ppermute | solution.py:25
  50.8 17.7 %collective-permute-start.13 = (bf16[128,768]{1,0:T(8,128)(2,1)S(1)}, bf16[128,768]{1,0:T(8,128)(2,1)S(1)}, u32[]{:S(2)}, u32[]{:S(2)}) collective-permute-start(bf16[128,768]{1,0:T(8,128)(2,1)S(1)} %collective-permute-done.7.refs_8_), channel_id=1, source_target_pairs={{0,2},{1,3},{2,0},{3,1},{4,6},{5,7},{6,4},{7,5},{8,10},{9,11},{10,... | collective-permute-start | bytes 589832 | tf_op jit(solution)/shard_map/ppermute | solution.py:25
  51.1 21.2 %collective-permute-start.12 = (bf16[128,768]{1,0:T(8,128)(2,1)S(1)}, bf16[128,768]{1,0:T(8,128)(2,1)S(1)}, u32[]{:S(2)}, u32[]{:S(2)}) collective-permute-start(bf16[128,768]{1,0:T(8,128)(2,1)S(1)} %collective-permute-done.6.refs_7_), channel_id=1, source_target_pairs={{0,2},{1,3},{2,0},{3,1},{4,6},{5,7},{6,4},{7,5},{8,10},{9,11},{10,... | collective-permute-start | bytes 589832 | tf_op jit(solution)/shard_map/ppermute | solution.py:25
  72.3 0.7 copy-start.2
  72.9 0.9 %copy-start.3 = (bf16[128,768]{1,0:T(8,128)(2,1)S(1)}, bf16[128,768]{1,0:T(8,128)(2,1)}, u32[]{:S(2)}) copy-start(bf16[128,768]{1,0:T(8,128)(2,1)} %copy-done.2) | copy-start | bytes 589828
  77.3 2.3 %collective-permute-start.15 = (f32[2,128,768]{2,1,0:T(8,128)S(1)}, f32[2,128,768]{2,1,0:T(8,128)S(1)}, u32[]{:S(2)}, u32[]{:S(2)}) collective-permute-start(f32[2,128,768]{2,1,0:T(8,128)S(1)} %get-tuple-element.19), channel_id=1, source_target_pairs={{0,1},{1,0},{2,3},{3,2},{4,5},{5,4},{6,7},{7,6},{8,9},{9,8},{10,11... | collective-permute-start | bytes 2359304 | tf_op jit(solution)/shard_map/ppermute | solution.py:25

commit v3 on v2

v3 whole, which is shorter than its diff:
```python
import functools

import jax
import jax.numpy as jnp
from jax import lax
from jax.experimental import pallas as pl
from jax.experimental.pallas import tpu as pltpu
from jax.sharding import PartitionSpec as P

STEPS = 4
LOGIT_SCALE = 5.0
AXES = ("batch", "span")
SPANS = 4
F32, BF16 = jnp.float32, jnp.bfloat16
VMEM_LIMIT = 32 * 1024 * 1024


def moved(value, target):
    count, spans = lax.axis_size("batch"), lax.axis_size("span")
    pairs = []
    for b in range(count):
        for s in range(spans):
            to_b, to_s = target(b, s)
            pairs.append((b * spans + s, (to_b % count) * spans + to_s))
    return lax.ppermute(value, AXES, pairs)


def over_core(value):
    return moved(value, lambda b, s: (b, s ^ 1))


def over_x(value):
    return moved(value, lambda b, s: (b, s ^ 2))


def along(value, steps):
    return moved(value, lambda b, s: (b + steps, s))


def in_pair(value):
    return moved(value, lambda b, s: (b ^ 1, s))


def across_pairs(value):
    return moved(value, lambda b, s: (b + (3 if b % 2 else -3), s))


def dot_t(a, b):
    return lax.dot_general(a, b, (((1,), (1,)), ((), ())), preferred_element_type=F32)


def call(kernel, out_shape, scratch, flops, *args, remote=()):
    whole = pl.BlockSpec(memory_space=pltpu.VMEM)
    size = sum(a.size * a.dtype.itemsize for a in args)
    return pl.pallas_call(
        kernel,
        out_shape=out_shape,
        in_specs=[pl.BlockSpec(memory_space=pl.ANY) if i in remote else whole for i in range(len(args))],
        out_specs=jax.tree.map(lambda _: whole, out_shape),
        scratch_shapes=scratch,
        compiler_params=pltpu.CompilerParams(vmem_limit_bytes=VMEM_LIMIT),
        cost_estimate=pl.CostEstimate(flops=flops, bytes_accessed=size, transcendentals=0),
    )(*args)


def cast_kernel(image, text, i_out, t_out, own, for_pair, for_across, i_in, t_in, sems):
    load_i = pltpu.make_async_copy(image, i_in, sems.at[0])
    load_t = pltpu.make_async_copy(text, t_in, sems.at[1])
    load_i.start()
    load_t.start()
    n = image.shape[0]
    odd = lax.rem(lax.axis_index("batch"), 2)
    load_i.wait()
    i = i_in[...].astype(BF16)
    i_out[...] = i
    own[n:] = i
    load_t.wait()
    t = t_in[...].astype(BF16)
    t_out[...] = t
    own[:n] = t

    @pl.when(odd == 0)
    def _():
        for_pair[...] = t
        for_across[...] = i

    @pl.when(odd == 1)
    def _():
        for_pair[...] = i
        for_across[...] = t


def fill_columns(cols, place, odd, own, a_t, a_i, b, pair, across):
    n = a_t.shape[0]
    at = slice(place * n, (place + 1) * n)
    cols[0, 0, at] = own[:n]
    cols[1, 0, at] = own[n:]
    cols[0, 1, at] = a_t[...]
    cols[1, 1, at] = a_i[...]
    cols[0, 2, at] = b[:n]
    cols[1, 2, at] = b[n:]
    cols[1 - odd, 3, at] = pair[...]
    cols[odd, 3, at] = across[...]


def stats_kernel(count, *refs):
    own, core, x, corex, a_t, a_i, b2, pair, across, out, rows, cols = refs
    n = a_t.shape[0]
    pos = lax.axis_index("span")
    odd = lax.rem(lax.axis_index("batch"), 2)
    fill_columns(cols, 0, odd, own, a_t, a_i, b2, pair, across)
    part = []
    for side in range(2):
        for q, ref in enumerate((own, core, x, corex)):
            rows[side, q * n : (q + 1) * n] = ref[n:] if side == 0 else ref[:n]
        s = dot_t(cols[side].reshape(STEPS * n, cols.shape[-1]), rows[side]) * LOGIT_SCALE
        top = jnp.max(s, axis=0, keepdims=True)
        lse = top + jnp.log(jnp.sum(jnp.exp(s - top), axis=0, keepdims=True))
        part += [lse[:, q * n : (q + 1) * n] for q in range(SPANS)]
    for sigma in range(SPANS):
        v = jnp.concatenate([part[4 * (r // 4) + ((r % 4) ^ sigma)] for r in range(2 * SPANS)])
        to = pos ^ sigma

        def store(b, _):
            out[b * SPANS + to] = v
            return 0

        lax.fori_loop(0, count, store, 0)


def grad_kernel(count, *refs):
    got, own, core, x, a_t, a_i, b2, pair, across, ax_t, ax_i, bx2, pairx, acrossx = refs[:14]
    image_lse, text_lse, kept, sent, rows, cols = refs[14:]
    n = a_t.shape[0]
    b = lax.axis_index("batch")
    odd = lax.rem(b, 2)

    def lse_of(block):
        at = lax.rem(block + count, count) * SPANS
        v = [got[at + s] for s in range(SPANS)]
        top = jnp.maximum(jnp.maximum(v[0], v[1]), jnp.maximum(v[2], v[3]))
        return top + jnp.log(sum(jnp.exp(a - top) for a in v))

    fill_columns(cols, 0, odd, own, a_t, a_i, b2, pair, across)
    fill_columns(cols, 1, odd, x, ax_t, ax_i, bx2, pairx, acrossx)
    mine = lse_of(b)
    image_lse[...] = mine[0]
    text_lse[...] = mine[4]
    turned = mine.T
    for side in range(2):
        half = slice(n, 2 * n) if side == 0 else slice(0, n)
        rows[side, :n] = own[half]
        rows[side, n:] = core[half]
        row_lse = jnp.concatenate([turned[:, 4 * side : 4 * side + 1], turned[:, 4 * side + 1 : 4 * side + 2]])
        total = jnp.zeros((2 * n, rows.shape[-1]), F32)
        steps = (0, -2, -1 - 2 * odd, -3 + 2 * odd) if side == 0 else (0, 2, 3 - 2 * odd, 1 + 2 * odd)
        for k, step in enumerate(steps):
            l = mine if k == 0 else lse_of(b + step)
            at = 4 if side == 0 else 0
            col_lse = jnp.concatenate([l[at : at + 1], l[at + 2 : at + 3]], axis=1)
            c = cols[side, k]
            s = dot_t(rows[side], c) * LOGIT_SCALE
            w = 0.5 * jnp.exp(s - row_lse) + 0.5 * jnp.exp(s - col_lse)
            if k == 0:
                i = lax.broadcasted_iota(jnp.int32, s.shape, 0)
                j = lax.broadcasted_iota(jnp.int32, s.shape, 1)
                w = w - ((i == j) & (i < n)).astype(F32)
            total = total + jnp.dot(w.astype(BF16), c, preferred_element_type=F32)
        kept[side] = LOGIT_SCALE * total[:n]
        sent[side] = LOGIT_SCALE * total[n:]


def add_kernel(kept, got, image_grad, text_grad):
    image_grad[...] = kept[0] + got[0]
    text_grad[...] = kept[1] + got[1]


def body(image_embeds, text_embeds):
    n, width = image_embeds.shape
    count = lax.axis_size("batch")
    assert count % 2 == 0
    piece = jax.ShapeDtypeStruct((n, width), BF16)
    i0, t0, own, for_pair, for_across = call(
        cast_kernel,
        (piece, piece, jax.ShapeDtypeStruct((2 * n, width), BF16), piece, piece),
        [pltpu.VMEM((n, width), F32), pltpu.VMEM((n, width), F32), pltpu.SemaphoreType.DMA((2,))],
        0, image_embeds, text_embeds, remote=(0, 1),
    )
    a_t, a_i = along(t0, 2), along(i0, -2)
    pair, across = in_pair(for_pair), across_pairs(for_across)
    b2 = in_pair(jnp.concatenate([a_t, a_i]))
    x = over_x(own)
    far = [over_x(v) for v in (a_t, a_i, b2, pair, across)]
    core = over_core(own)
    corex = over_core(x)
    send = call(
        functools.partial(stats_kernel, count),
        jax.ShapeDtypeStruct((count * SPANS, 2 * SPANS, n), F32),
        [pltpu.VMEM((2, SPANS * n, width), BF16), pltpu.VMEM((2, STEPS, n, width), BF16)],
        4 * SPANS * n * STEPS * n * width,
        own, core, x, corex, a_t, a_i, b2, pair, across,
    )
    got = lax.all_to_all(send, AXES, 0, 0, tiled=True)
    row = jax.ShapeDtypeStruct((n,), F32)
    both = jax.ShapeDtypeStruct((2, n, width), F32)
    image_lse, text_lse, kept, sent = call(
        functools.partial(grad_kernel, count),
        (row, row, both, both),
        [pltpu.VMEM((2, 2 * n, width), BF16), pltpu.VMEM((2, STEPS, 2 * n, width), BF16)],
        8 * 2 * n * STEPS * 2 * n * width,
        got, own, core, x, a_t, a_i, b2, pair, across, *far,
    )
    grad = jax.ShapeDtypeStruct((n, width), F32)
    image_grad, text_grad = call(add_kernel, (grad, grad), [], 0, kept, over_core(sent))
    return (image_lse, text_lse, image_grad, text_grad)


def solution(mesh):
    in_specs = (P(("batch", "span"), None), P(("batch", "span"), None))
    out_specs = (
        P(("batch", "span")),
        P(("batch", "span")),
        P(("batch", "span"), None),
        P(("batch", "span"), None),
    )
    return jax.shard_map(body, mesh=mesh, in_specs=in_specs, out_specs=out_specs, check_vma=False)
```

time: 80.8 us -> 72 us (0.89)
  waiting for transfers between devices: 47.3 us -> 40.8 us
  starting transfers between devices: 22.3 us -> 19.4 us
    ppermute x16 -> x14, waiting for transfers between devices: 47.3 us -> 40.8 us  [moved(): return lax.ppermute(value, AXES, pairs)]
    all_to_all x1, starting transfers between devices: 6.27 us -> 3.09 us  [body(): got = lax.all_to_all(send, AXES, 0, 0, tiled=True)]
    ppermute x16 -> x14, starting transfers between devices: 16 us -> 16.3 us  [moved(): return lax.ppermute(value, AXES, pairs)]
  transfers between devices with their start and end apart: 17 -> 15, of which waited for: 11 -> 9; matrix products, arithmetic and copies ran while one was open for 0% -> 0% of each run, Pallas kernels for 3% -> 3%
where the time goes in v3:
time: 72 us; the launch traced here: 71.7 us
  waiting for transfers between devices  40.8 us (57%)
  starting transfers between devices  19.4 us (27%)
  Pallas kernels  7.13 us (10%)
  local copies, waits for them, and re-layouts  3.59 us (5%)
    ppermute x14, waiting for transfers between devices, moved(): return lax.ppermute(value, AXES, pairs)  40.8 us
    ppermute x14, starting transfers between devices, moved(): return lax.ppermute(value, AXES, pairs)  16.3 us
    pallas_call x4, Pallas kernels, call(): pl.pallas_call(kernel, out_shape=out_shape, in_specs=[pl.BlockSpec(memory...  7.13 us
    unnamed x8, local copies, waits for them, and re-layouts  3.59 us
    all_to_all x1, starting transfers between devices, body(): got = lax.all_to_all(send, AXES, 0, 0, tiled=True)  3.09 us
  transfers between devices with their start and end apart: 15, of which 9 were waited for; matrix products, arithmetic and copies ran while one was open for 0% of the time, Pallas kernels for 3%

profile of v3, /device:TPU:0, one launch (start us, length us, event | category | flops | bytes accessed | tf_op | source)
XLA Modules:
  0.0 71.7 jit_solution(16364381088912129492)
XLA Ops:
  0.6 1.0 %copy-done = f32[128,768]{1,0:T(8,128)S(1)} copy-done((f32[128,768]{1,0:T(8,128)S(1)}, f32[128,768]{1,0:T(8,128)}, u32[]{:S(2)}) %copy-start) | copy-done | bytes 393240
  1.6 1.0 %copy-done.1 = f32[128,768]{1,0:T(8,128)S(1)} copy-done((f32[128,768]{1,0:T(8,128)S(1)}, f32[128,768]{1,0:T(8,128)}, u32[]{:S(2)}) %copy-start.1) | copy-done | bytes 393240
  3.1 3.0 %collective-permute-start.1 = (bf16[256,768]{1,0:T(8,128)(2,1)S(1)}, bf16[256,768]{1,0:T(8,128)(2,1)S(1)}, u32[]{:S(2)}, u32[]{:S(2)}) collective-permute-start(bf16[256,768]{1,0:T(8,128)(2,1)S(1)} %get-tuple-element.15.refs_0_.refs_1_), channel_id=1, source_target_pairs={{0,2},{1,3},{2,0},{3,1},{4,6},{5,7},{6,4},{7,5},{8,10},{9,11},{10,... | collective-permute-start | bytes 1179656 | tf_op jit(solution)/shard_map/ppermute | solution.py:25
  6.1 1.6 %collective-permute-start.3 = (bf16[128,768]{1,0:T(8,128)(2,1)S(1)}, bf16[128,768]{1,0:T(8,128)(2,1)S(1)}, u32[]{:S(2)}, u32[]{:S(2)}) collective-permute-start(bf16[128,768]{1,0:T(8,128)(2,1)S(1)} %get-tuple-element.16), channel_id=1, source_target_pairs={{0,8},{1,9},{2,10},{3,11},{4,12},{5,13},{6,14},{7,15},{8,16},{9,17... | collective-permute-start | bytes 589832 | tf_op jit(solution)/shard_map/ppermute | solution.py:25
  7.7 2.2 %collective-permute-start.4 = (bf16[128,768]{1,0:T(8,128)(2,1)S(1)}, bf16[128,768]{1,0:T(8,128)(2,1)S(1)}, u32[]{:S(2)}, u32[]{:S(2)}) collective-permute-start(bf16[128,768]{1,0:T(8,128)(2,1)S(1)} %get-tuple-element.17), channel_id=1, source_target_pairs={{0,24},{1,25},{2,26},{3,27},{4,28},{5,29},{6,30},{7,31},{8,0},{9,1... | collective-permute-start | bytes 589832 | tf_op jit(solution)/shard_map/ppermute | solution.py:25
  10.0 5.8 %collective-permute-done.3.refs_4_ = bf16[128,768]{1,0:T(8,128)(2,1)S(1)} collective-permute-done((bf16[128,768]{1,0:T(8,128)(2,1)S(1)}, bf16[128,768]{1,0:T(8,128)(2,1)S(1)}, u32[]{:S(2)}, u32[]{:S(2)}) %collective-permute-start.3) | collective-permute-done | bytes 196640 | tf_op jit(solution)/shard_map/ppermute | solution.py:25
  15.8 2.2 %collective-permute-done.4.refs_5_ = bf16[128,768]{1,0:T(8,128)(2,1)S(1)} collective-permute-done((bf16[128,768]{1,0:T(8,128)(2,1)S(1)}, bf16[128,768]{1,0:T(8,128)(2,1)S(1)}, u32[]{:S(2)}, u32[]{:S(2)}) %collective-permute-start.4) | collective-permute-done | bytes 196640 | tf_op jit(solution)/shard_map/ppermute | solution.py:25
  18.0 1.6 %collective-permute-start.5 = (bf16[256,768]{1,0:T(8,128)(2,1)S(1)}, bf16[256,768]{1,0:T(8,128)(2,1)S(1)}, u32[]{:S(2)}, u32[]{:S(2)}) collective-permute-start(bf16[256,768]{1,0:T(8,128)(2,1)S(1)} %pad_maximum_fusion), channel_id=1, source_target_pairs={{0,4},{1,5},{2,6},{3,7},{4,0},{5,1},{6,2},{7,3},{8,12},{9,13},{10,... | collective-permute-start | bytes 1179656 | tf_op jit(solution)/shard_map/ppermute | solution.py:25
  20.6 2.2 %collective-permute-start.7 = (bf16[128,768]{1,0:T(8,128)(2,1)S(1)}, bf16[128,768]{1,0:T(8,128)(2,1)S(1)}, u32[]{:S(2)}, u32[]{:S(2)}) collective-permute-start(bf16[128,768]{1,0:T(8,128)(2,1)S(1)} %get-tuple-element.19), channel_id=1, source_target_pairs={{0,20},{1,21},{2,22},{3,23},{4,16},{5,17},{6,18},{7,19},{8,28},{9,... | collective-permute-start | bytes 589832 | tf_op jit(solution)/shard_map/ppermute | solution.py:25
  22.9 11.5 %collective-permute-done.5.refs_6_ = bf16[256,768]{1,0:T(8,128)(2,1)S(1)} collective-permute-done((bf16[256,768]{1,0:T(8,128)(2,1)S(1)}, bf16[256,768]{1,0:T(8,128)(2,1)S(1)}, u32[]{:S(2)}, u32[]{:S(2)}) %collective-permute-start.5) | collective-permute-done | bytes 393248 | tf_op jit(solution)/shard_map/ppermute | solution.py:25
  34.9 2.0 %collective-permute-done.6.refs_7_ = bf16[128,768]{1,0:T(8,128)(2,1)S(1)} collective-permute-done((bf16[128,768]{1,0:T(8,128)(2,1)S(1)}, bf16[128,768]{1,0:T(8,128)(2,1)S(1)}, u32[]{:S(2)}, u32[]{:S(2)}) %collective-permute-start.6) | collective-permute-done | bytes 196640 | tf_op jit(solution)/shard_map/ppermute | solution.py:25
  36.9 2.2 %shard_map.58 = f32[32,8,128]{2,1,0:T(8,128)} custom-call(bf16[256,768]{1,0:T(8,128)(2,1)S(1)} %get-tuple-element.15.refs_0_.refs_1_, bf16[256,768]{1,0:T(8,128)(2,1)S(1)} %collective-permute-done.refs_1_.refs_2_, bf16[256,768]{1,0:T(8,128)(2,1)S(1)} %collective-permute-done.1.refs_2_.refs_3_, bf16[256,768]{1,0:T(8,128)(2,1)S(1)} %collective-permute-done.2.refs_3_, ...), custom_call_target="tpu_custom_call" | custom-call | flops 805306368 | bytes 2752512 | tf_op jit(solution)/shard_map/pallas_call | solution.py:55
  39.1 3.1 %all-to-all-start = ((f32[32,8,128]{2,1,0:T(8,128)}), f32[32,8,128]{2,1,0:T(8,128)S(1)}, u32[]{:S(2)}, u32[]{:S(2)}) async-start(f32[32,8,128]{2,1,0:T(8,128)} %shard_map.58), calls=%async_computation | async-start | bytes 262144 | tf_op jit(solution)/shard_map/all_to_all | solution.py:203
  42.2 1.8 %collective-permute-start.8 = (bf16[128,768]{1,0:T(8,128)(2,1)S(1)}, bf16[128,768]{1,0:T(8,128)(2,1)S(1)}, u32[]{:S(2)}, u32[]{:S(2)}) collective-permute-start(bf16[128,768]{1,0:T(8,128)(2,1)S(1)} %collective-permute-done.3.refs_4_), channel_id=1, source_target_pairs={{0,2},{1,3},{2,0},{3,1},{4,6},{5,7},{6,4},{7,5},{8,10},{9,11},{10,... | collective-permute-start | bytes 589832 | tf_op jit(solution)/shard_map/ppermute | solution.py:25
  44.3 1.8 %collective-permute-start.11 = (bf16[128,768]{1,0:T(8,128)(2,1)S(1)}, bf16[128,768]{1,0:T(8,128)(2,1)S(1)}, u32[]{:S(2)}, u32[]{:S(2)}) collective-permute-start(bf16[128,768]{1,0:T(8,128)(2,1)S(1)} %collective-permute-done.6.refs_7_), channel_id=1, source_target_pairs={{0,2},{1,3},{2,0},{3,1},{4,6},{5,7},{6,4},{7,5},{8,10},{9,11},{10,... | collective-permute-start | bytes 589832 | tf_op jit(solution)/shard_map/ppermute | solution.py:25
  46.3 4.8 %collective-permute-done.8.refs_9_ = bf16[128,768]{1,0:T(8,128)(2,1)S(1)} collective-permute-done((bf16[128,768]{1,0:T(8,128)(2,1)S(1)}, bf16[128,768]{1,0:T(8,128)(2,1)S(1)}, u32[]{:S(2)}, u32[]{:S(2)}) %collective-permute-start.8) | collective-permute-done | bytes 196640 | tf_op jit(solution)/shard_map/ppermute | solution.py:25
  51.2 4.2 %collective-permute-done.9.refs_10_ = bf16[128,768]{1,0:T(8,128)(2,1)S(1)} collective-permute-done((bf16[128,768]{1,0:T(8,128)(2,1)S(1)}, bf16[128,768]{1,0:T(8,128)(2,1)S(1)}, u32[]{:S(2)}, u32[]{:S(2)}) %collective-permute-start.9) | collective-permute-done | bytes 196640 | tf_op jit(solution)/shard_map/ppermute | solution.py:25
  55.4 4.2 %collective-permute-done.11.refs_12_ = bf16[128,768]{1,0:T(8,128)(2,1)S(1)} collective-permute-done((bf16[128,768]{1,0:T(8,128)(2,1)S(1)}, bf16[128,768]{1,0:T(8,128)(2,1)S(1)}, u32[]{:S(2)}, u32[]{:S(2)}) %collective-permute-start.11) | collective-permute-done | bytes 196640 | tf_op jit(solution)/shard_map/ppermute | solution.py:25
  59.6 3.7 %collective-permute-done.12.refs_13_ = bf16[128,768]{1,0:T(8,128)(2,1)S(1)} collective-permute-done((bf16[128,768]{1,0:T(8,128)(2,1)S(1)}, bf16[128,768]{1,0:T(8,128)(2,1)S(1)}, u32[]{:S(2)}, u32[]{:S(2)}) %collective-permute-start.12) | collective-permute-done | bytes 196640 | tf_op jit(solution)/shard_map/ppermute | solution.py:25
  63.3 0.7 copy-done.2
  64.0 0.9 %copy-done.3 = bf16[128,768]{1,0:T(8,128)(2,1)S(1)} copy-done((bf16[128,768]{1,0:T(8,128)(2,1)S(1)}, bf16[128,768]{1,0:T(8,128)(2,1)}, u32[]{:S(2)}) %copy-start.3) | copy-done | bytes 196632
  65.0 3.5 %shard_map.59 = (f32[128]{0:T(128)}, f32[128]{0:T(128)}, f32[2,128,768]{2,1,0:T(8,128)S(1)}, f32[2,128,768]{2,1,0:T(8,128)S(1)}) custom-call(f32[32,8,128]{2,1,0:T(8,128)S(1)} %all-to-all-done.refs_0_, bf16[256,768]{1,0:T(8,128)(2,1)S(1)} %get-tuple-element.15.refs_0_.refs_1_, bf16[256,768]{1,0:T(8,128)(2,1)S(1)} %collective-permute-done.refs_1_.refs_2_, ...), custom_call_target="tpu_custom_call" | custom-call | flops 1610612736 | bytes 3670016 | tf_op jit(solution)/shard_map/pallas_call | solution.py:55
  68.4 2.3 %collective-permute-done.13.got = f32[2,128,768]{2,1,0:T(8,128)S(1)} collective-permute-done((f32[2,128,768]{2,1,0:T(8,128)S(1)}, f32[2,128,768]{2,1,0:T(8,128)S(1)}, u32[]{:S(2)}, u32[]{:S(2)}) %collective-permute-start.13) | collective-permute-done | bytes 786464 | tf_op jit(solution)/shard_map/ppermute | solution.py:25
  70.7 1.0 %shard_map.60 = (f32[128,768]{1,0:T(8,128)}, f32[128,768]{1,0:T(8,128)}) custom-call(f32[2,128,768]{2,1,0:T(8,128)S(1)} %get-tuple-element.22.kept, f32[2,128,768]{2,1,0:T(8,128)S(1)} %collective-permute-done.13.got), custom_call_target="tpu_custom_call" | custom-call | bytes 1572864 | tf_op jit(solution)/shard_map/pallas_call | solution.py:55
  (19 shorter events, 2.6 us)
Async XLA Ops:
  0.6 1.0 %copy-start = (f32[128,768]{1,0:T(8,128)S(1)}, f32[128,768]{1,0:T(8,128)}, u32[]{:S(2)}) copy-start(f32[128,768]{1,0:T(8,128)} %image.1) | copy-start | bytes 1179652
  1.6 1.0 %copy-start.1 = (f32[128,768]{1,0:T(8,128)S(1)}, f32[128,768]{1,0:T(8,128)}, u32[]{:S(2)}) copy-start(f32[128,768]{1,0:T(8,128)} %text.1) | copy-start | bytes 1179652
  3.1 16.5 %collective-permute-start.1 = (bf16[256,768]{1,0:T(8,128)(2,1)S(1)}, bf16[256,768]{1,0:T(8,128)(2,1)S(1)}, u32[]{:S(2)}, u32[]{:S(2)}) collective-permute-start(bf16[256,768]{1,0:T(8,128)(2,1)S(1)} %get-tuple-element.15.refs_0_.refs_1_), channel_id=1, source_target_pairs={{0,2},{1,3},{2,0},{3,1},{4,6},{5,7},{6,4},{7,5},{8,10},{9,11},{10,... | collective-permute-start | bytes 1179656 | tf_op jit(solution)/shard_map/ppermute | solution.py:25
  6.1 9.7 %collective-permute-start.3 = (bf16[128,768]{1,0:T(8,128)(2,1)S(1)}, bf16[128,768]{1,0:T(8,128)(2,1)S(1)}, u32[]{:S(2)}, u32[]{:S(2)}) collective-permute-start(bf16[128,768]{1,0:T(8,128)(2,1)S(1)} %get-tuple-element.16), channel_id=1, source_target_pairs={{0,8},{1,9},{2,10},{3,11},{4,12},{5,13},{6,14},{7,15},{8,16},{9,17... | collective-permute-start | bytes 589832 | tf_op jit(solution)/shard_map/ppermute | solution.py:25
  7.7 10.3 %collective-permute-start.4 = (bf16[128,768]{1,0:T(8,128)(2,1)S(1)}, bf16[128,768]{1,0:T(8,128)(2,1)S(1)}, u32[]{:S(2)}, u32[]{:S(2)}) collective-permute-start(bf16[128,768]{1,0:T(8,128)(2,1)S(1)} %get-tuple-element.17), channel_id=1, source_target_pairs={{0,24},{1,25},{2,26},{3,27},{4,28},{5,29},{6,30},{7,31},{8,0},{9,1... | collective-permute-start | bytes 589832 | tf_op jit(solution)/shard_map/ppermute | solution.py:25
  18.0 16.3 %collective-permute-start.5 = (bf16[256,768]{1,0:T(8,128)(2,1)S(1)}, bf16[256,768]{1,0:T(8,128)(2,1)S(1)}, u32[]{:S(2)}, u32[]{:S(2)}) collective-permute-start(bf16[256,768]{1,0:T(8,128)(2,1)S(1)} %pad_maximum_fusion), channel_id=1, source_target_pairs={{0,4},{1,5},{2,6},{3,7},{4,0},{5,1},{6,2},{7,3},{8,12},{9,13},{10,... | collective-permute-start | bytes 1179656 | tf_op jit(solution)/shard_map/ppermute | solution.py:25
  19.6 17.3 %collective-permute-start = (bf16[256,768]{1,0:T(8,128)(2,1)S(1)}, bf16[256,768]{1,0:T(8,128)(2,1)S(1)}, u32[]{:S(2)}, u32[]{:S(2)}) collective-permute-start(bf16[256,768]{1,0:T(8,128)(2,1)S(1)} %get-tuple-element.15.refs_0_.refs_1_), channel_id=1, source_target_pairs={{0,1},{1,0},{2,3},{3,2},{4,5},{5,4},{6,7},{7,6},{8,9},{9,8},{10,11... | collective-permute-start | bytes 1179656 | tf_op jit(solution)/shard_map/ppermute | solution.py:25
  19.6 17.3 %collective-permute-start.2 = (bf16[256,768]{1,0:T(8,128)(2,1)S(1)}, bf16[256,768]{1,0:T(8,128)(2,1)S(1)}, u32[]{:S(2)}, u32[]{:S(2)}) collective-permute-start(bf16[256,768]{1,0:T(8,128)(2,1)S(1)} %collective-permute-done.1.refs_2_.refs_3_), channel_id=1, source_target_pairs={{0,1},{1,0},{2,3},{3,2},{4,5},{5,4},{6,7},{7,6},{8,9},{9,8},{10,11... | collective-permute-start | bytes 1179656 | tf_op jit(solution)/shard_map/ppermute | solution.py:25
  20.1 16.8 %collective-permute-start.6 = (bf16[128,768]{1,0:T(8,128)(2,1)S(1)}, bf16[128,768]{1,0:T(8,128)(2,1)S(1)}, u32[]{:S(2)}, u32[]{:S(2)}) collective-permute-start(bf16[128,768]{1,0:T(8,128)(2,1)S(1)} %get-tuple-element.18), channel_id=1, source_target_pairs={{0,4},{1,5},{2,6},{3,7},{4,0},{5,1},{6,2},{7,3},{8,12},{9,13},{10,... | collective-permute-start | bytes 589832 | tf_op jit(solution)/shard_map/ppermute | solution.py:25
  20.6 16.3 %collective-permute-start.7 = (bf16[128,768]{1,0:T(8,128)(2,1)S(1)}, bf16[128,768]{1,0:T(8,128)(2,1)S(1)}, u32[]{:S(2)}, u32[]{:S(2)}) collective-permute-start(bf16[128,768]{1,0:T(8,128)(2,1)S(1)} %get-tuple-element.19), channel_id=1, source_target_pairs={{0,20},{1,21},{2,22},{3,23},{4,16},{5,17},{6,18},{7,19},{8,28},{9,... | collective-permute-start | bytes 589832 | tf_op jit(solution)/shard_map/ppermute | solution.py:25
  34.4 29.7 %collective-permute-start.10 = (bf16[256,768]{1,0:T(8,128)(2,1)S(1)}, bf16[256,768]{1,0:T(8,128)(2,1)S(1)}, u32[]{:S(2)}, u32[]{:S(2)}) collective-permute-start(bf16[256,768]{1,0:T(8,128)(2,1)S(1)} %collective-permute-done.5.refs_6_), channel_id=1, source_target_pairs={{0,2},{1,3},{2,0},{3,1},{4,6},{5,7},{6,4},{7,5},{8,10},{9,11},{10,... | collective-permute-start | bytes 1179656 | tf_op jit(solution)/shard_map/ppermute | solution.py:25
  39.1 24.9 %all-to-all-start = ((f32[32,8,128]{2,1,0:T(8,128)}), f32[32,8,128]{2,1,0:T(8,128)S(1)}, u32[]{:S(2)}, u32[]{:S(2)}) async-start(f32[32,8,128]{2,1,0:T(8,128)} %shard_map.58), calls=%async_computation | async-start | bytes 262144 | tf_op jit(solution)/shard_map/all_to_all | solution.py:203
  42.2 9.0 %collective-permute-start.8 = (bf16[128,768]{1,0:T(8,128)(2,1)S(1)}, bf16[128,768]{1,0:T(8,128)(2,1)S(1)}, u32[]{:S(2)}, u32[]{:S(2)}) collective-permute-start(bf16[128,768]{1,0:T(8,128)(2,1)S(1)} %collective-permute-done.3.refs_4_), channel_id=1, source_target_pairs={{0,2},{1,3},{2,0},{3,1},{4,6},{5,7},{6,4},{7,5},{8,10},{9,11},{10,... | collective-permute-start | bytes 589832 | tf_op jit(solution)/shard_map/ppermute | solution.py:25
  44.1 11.3 %collective-permute-start.9 = (bf16[128,768]{1,0:T(8,128)(2,1)S(1)}, bf16[128,768]{1,0:T(8,128)(2,1)S(1)}, u32[]{:S(2)}, u32[]{:S(2)}) collective-permute-start(bf16[128,768]{1,0:T(8,128)(2,1)S(1)} %collective-permute-done.4.refs_5_), channel_id=1, source_target_pairs={{0,2},{1,3},{2,0},{3,1},{4,6},{5,7},{6,4},{7,5},{8,10},{9,11},{10,... | collective-permute-start | bytes 589832 | tf_op jit(solution)/shard_map/ppermute | solution.py:25
  44.3 15.3 %collective-permute-start.11 = (bf16[128,768]{1,0:T(8,128)(2,1)S(1)}, bf16[128,768]{1,0:T(8,128)(2,1)S(1)}, u32[]{:S(2)}, u32[]{:S(2)}) collective-permute-start(bf16[128,768]{1,0:T(8,128)(2,1)S(1)} %collective-permute-done.6.refs_7_), channel_id=1, source_target_pairs={{0,2},{1,3},{2,0},{3,1},{4,6},{5,7},{6,4},{7,5},{8,10},{9,11},{10,... | collective-permute-start | bytes 589832 | tf_op jit(solution)/shard_map/ppermute | solution.py:25
  46.1 17.3 %collective-permute-start.12 = (bf16[128,768]{1,0:T(8,128)(2,1)S(1)}, bf16[128,768]{1,0:T(8,128)(2,1)S(1)}, u32[]{:S(2)}, u32[]{:S(2)}) collective-permute-start(bf16[128,768]{1,0:T(8,128)(2,1)S(1)} %collective-permute-done.7.refs_8_), channel_id=1, source_target_pairs={{0,2},{1,3},{2,0},{3,1},{4,6},{5,7},{6,4},{7,5},{8,10},{9,11},{10,... | collective-permute-start | bytes 589832 | tf_op jit(solution)/shard_map/ppermute | solution.py:25
  63.3 0.7 copy-start.2
  64.0 0.9 %copy-start.3 = (bf16[128,768]{1,0:T(8,128)(2,1)S(1)}, bf16[128,768]{1,0:T(8,128)(2,1)}, u32[]{:S(2)}) copy-start(bf16[128,768]{1,0:T(8,128)(2,1)} %copy-done.2) | copy-start | bytes 589828
  68.4 2.3 %collective-permute-start.13 = (f32[2,128,768]{2,1,0:T(8,128)S(1)}, f32[2,128,768]{2,1,0:T(8,128)S(1)}, u32[]{:S(2)}, u32[]{:S(2)}) collective-permute-start(f32[2,128,768]{2,1,0:T(8,128)S(1)} %get-tuple-element.23), channel_id=1, source_target_pairs={{0,1},{1,0},{2,3},{3,2},{4,5},{5,4},{6,7},{7,6},{8,9},{9,8},{10,11... | collective-permute-start | bytes 2359304 | tf_op jit(solution)/shard_map/ppermute | solution.py:25

commit v4 on v3

--- a/solution.py
+++ b/solution.py
@@ -12,7 +12,7 @@
 AXES = ("batch", "span")
 SPANS = 4
 F32, BF16 = jnp.float32, jnp.bfloat16
-VMEM_LIMIT = 32 * 1024 * 1024
+VMEM_LIMIT = 16 * 1024 * 1024
 
 
 def moved(value, target):
@@ -45,6 +45,10 @@
     return moved(value, lambda b, s: (b + (3 if b % 2 else -3), s))
 
 
+def after(value, first):
+    return lax.optimization_barrier((value, first))[0]
+
+
 def dot_t(a, b):
     return lax.dot_general(a, b, (((1,), (1,)), ((), ())), preferred_element_type=F32)
 
@@ -55,7 +59,7 @@
     return pl.pallas_call(
         kernel,
         out_shape=out_shape,
-        in_specs=[pl.BlockSpec(memory_space=pl.ANY) if i in remote else whole for i in range(len(args))],
+        in_specs=[pl.BlockSpec(memory_space=pltpu.HBM) if i in remote else whole for i in range(len(args))],
         out_specs=jax.tree.map(lambda _: whole, out_shape),
         scratch_shapes=scratch,
         compiler_params=pltpu.CompilerParams(vmem_limit_bytes=VMEM_LIMIT),
@@ -63,52 +67,39 @@
     )(*args)
 
 
-def cast_kernel(image, text, i_out, t_out, own, for_pair, for_across, i_in, t_in, sems):
-    load_i = pltpu.make_async_copy(image, i_in, sems.at[0])
-    load_t = pltpu.make_async_copy(text, t_in, sems.at[1])
-    load_i.start()
-    load_t.start()
+def pack_kernel(image, text, own, for_pair, for_across):
     n = image.shape[0]
     odd = lax.rem(lax.axis_index("batch"), 2)
-    load_i.wait()
-    i = i_in[...].astype(BF16)
-    i_out[...] = i
-    own[n:] = i
-    load_t.wait()
-    t = t_in[...].astype(BF16)
-    t_out[...] = t
-    own[:n] = t
+    own[:n] = text[...]
+    own[n:] = image[...]
 
     @pl.when(odd == 0)
     def _():
-        for_pair[...] = t
-        for_across[...] = i
+        for_pair[...] = text[...]
+        for_across[...] = image[...]
 
     @pl.when(odd == 1)
     def _():
-        for_pair[...] = i
-        for_across[...] = t
-
-
-def fill_columns(cols, place, odd, own, a_t, a_i, b, pair, across):
-    n = a_t.shape[0]
+        for_pair[...] = image[...]
+        for_across[...] = text[...]
+
+
+def fill_columns(cols, place, odd, own, ab, b, pc):
+    n = own.shape[0] // 2
     at = slice(place * n, (place + 1) * n)
-    cols[0, 0, at] = own[:n]
-    cols[1, 0, at] = own[n:]
-    cols[0, 1, at] = a_t[...]
-    cols[1, 1, at] = a_i[...]
-    cols[0, 2, at] = b[:n]
-    cols[1, 2, at] = b[n:]
-    cols[1 - odd, 3, at] = pair[...]
-    cols[odd, 3, at] = across[...]
+    for side in range(2):
+        for slot, ref in enumerate((own, ab, b)):
+            cols[side, slot, at] = ref[side * n : (side + 1) * n]
+    cols[1 - odd, 3, at] = pc[:n]
+    cols[odd, 3, at] = pc[n:]
 
 
 def stats_kernel(count, *refs):
-    own, core, x, corex, a_t, a_i, b2, pair, across, out, rows, cols = refs
-    n = a_t.shape[0]
+    own, core, x, corex, ab, b2, pc, out, rows, cols = refs
+    n = own.shape[0] // 2
     pos = lax.axis_index("span")
     odd = lax.rem(lax.axis_index("batch"), 2)
-    fill_columns(cols, 0, odd, own, a_t, a_i, b2, pair, across)
+    fill_columns(cols, 0, odd, own, ab, b2, pc)
     part = []
     for side in range(2):
         for q, ref in enumerate((own, core, x, corex)):
@@ -129,20 +120,23 @@
 
 
 def grad_kernel(count, *refs):
-    got, own, core, x, a_t, a_i, b2, pair, across, ax_t, ax_i, bx2, pairx, acrossx = refs[:14]
-    image_lse, text_lse, kept, sent, rows, cols = refs[14:]
-    n = a_t.shape[0]
+    got, own, core, x, ab, b2, pc, abx, bx2, pcx = refs[:10]
+    image_lse, text_lse, kept, sent, got_in, rows, cols, sem = refs[10:]
+    load = pltpu.make_async_copy(got, got_in, sem)
+    load.start()
+    n = own.shape[0] // 2
     b = lax.axis_index("batch")
     odd = lax.rem(b, 2)
 
     def lse_of(block):
         at = lax.rem(block + count, count) * SPANS
-        v = [got[at + s] for s in range(SPANS)]
+        v = [got_in[at + s] for s in range(SPANS)]
         top = jnp.maximum(jnp.maximum(v[0], v[1]), jnp.maximum(v[2], v[3]))
         return top + jnp.log(sum(jnp.exp(a - top) for a in v))
 
-    fill_columns(cols, 0, odd, own, a_t, a_i, b2, pair, across)
-    fill_columns(cols, 1, odd, x, ax_t, ax_i, bx2, pairx, acrossx)
+    fill_columns(cols, 0, odd, own, ab, b2, pc)
+    fill_columns(cols, 1, odd, x, abx, bx2, pcx)
+    load.wait()
     mine = lse_of(b)
     image_lse[...] = mine[0]
     text_lse[...] = mine[4]
@@ -180,35 +174,41 @@
     count = lax.axis_size("batch")
     assert count % 2 == 0
     piece = jax.ShapeDtypeStruct((n, width), BF16)
-    i0, t0, own, for_pair, for_across = call(
-        cast_kernel,
-        (piece, piece, jax.ShapeDtypeStruct((2 * n, width), BF16), piece, piece),
-        [pltpu.VMEM((n, width), F32), pltpu.VMEM((n, width), F32), pltpu.SemaphoreType.DMA((2,))],
-        0, image_embeds, text_embeds, remote=(0, 1),
+    i0, t0 = image_embeds.astype(BF16), text_embeds.astype(BF16)
+    own, for_pair, for_across = call(
+        pack_kernel, (jax.ShapeDtypeStruct((2 * n, width), BF16), piece, piece), [], 0, i0, t0
     )
     a_t, a_i = along(t0, 2), along(i0, -2)
     pair, across = in_pair(for_pair), across_pairs(for_across)
-    b2 = in_pair(jnp.concatenate([a_t, a_i]))
+    ab, pc = jnp.concatenate([a_t, a_i]), jnp.concatenate([pair, across])
+    b2 = in_pair(ab)
+    core = over_core(own)
     x = over_x(own)
-    far = [over_x(v) for v in (a_t, a_i, b2, pair, across)]
-    core = over_core(own)
     corex = over_core(x)
+    far_ab, far_b, far_pc = [over_x(v) for v in (ab, b2, pc)]
+    far_ab, core, _ = lax.optimization_barrier((far_ab, core, over_core(pc)))
     send = call(
         functools.partial(stats_kernel, count),
         jax.ShapeDtypeStruct((count * SPANS, 2 * SPANS, n), F32),
         [pltpu.VMEM((2, SPANS * n, width), BF16), pltpu.VMEM((2, STEPS, n, width), BF16)],
         4 * SPANS * n * STEPS * n * width,
-        own, core, x, corex, a_t, a_i, b2, pair, across,
-    )
+        own, core, x, corex, ab, b2, pc,
+    )
+    far_pc, send = lax.optimization_barrier((far_pc, send))
     got = lax.all_to_all(send, AXES, 0, 0, tiled=True)
     row = jax.ShapeDtypeStruct((n,), F32)
     both = jax.ShapeDtypeStruct((2, n, width), F32)
     image_lse, text_lse, kept, sent = call(
         functools.partial(grad_kernel, count),
         (row, row, both, both),
-        [pltpu.VMEM((2, 2 * n, width), BF16), pltpu.VMEM((2, STEPS, 2 * n, width), BF16)],
+        [
+            pltpu.VMEM(got.shape, F32),
+            pltpu.VMEM((2, 2 * n, width), BF16),
+            pltpu.VMEM((2, STEPS, 2 * n, width), BF16),
+            pltpu.SemaphoreType.DMA,
+        ],
         8 * 2 * n * STEPS * 2 * n * width,
-        got, own, core, x, a_t, a_i, b2, pair, across, *far,
+        got, own, core, x, ab, b2, pc, far_ab, far_b, far_pc, remote=(0,),
     )
     grad = jax.ShapeDtypeStruct((n, width), F32)
     image_grad, text_grad = call(add_kernel, (grad, grad), [], 0, kept, over_core(sent))

time: 72 us -> 58.2 us (0.81)
  waiting for transfers between devices: 40.8 us -> 22.9 us
  starting transfers between devices: 19.4 us -> 25.2 us
  local copies, waits for them, and re-layouts: 3.59 us -> 0.06 us
  other arithmetic: 0.03 us -> 1.09 us
  Pallas kernels: 7.13 us -> 7.98 us
    ppermute x14 -> x12, waiting for transfers between devices: 40.8 us -> 17.9 us  [moved(): return lax.ppermute(value, AXES, pairs)]
    all_to_all x1, waiting for transfers between devices: 0.01 us -> 4.99 us  [body(): got = lax.all_to_all(send, AXES, 0, 0, tiled=True)]
    ppermute x14 -> x12, starting transfers between devices: 16.3 us -> 21 us  [moved(): return lax.ppermute(value, AXES, pairs)]
    unnamed x8 -> x4, local copies, waits for them, and re-layouts: 3.59 us -> 0.03 us
    convert_element_type x0 -> x2, other arithmetic: none -> 1.09 us  [body(): i0, t0 = (image_embeds.astype(BF16), text_embeds.astype(BF16))]
    all_to_all x1, starting transfers between devices: 3.09 us -> 4.14 us  [body(): got = lax.all_to_all(send, AXES, 0, 0, tiled=True)]
    pallas_call x4, Pallas kernels: 7.13 us -> 7.98 us  [call(): pl.pallas_call(kernel, out_shape=out_shape, in_specs=[pl.BlockSpec(memory...]
  transfers between devices with their start and end apart: 15 -> 13, of which waited for: 9 -> 7; matrix products, arithmetic and copies ran while one was open for 0% -> 0% of each run, Pallas kernels for 3% -> 4%
where the time goes in v4:
time: 58.2 us; the launch traced here: 58 us
  starting transfers between devices  25.2 us (43%)
  waiting for transfers between devices  22.9 us (39%)
  Pallas kernels  7.98 us (14%)
  other arithmetic  1.09 us (2%)
  between operations  0.74 us (1%)
    ppermute x12, starting transfers between devices, moved(): return lax.ppermute(value, AXES, pairs)  21 us
    ppermute x12, waiting for transfers between devices, moved(): return lax.ppermute(value, AXES, pairs)  17.9 us
    pallas_call x4, Pallas kernels, call(): pl.pallas_call(kernel, out_shape=out_shape, in_specs=[pl.BlockSpec(memory...  7.98 us
    all_to_all x1, waiting for transfers between devices, body(): got = lax.all_to_all(send, AXES, 0, 0, tiled=True)  4.99 us
    all_to_all x1, starting transfers between devices, body(): got = lax.all_to_all(send, AXES, 0, 0, tiled=True)  4.14 us
  transfers between devices with their start and end apart: 13, of which 7 were waited for; matrix products, arithmetic and copies ran while one was open for 0% of the time, Pallas kernels for 4%

profile of v4, /device:TPU:0, one launch (start us, length us, event | category | flops | bytes accessed | tf_op | source)
XLA Modules:
  0.0 58.0 jit_solution(8270214606497388683)
XLA Ops:
  0.6 1.1 %convert_element_type.7.text = bf16[128,768]{1,0:T(8,128)(2,1)S(1)} convert(f32[128,768]{1,0:T(8,128)} %param.3) | non-fusion elementwise | flops 98304 | bytes 589824 | tf_op jit(solution)/shard_map/convert_element_type | solution.py:177
  1.7 3.1 %collective-permute-start.3 = (bf16[128,768]{1,0:T(8,128)(2,1)S(1)}, bf16[128,768]{1,0:T(8,128)(2,1)S(1)}, u32[]{:S(2)}, u32[]{:S(2)}) collective-permute-start(bf16[128,768]{1,0:T(8,128)(2,1)S(1)} %convert_element_type.7.text), channel_id=1, source_target_pairs={{0,8},{1,9},{2,10},{3,11},{4,12},{5,13},{6,14},{7,15},{8,16},{9,17... | collective-permute-start | bytes 589832 | tf_op jit(solution)/shard_map/ppermute | solution.py:25
  4.8 2.1 %collective-permute-start.4 = (bf16[128,768]{1,0:T(8,128)(2,1)S(1)}, bf16[128,768]{1,0:T(8,128)(2,1)S(1)}, u32[]{:S(2)}, u32[]{:S(2)}) collective-permute-start(bf16[128,768]{1,0:T(8,128)(2,1)S(1)} %convert_element_type.6.image), channel_id=1, source_target_pairs={{0,24},{1,25},{2,26},{3,27},{4,28},{5,29},{6,30},{7,31},{8,0},{9,1... | collective-permute-start | bytes 589832 | tf_op jit(solution)/shard_map/ppermute | solution.py:25
  6.9 0.1 shard_map.57
  7.0 1.8 %collective-permute-start.7 = (bf16[256,768]{1,0:T(8,128)(2,1)S(1)}, bf16[256,768]{1,0:T(8,128)(2,1)S(1)}, u32[]{:S(2)}, u32[]{:S(2)}) collective-permute-start(bf16[256,768]{1,0:T(8,128)(2,1)S(1)} %get-tuple-element.19.refs_0_.refs_1_), channel_id=1, source_target_pairs={{0,2},{1,3},{2,0},{3,1},{4,6},{5,7},{6,4},{7,5},{8,10},{9,11},{10,... | collective-permute-start | bytes 1179656 | tf_op jit(solution)/shard_map/ppermute | solution.py:25
  8.7 1.5 %collective-permute-start = (bf16[128,768]{1,0:T(8,128)(2,1)S(1)}, bf16[128,768]{1,0:T(8,128)(2,1)S(1)}, u32[]{:S(2)}, u32[]{:S(2)}) collective-permute-start(bf16[128,768]{1,0:T(8,128)(2,1)S(1)} %get-tuple-element.17), channel_id=1, source_target_pairs={{0,4},{1,5},{2,6},{3,7},{4,0},{5,1},{6,2},{7,3},{8,12},{9,13},{10,... | collective-permute-start | bytes 589832 | tf_op jit(solution)/shard_map/ppermute | solution.py:25
  10.3 2.3 %collective-permute-done.3 = bf16[128,768]{1,0:T(8,128)(2,1)S(1)} collective-permute-done((bf16[128,768]{1,0:T(8,128)(2,1)S(1)}, bf16[128,768]{1,0:T(8,128)(2,1)S(1)}, u32[]{:S(2)}, u32[]{:S(2)}) %collective-permute-start.3) | collective-permute-done | bytes 196640 | tf_op jit(solution)/shard_map/ppermute | solution.py:25
  12.6 7.1 %collective-permute-start.1 = (bf16[128,768]{1,0:T(8,128)(2,1)S(1)}, bf16[128,768]{1,0:T(8,128)(2,1)S(1)}, u32[]{:S(2)}, u32[]{:S(2)}) collective-permute-start(bf16[128,768]{1,0:T(8,128)(2,1)S(1)} %get-tuple-element.18), channel_id=1, source_target_pairs={{0,20},{1,21},{2,22},{3,23},{4,16},{5,17},{6,18},{7,19},{8,28},{9,... | collective-permute-start | bytes 589832 | tf_op jit(solution)/shard_map/ppermute | solution.py:25
  19.8 0.1 collective-permute-start.9
  19.9 2.0 %collective-permute-start.5 = (bf16[256,768]{1,0:T(8,128)(2,1)S(1)}, bf16[256,768]{1,0:T(8,128)(2,1)S(1)}, u32[]{:S(2)}, u32[]{:S(2)}) collective-permute-start(bf16[256,768]{1,0:T(8,128)(2,1)S(1)} %constant_dynamic-update-slice_fusion.2.refs_4_), channel_id=1, source_target_pairs={{0,2},{1,3},{2,0},{3,1},{4,6},{5,7},{6,4},{7,5},{8,10},{9,11},{10,... | collective-permute-start | bytes 1179656 | tf_op jit(solution)/shard_map/ppermute | solution.py:25
  21.9 0.1 collective-permute-start.8
  21.9 3.5 %collective-permute-done.1 = bf16[128,768]{1,0:T(8,128)(2,1)S(1)} collective-permute-done((bf16[128,768]{1,0:T(8,128)(2,1)S(1)}, bf16[128,768]{1,0:T(8,128)(2,1)S(1)}, u32[]{:S(2)}, u32[]{:S(2)}) %collective-permute-start.1) | collective-permute-done | bytes 196640 | tf_op jit(solution)/shard_map/ppermute | solution.py:25
  25.4 1.6 %collective-permute-start.2 = (bf16[256,768]{1,0:T(8,128)(2,1)S(1)}, bf16[256,768]{1,0:T(8,128)(2,1)S(1)}, u32[]{:S(2)}, u32[]{:S(2)}) collective-permute-start(bf16[256,768]{1,0:T(8,128)(2,1)S(1)} %constant_dynamic-update-slice_fusion.refs_6_), channel_id=1, source_target_pairs={{0,2},{1,3},{2,0},{3,1},{4,6},{5,7},{6,4},{7,5},{8,10},{9,11},{10,... | collective-permute-start | bytes 1179656 | tf_op jit(solution)/shard_map/ppermute | solution.py:25
  27.0 3.2 %collective-permute-done.9.refs_5_ = bf16[256,768]{1,0:T(8,128)(2,1)S(1)} collective-permute-done((bf16[256,768]{1,0:T(8,128)(2,1)S(1)}, bf16[256,768]{1,0:T(8,128)(2,1)S(1)}, u32[]{:S(2)}, u32[]{:S(2)}) %collective-permute-start.9) | collective-permute-done | bytes 393248 | tf_op jit(solution)/shard_map/ppermute | solution.py:25
  30.2 1.5 %collective-permute-start.10 = (bf16[256,768]{1,0:T(8,128)(2,1)S(1)}, bf16[256,768]{1,0:T(8,128)(2,1)}, u32[]{:S(2)}, u32[]{:S(2)}) collective-permute-start(bf16[256,768]{1,0:T(8,128)(2,1)S(1)} %collective-permute-done.9.refs_5_), channel_id=1, source_target_pairs={{0,2},{1,3},{2,0},{3,1},{4,6},{5,7},{6,4},{7,5},{8,10},{9,11},{10,... | collective-permute-start | bytes 1179656 | tf_op jit(solution)/shard_map/ppermute | solution.py:25
  31.7 2.2 %shard_map.58 = f32[32,8,128]{2,1,0:T(8,128)} custom-call(bf16[256,768]{1,0:T(8,128)(2,1)S(1)} %get-tuple-element.19.refs_0_.refs_1_, bf16[256,768]{1,0:T(8,128)(2,1)S(1)} %collective-permute-done.6.refs_1_.refs_2_, bf16[256,768]{1,0:T(8,128)(2,1)S(1)} %collective-permute-done.7.refs_2_.refs_3_, bf16[256,768]{1,0:T(8,128)(2,1)S(1)} %collective-permute-done.8.refs_3_, ...), custom_call_target="tpu_custom_call" | custom-call | flops 805306368 | bytes 2752512 | tf_op jit(solution)/shard_map/pallas_call | solution.py:59
  33.9 3.6 %collective-permute-done.2.refs_9_ = bf16[256,768]{1,0:T(8,128)(2,1)S(1)} collective-permute-done((bf16[256,768]{1,0:T(8,128)(2,1)S(1)}, bf16[256,768]{1,0:T(8,128)(2,1)S(1)}, u32[]{:S(2)}, u32[]{:S(2)}) %collective-permute-start.2) | collective-permute-done | bytes 393248 | tf_op jit(solution)/shard_map/ppermute | solution.py:25
  37.5 4.1 %all-to-all-start = ((f32[32,8,128]{2,1,0:T(8,128)}), f32[32,8,128]{2,1,0:T(8,128)S(1)}, u32[]{:S(2)}, u32[]{:S(2)}) async-start(f32[32,8,128]{2,1,0:T(8,128)} %shard_map.58), calls=%async_computation | async-start | bytes 262144 | tf_op jit(solution)/shard_map/all_to_all | solution.py:198
  41.7 3.2 %collective-permute-done.10.refs_8_ = bf16[256,768]{1,0:T(8,128)(2,1)} collective-permute-done((bf16[256,768]{1,0:T(8,128)(2,1)S(1)}, bf16[256,768]{1,0:T(8,128)(2,1)}, u32[]{:S(2)}, u32[]{:S(2)}) %collective-permute-start.10) | collective-permute-done | bytes 393248 | tf_op jit(solution)/shard_map/ppermute | solution.py:25
  44.9 5.0 %all-to-all-done.refs_0_ = f32[32,8,128]{2,1,0:T(8,128)S(1)} async-done(((f32[32,8,128]{2,1,0:T(8,128)}), f32[32,8,128]{2,1,0:T(8,128)S(1)}, u32[]{:S(2)}, u32[]{:S(2)}) %all-to-all-start) | async-done | bytes 131104 | tf_op jit(solution)/shard_map/all_to_all | solution.py:198
  49.9 4.8 %shard_map.59 = (f32[128]{0:T(128)}, f32[128]{0:T(128)}, f32[2,128,768]{2,1,0:T(8,128)S(1)}, f32[2,128,768]{2,1,0:T(8,128)S(1)}) custom-call(f32[32,8,128]{2,1,0:T(8,128)S(1)} %all-to-all-done.refs_0_, bf16[256,768]{1,0:T(8,128)(2,1)S(1)} %get-tuple-element.19.refs_0_.refs_1_, bf16[256,768]{1,0:T(8,128)(2,1)S(1)} %collective-permute-done.6.refs_1_.refs_2_, ...), custom_call_target="tpu_custom_call" | custom-call | flops 1610612736 | bytes 3670016 | tf_op jit(solution)/shard_map/pallas_call | solution.py:59
  54.7 0.3 collective-permute-start.11
  55.0 2.1 %collective-permute-done.11.got = f32[2,128,768]{2,1,0:T(8,128)S(1)} collective-permute-done((f32[2,128,768]{2,1,0:T(8,128)S(1)}, f32[2,128,768]{2,1,0:T(8,128)S(1)}, u32[]{:S(2)}, u32[]{:S(2)}) %collective-permute-start.11) | collective-permute-done | bytes 786464 | tf_op jit(solution)/shard_map/ppermute | solution.py:25
  57.0 1.0 %shard_map.60 = (f32[128,768]{1,0:T(8,128)}, f32[128,768]{1,0:T(8,128)}) custom-call(f32[2,128,768]{2,1,0:T(8,128)S(1)} %get-tuple-element.26.kept, f32[2,128,768]{2,1,0:T(8,128)S(1)} %collective-permute-done.11.got), custom_call_target="tpu_custom_call" | custom-call | bytes 1572864 | tf_op jit(solution)/shard_map/pallas_call | solution.py:59
  (14 shorter events, 0.1 us)
Async XLA Ops:
  0.6 4.2 %copy-start = (f32[128,768]{1,0:T(8,128)S(1)}, f32[128,768]{1,0:T(8,128)}, u32[]{:S(2)}) copy-start(f32[128,768]{1,0:T(8,128)} %param.2) | copy-start | bytes 1179652
  1.7 10.9 %collective-permute-start.3 = (bf16[128,768]{1,0:T(8,128)(2,1)S(1)}, bf16[128,768]{1,0:T(8,128)(2,1)S(1)}, u32[]{:S(2)}, u32[]{:S(2)}) collective-permute-start(bf16[128,768]{1,0:T(8,128)(2,1)S(1)} %convert_element_type.7.text), channel_id=1, source_target_pairs={{0,8},{1,9},{2,10},{3,11},{4,12},{5,13},{6,14},{7,15},{8,16},{9,17... | collective-permute-start | bytes 589832 | tf_op jit(solution)/shard_map/ppermute | solution.py:25
  4.8 14.9 %collective-permute-start.4 = (bf16[128,768]{1,0:T(8,128)(2,1)S(1)}, bf16[128,768]{1,0:T(8,128)(2,1)S(1)}, u32[]{:S(2)}, u32[]{:S(2)}) collective-permute-start(bf16[128,768]{1,0:T(8,128)(2,1)S(1)} %convert_element_type.6.image), channel_id=1, source_target_pairs={{0,24},{1,25},{2,26},{3,27},{4,28},{5,29},{6,30},{7,31},{8,0},{9,1... | collective-permute-start | bytes 589832 | tf_op jit(solution)/shard_map/ppermute | solution.py:25
  7.0 14.9 %collective-permute-start.7 = (bf16[256,768]{1,0:T(8,128)(2,1)S(1)}, bf16[256,768]{1,0:T(8,128)(2,1)S(1)}, u32[]{:S(2)}, u32[]{:S(2)}) collective-permute-start(bf16[256,768]{1,0:T(8,128)(2,1)S(1)} %get-tuple-element.19.refs_0_.refs_1_), channel_id=1, source_target_pairs={{0,2},{1,3},{2,0},{3,1},{4,6},{5,7},{6,4},{7,5},{8,10},{9,11},{10,... | collective-permute-start | bytes 1179656 | tf_op jit(solution)/shard_map/ppermute | solution.py:25
  8.7 23.0 %collective-permute-start.6 = (bf16[256,768]{1,0:T(8,128)(2,1)S(1)}, bf16[256,768]{1,0:T(8,128)(2,1)S(1)}, u32[]{:S(2)}, u32[]{:S(2)}) collective-permute-start(bf16[256,768]{1,0:T(8,128)(2,1)S(1)} %get-tuple-element.19.refs_0_.refs_1_), channel_id=1, source_target_pairs={{0,1},{1,0},{2,3},{3,2},{4,5},{5,4},{6,7},{7,6},{8,9},{9,8},{10,11... | collective-permute-start | bytes 1179656 | tf_op jit(solution)/shard_map/ppermute | solution.py:25
  8.7 11.1 %collective-permute-start = (bf16[128,768]{1,0:T(8,128)(2,1)S(1)}, bf16[128,768]{1,0:T(8,128)(2,1)S(1)}, u32[]{:S(2)}, u32[]{:S(2)}) collective-permute-start(bf16[128,768]{1,0:T(8,128)(2,1)S(1)} %get-tuple-element.17), channel_id=1, source_target_pairs={{0,4},{1,5},{2,6},{3,7},{4,0},{5,1},{6,2},{7,3},{8,12},{9,13},{10,... | collective-permute-start | bytes 589832 | tf_op jit(solution)/shard_map/ppermute | solution.py:25
  12.6 12.8 %collective-permute-start.1 = (bf16[128,768]{1,0:T(8,128)(2,1)S(1)}, bf16[128,768]{1,0:T(8,128)(2,1)S(1)}, u32[]{:S(2)}, u32[]{:S(2)}) collective-permute-start(bf16[128,768]{1,0:T(8,128)(2,1)S(1)} %get-tuple-element.18), channel_id=1, source_target_pairs={{0,20},{1,21},{2,22},{3,23},{4,16},{5,17},{6,18},{7,19},{8,28},{9,... | collective-permute-start | bytes 589832 | tf_op jit(solution)/shard_map/ppermute | solution.py:25
  19.8 10.5 %collective-permute-start.9 = (bf16[256,768]{1,0:T(8,128)(2,1)S(1)}, bf16[256,768]{1,0:T(8,128)(2,1)S(1)}, u32[]{:S(2)}, u32[]{:S(2)}) collective-permute-start(bf16[256,768]{1,0:T(8,128)(2,1)S(1)} %constant_dynamic-update-slice_fusion.2.refs_4_), channel_id=1, source_target_pairs={{0,4},{1,5},{2,6},{3,7},{4,0},{5,1},{6,2},{7,3},{8,12},{9,13},{10,... | collective-permute-start | bytes 1179656 | tf_op jit(solution)/shard_map/ppermute | solution.py:25
  19.9 11.9 %collective-permute-start.5 = (bf16[256,768]{1,0:T(8,128)(2,1)S(1)}, bf16[256,768]{1,0:T(8,128)(2,1)S(1)}, u32[]{:S(2)}, u32[]{:S(2)}) collective-permute-start(bf16[256,768]{1,0:T(8,128)(2,1)S(1)} %constant_dynamic-update-slice_fusion.2.refs_4_), channel_id=1, source_target_pairs={{0,2},{1,3},{2,0},{3,1},{4,6},{5,7},{6,4},{7,5},{8,10},{9,11},{10,... | collective-permute-start | bytes 1179656 | tf_op jit(solution)/shard_map/ppermute | solution.py:25
  21.9 9.9 %collective-permute-start.8 = (bf16[256,768]{1,0:T(8,128)(2,1)S(1)}, bf16[256,768]{1,0:T(8,128)(2,1)S(1)}, u32[]{:S(2)}, u32[]{:S(2)}) collective-permute-start(bf16[256,768]{1,0:T(8,128)(2,1)S(1)} %collective-permute-done.7.refs_2_.refs_3_), channel_id=1, source_target_pairs={{0,1},{1,0},{2,3},{3,2},{4,5},{5,4},{6,7},{7,6},{8,9},{9,8},{10,11... | collective-permute-start | bytes 1179656 | tf_op jit(solution)/shard_map/ppermute | solution.py:25
  25.4 12.1 %collective-permute-start.2 = (bf16[256,768]{1,0:T(8,128)(2,1)S(1)}, bf16[256,768]{1,0:T(8,128)(2,1)S(1)}, u32[]{:S(2)}, u32[]{:S(2)}) collective-permute-start(bf16[256,768]{1,0:T(8,128)(2,1)S(1)} %constant_dynamic-update-slice_fusion.refs_6_), channel_id=1, source_target_pairs={{0,2},{1,3},{2,0},{3,1},{4,6},{5,7},{6,4},{7,5},{8,10},{9,11},{10,... | collective-permute-start | bytes 1179656 | tf_op jit(solution)/shard_map/ppermute | solution.py:25
  30.2 14.7 %collective-permute-start.10 = (bf16[256,768]{1,0:T(8,128)(2,1)S(1)}, bf16[256,768]{1,0:T(8,128)(2,1)}, u32[]{:S(2)}, u32[]{:S(2)}) collective-permute-start(bf16[256,768]{1,0:T(8,128)(2,1)S(1)} %collective-permute-done.9.refs_5_), channel_id=1, source_target_pairs={{0,2},{1,3},{2,0},{3,1},{4,6},{5,7},{6,4},{7,5},{8,10},{9,11},{10,... | collective-permute-start | bytes 1179656 | tf_op jit(solution)/shard_map/ppermute | solution.py:25
  37.5 12.4 %all-to-all-start = ((f32[32,8,128]{2,1,0:T(8,128)}), f32[32,8,128]{2,1,0:T(8,128)S(1)}, u32[]{:S(2)}, u32[]{:S(2)}) async-start(f32[32,8,128]{2,1,0:T(8,128)} %shard_map.58), calls=%async_computation | async-start | bytes 262144 | tf_op jit(solution)/shard_map/all_to_all | solution.py:198
  54.7 2.4 %collective-permute-start.11 = (f32[2,128,768]{2,1,0:T(8,128)S(1)}, f32[2,128,768]{2,1,0:T(8,128)S(1)}, u32[]{:S(2)}, u32[]{:S(2)}) collective-permute-start(f32[2,128,768]{2,1,0:T(8,128)S(1)} %get-tuple-element.27), channel_id=1, source_target_pairs={{0,1},{1,0},{2,3},{3,2},{4,5},{5,4},{6,7},{7,6},{8,9},{9,8},{10,11... | collective-permute-start | bytes 2359304 | tf_op jit(solution)/shard_map/ppermute | solution.py:25

commit v5 on v4

--- a/solution.py
+++ b/solution.py
@@ -185,7 +185,8 @@
     core = over_core(own)
     x = over_x(own)
     corex = over_core(x)
-    far_ab, far_b, far_pc = [over_x(v) for v in (ab, b2, pc)]
+    far_ab, far_pc = over_x(ab), over_x(pc)
+    far_b = in_pair(far_ab)
     far_ab, core, _ = lax.optimization_barrier((far_ab, core, over_core(pc)))
     send = call(
         functools.partial(stats_kernel, count),

time: 58.2 us -> 56.1 us (0.964)
  waiting for transfers between devices: 22.9 us -> 19.4 us
  starting transfers between devices: 25.2 us -> 26.6 us
    ppermute x12, waiting for transfers between devices: 17.9 us -> 11.2 us  [moved(): return lax.ppermute(value, AXES, pairs)]
    all_to_all x1, waiting for transfers between devices: 4.99 us -> 8.22 us  [body(): got = lax.all_to_all(send, AXES, 0, 0, tiled=True)]
    ppermute x12, starting transfers between devices: 21 us -> 23.3 us  [moved(): return lax.ppermute(value, AXES, pairs)]
    all_to_all x1, starting transfers between devices: 4.14 us -> 3.24 us  [body(): got = lax.all_to_all(send, AXES, 0, 0, tiled=True)]
  transfers between devices with their start and end apart: 13 -> 13, of which waited for: 7 -> 6; matrix products, arithmetic and copies ran while one was open for 0% -> 0% of each run, Pallas kernels for 4% -> 4%
where the time goes in v5:
time: 56.1 us; the launch traced here: 55.8 us
  starting transfers between devices  26.6 us (47%)
  waiting for transfers between devices  19.4 us (35%)
  Pallas kernels  7.98 us (14%)
  other arithmetic  1.09 us (2%)
  between operations  0.75 us (1%)
    ppermute x12, starting transfers between devices, moved(): return lax.ppermute(value, AXES, pairs)  23.3 us
    ppermute x12, waiting for transfers between devices, moved(): return lax.ppermute(value, AXES, pairs)  11.2 us
    all_to_all x1, waiting for transfers between devices, body(): got = lax.all_to_all(send, AXES, 0, 0, tiled=True)  8.22 us
    pallas_call x4, Pallas kernels, call(): pl.pallas_call(kernel, out_shape=out_shape, in_specs=[pl.BlockSpec(memory...  7.98 us
    all_to_all x1, starting transfers between devices, body(): got = lax.all_to_all(send, AXES, 0, 0, tiled=True)  3.24 us
  transfers between devices with their start and end apart: 13, of which 6 were waited for; matrix products, arithmetic and copies ran while one was open for 0% of the time, Pallas kernels for 4%

profile of v5, /device:TPU:0, one launch (start us, length us, event | category | flops | bytes accessed | tf_op | source)
XLA Modules:
  0.0 55.8 jit_solution(15027197675664847625)
XLA Ops:
  0.6 1.1 %convert_element_type.7.text = bf16[128,768]{1,0:T(8,128)(2,1)S(1)} convert(f32[128,768]{1,0:T(8,128)} %param.3) | non-fusion elementwise | flops 98304 | bytes 589824 | tf_op jit(solution)/shard_map/convert_element_type | solution.py:177
  1.7 3.1 %collective-permute-start.3 = (bf16[128,768]{1,0:T(8,128)(2,1)S(1)}, bf16[128,768]{1,0:T(8,128)(2,1)S(1)}, u32[]{:S(2)}, u32[]{:S(2)}) collective-permute-start(bf16[128,768]{1,0:T(8,128)(2,1)S(1)} %convert_element_type.7.text), channel_id=1, source_target_pairs={{0,8},{1,9},{2,10},{3,11},{4,12},{5,13},{6,14},{7,15},{8,16},{9,17... | collective-permute-start | bytes 589832 | tf_op jit(solution)/shard_map/ppermute | solution.py:25
  4.8 2.1 %collective-permute-start.4 = (bf16[128,768]{1,0:T(8,128)(2,1)S(1)}, bf16[128,768]{1,0:T(8,128)(2,1)S(1)}, u32[]{:S(2)}, u32[]{:S(2)}) collective-permute-start(bf16[128,768]{1,0:T(8,128)(2,1)S(1)} %convert_element_type.6.image), channel_id=1, source_target_pairs={{0,24},{1,25},{2,26},{3,27},{4,28},{5,29},{6,30},{7,31},{8,0},{9,1... | collective-permute-start | bytes 589832 | tf_op jit(solution)/shard_map/ppermute | solution.py:25
  6.9 0.1 shard_map.57
  7.0 1.8 %collective-permute-start.7 = (bf16[256,768]{1,0:T(8,128)(2,1)S(1)}, bf16[256,768]{1,0:T(8,128)(2,1)S(1)}, u32[]{:S(2)}, u32[]{:S(2)}) collective-permute-start(bf16[256,768]{1,0:T(8,128)(2,1)S(1)} %get-tuple-element.19.refs_0_.refs_1_), channel_id=1, source_target_pairs={{0,2},{1,3},{2,0},{3,1},{4,6},{5,7},{6,4},{7,5},{8,10},{9,11},{10,... | collective-permute-start | bytes 1179656 | tf_op jit(solution)/shard_map/ppermute | solution.py:25
  8.7 0.0 collective-permute-start.6
  8.7 1.5 %collective-permute-start = (bf16[128,768]{1,0:T(8,128)(2,1)S(1)}, bf16[128,768]{1,0:T(8,128)(2,1)S(1)}, u32[]{:S(2)}, u32[]{:S(2)}) collective-permute-start(bf16[128,768]{1,0:T(8,128)(2,1)S(1)} %get-tuple-element.17), channel_id=1, source_target_pairs={{0,4},{1,5},{2,6},{3,7},{4,0},{5,1},{6,2},{7,3},{8,12},{9,13},{10,... | collective-permute-start | bytes 589832 | tf_op jit(solution)/shard_map/ppermute | solution.py:25
  10.3 2.3 %collective-permute-done.3 = bf16[128,768]{1,0:T(8,128)(2,1)S(1)} collective-permute-done((bf16[128,768]{1,0:T(8,128)(2,1)S(1)}, bf16[128,768]{1,0:T(8,128)(2,1)S(1)}, u32[]{:S(2)}, u32[]{:S(2)}) %collective-permute-start.3) | collective-permute-done | bytes 196640 | tf_op jit(solution)/shard_map/ppermute | solution.py:25
  12.6 7.1 %collective-permute-start.1 = (bf16[128,768]{1,0:T(8,128)(2,1)S(1)}, bf16[128,768]{1,0:T(8,128)(2,1)S(1)}, u32[]{:S(2)}, u32[]{:S(2)}) collective-permute-start(bf16[128,768]{1,0:T(8,128)(2,1)S(1)} %get-tuple-element.18), channel_id=1, source_target_pairs={{0,20},{1,21},{2,22},{3,23},{4,16},{5,17},{6,18},{7,19},{8,28},{9,... | collective-permute-start | bytes 589832 | tf_op jit(solution)/shard_map/ppermute | solution.py:25
  19.8 0.1 collective-permute-start.9
  19.9 2.0 %collective-permute-start.5 = (bf16[256,768]{1,0:T(8,128)(2,1)S(1)}, bf16[256,768]{1,0:T(8,128)(2,1)S(1)}, u32[]{:S(2)}, u32[]{:S(2)}) collective-permute-start(bf16[256,768]{1,0:T(8,128)(2,1)S(1)} %constant_dynamic-update-slice_fusion.2.refs_4_), channel_id=1, source_target_pairs={{0,2},{1,3},{2,0},{3,1},{4,6},{5,7},{6,4},{7,5},{8,10},{9,11},{10,... | collective-permute-start | bytes 1179656 | tf_op jit(solution)/shard_map/ppermute | solution.py:25
  21.9 0.1 collective-permute-start.8
  21.9 3.5 %collective-permute-done.1 = bf16[128,768]{1,0:T(8,128)(2,1)S(1)} collective-permute-done((bf16[128,768]{1,0:T(8,128)(2,1)S(1)}, bf16[128,768]{1,0:T(8,128)(2,1)S(1)}, u32[]{:S(2)}, u32[]{:S(2)}) %collective-permute-start.1) | collective-permute-done | bytes 196640 | tf_op jit(solution)/shard_map/ppermute | solution.py:25
  25.4 1.6 %collective-permute-start.2 = (bf16[256,768]{1,0:T(8,128)(2,1)S(1)}, bf16[256,768]{1,0:T(8,128)(2,1)S(1)}, u32[]{:S(2)}, u32[]{:S(2)}) collective-permute-start(bf16[256,768]{1,0:T(8,128)(2,1)S(1)} %constant_dynamic-update-slice_fusion.refs_6_), channel_id=1, source_target_pairs={{0,2},{1,3},{2,0},{3,1},{4,6},{5,7},{6,4},{7,5},{8,10},{9,11},{10,... | collective-permute-start | bytes 1179656 | tf_op jit(solution)/shard_map/ppermute | solution.py:25
  27.0 0.7 %collective-permute-done.5.refs_7_ = bf16[256,768]{1,0:T(8,128)(2,1)S(1)} collective-permute-done((bf16[256,768]{1,0:T(8,128)(2,1)S(1)}, bf16[256,768]{1,0:T(8,128)(2,1)S(1)}, u32[]{:S(2)}, u32[]{:S(2)}) %collective-permute-start.5) | collective-permute-done | bytes 393248 | tf_op jit(solution)/shard_map/ppermute | solution.py:25
  27.7 3.8 %collective-permute-start.10 = (bf16[256,768]{1,0:T(8,128)(2,1)S(1)}, bf16[256,768]{1,0:T(8,128)(2,1)}, u32[]{:S(2)}, u32[]{:S(2)}) collective-permute-start(bf16[256,768]{1,0:T(8,128)(2,1)S(1)} %collective-permute-done.5.refs_7_), channel_id=1, source_target_pairs={{0,4},{1,5},{2,6},{3,7},{4,0},{5,1},{6,2},{7,3},{8,12},{9,13},{10,... | collective-permute-start | bytes 1179656 | tf_op jit(solution)/shard_map/ppermute | solution.py:25
  31.5 2.2 %shard_map.58 = f32[32,8,128]{2,1,0:T(8,128)} custom-call(bf16[256,768]{1,0:T(8,128)(2,1)S(1)} %get-tuple-element.19.refs_0_.refs_1_, bf16[256,768]{1,0:T(8,128)(2,1)S(1)} %collective-permute-done.6.refs_1_.refs_2_, bf16[256,768]{1,0:T(8,128)(2,1)S(1)} %collective-permute-done.7.refs_2_.refs_3_, bf16[256,768]{1,0:T(8,128)(2,1)S(1)} %collective-permute-done.8.refs_3_, ...), custom_call_target="tpu_custom_call" | custom-call | flops 805306368 | bytes 2752512 | tf_op jit(solution)/shard_map/pallas_call | solution.py:59
  33.7 2.5 %collective-permute-done.2.refs_9_ = bf16[256,768]{1,0:T(8,128)(2,1)S(1)} collective-permute-done((bf16[256,768]{1,0:T(8,128)(2,1)S(1)}, bf16[256,768]{1,0:T(8,128)(2,1)S(1)}, u32[]{:S(2)}, u32[]{:S(2)}) %collective-permute-start.2) | collective-permute-done | bytes 393248 | tf_op jit(solution)/shard_map/ppermute | solution.py:25
  36.3 3.2 %all-to-all-start = ((f32[32,8,128]{2,1,0:T(8,128)}), f32[32,8,128]{2,1,0:T(8,128)S(1)}, u32[]{:S(2)}, u32[]{:S(2)}) async-start(f32[32,8,128]{2,1,0:T(8,128)} %shard_map.58), calls=%async_computation | async-start | bytes 262144 | tf_op jit(solution)/shard_map/all_to_all | solution.py:199
  39.5 8.2 %all-to-all-done.refs_0_ = f32[32,8,128]{2,1,0:T(8,128)S(1)} async-done(((f32[32,8,128]{2,1,0:T(8,128)}), f32[32,8,128]{2,1,0:T(8,128)S(1)}, u32[]{:S(2)}, u32[]{:S(2)}) %all-to-all-start) | async-done | bytes 131104 | tf_op jit(solution)/shard_map/all_to_all | solution.py:199
  47.7 4.8 %shard_map.59 = (f32[128]{0:T(128)}, f32[128]{0:T(128)}, f32[2,128,768]{2,1,0:T(8,128)S(1)}, f32[2,128,768]{2,1,0:T(8,128)S(1)}) custom-call(f32[32,8,128]{2,1,0:T(8,128)S(1)} %all-to-all-done.refs_0_, bf16[256,768]{1,0:T(8,128)(2,1)S(1)} %get-tuple-element.19.refs_0_.refs_1_, bf16[256,768]{1,0:T(8,128)(2,1)S(1)} %collective-permute-done.6.refs_1_.refs_2_, ...), custom_call_target="tpu_custom_call" | custom-call | flops 1610612736 | bytes 3670016 | tf_op jit(solution)/shard_map/pallas_call | solution.py:59
  52.5 0.3 collective-permute-start.11
  52.8 2.1 %collective-permute-done.11.got = f32[2,128,768]{2,1,0:T(8,128)S(1)} collective-permute-done((f32[2,128,768]{2,1,0:T(8,128)S(1)}, f32[2,128,768]{2,1,0:T(8,128)S(1)}, u32[]{:S(2)}, u32[]{:S(2)}) %collective-permute-start.11) | collective-permute-done | bytes 786464 | tf_op jit(solution)/shard_map/ppermute | solution.py:25
  54.9 1.0 %shard_map.60 = (f32[128,768]{1,0:T(8,128)}, f32[128,768]{1,0:T(8,128)}) custom-call(f32[2,128,768]{2,1,0:T(8,128)S(1)} %get-tuple-element.26.kept, f32[2,128,768]{2,1,0:T(8,128)S(1)} %collective-permute-done.11.got), custom_call_target="tpu_custom_call" | custom-call | bytes 1572864 | tf_op jit(solution)/shard_map/pallas_call | solution.py:59
  (14 shorter events, 0.1 us)
Async XLA Ops:
  0.6 4.2 %copy-start = (f32[128,768]{1,0:T(8,128)S(1)}, f32[128,768]{1,0:T(8,128)}, u32[]{:S(2)}) copy-start(f32[128,768]{1,0:T(8,128)} %param.2) | copy-start | bytes 1179652
  1.7 10.9 %collective-permute-start.3 = (bf16[128,768]{1,0:T(8,128)(2,1)S(1)}, bf16[128,768]{1,0:T(8,128)(2,1)S(1)}, u32[]{:S(2)}, u32[]{:S(2)}) collective-permute-start(bf16[128,768]{1,0:T(8,128)(2,1)S(1)} %convert_element_type.7.text), channel_id=1, source_target_pairs={{0,8},{1,9},{2,10},{3,11},{4,12},{5,13},{6,14},{7,15},{8,16},{9,17... | collective-permute-start | bytes 589832 | tf_op jit(solution)/shard_map/ppermute | solution.py:25
  4.8 14.9 %collective-permute-start.4 = (bf16[128,768]{1,0:T(8,128)(2,1)S(1)}, bf16[128,768]{1,0:T(8,128)(2,1)S(1)}, u32[]{:S(2)}, u32[]{:S(2)}) collective-permute-start(bf16[128,768]{1,0:T(8,128)(2,1)S(1)} %convert_element_type.6.image), channel_id=1, source_target_pairs={{0,24},{1,25},{2,26},{3,27},{4,28},{5,29},{6,30},{7,31},{8,0},{9,1... | collective-permute-start | bytes 589832 | tf_op jit(solution)/shard_map/ppermute | solution.py:25
  7.0 14.9 %collective-permute-start.7 = (bf16[256,768]{1,0:T(8,128)(2,1)S(1)}, bf16[256,768]{1,0:T(8,128)(2,1)S(1)}, u32[]{:S(2)}, u32[]{:S(2)}) collective-permute-start(bf16[256,768]{1,0:T(8,128)(2,1)S(1)} %get-tuple-element.19.refs_0_.refs_1_), channel_id=1, source_target_pairs={{0,2},{1,3},{2,0},{3,1},{4,6},{5,7},{6,4},{7,5},{8,10},{9,11},{10,... | collective-permute-start | bytes 1179656 | tf_op jit(solution)/shard_map/ppermute | solution.py:25
  8.7 22.8 %collective-permute-start.6 = (bf16[256,768]{1,0:T(8,128)(2,1)S(1)}, bf16[256,768]{1,0:T(8,128)(2,1)S(1)}, u32[]{:S(2)}, u32[]{:S(2)}) collective-permute-start(bf16[256,768]{1,0:T(8,128)(2,1)S(1)} %get-tuple-element.19.refs_0_.refs_1_), channel_id=1, source_target_pairs={{0,1},{1,0},{2,3},{3,2},{4,5},{5,4},{6,7},{7,6},{8,9},{9,8},{10,11... | collective-permute-start | bytes 1179656 | tf_op jit(solution)/shard_map/ppermute | solution.py:25
  8.7 11.1 %collective-permute-start = (bf16[128,768]{1,0:T(8,128)(2,1)S(1)}, bf16[128,768]{1,0:T(8,128)(2,1)S(1)}, u32[]{:S(2)}, u32[]{:S(2)}) collective-permute-start(bf16[128,768]{1,0:T(8,128)(2,1)S(1)} %get-tuple-element.17), channel_id=1, source_target_pairs={{0,4},{1,5},{2,6},{3,7},{4,0},{5,1},{6,2},{7,3},{8,12},{9,13},{10,... | collective-permute-start | bytes 589832 | tf_op jit(solution)/shard_map/ppermute | solution.py:25
  12.6 12.8 %collective-permute-start.1 = (bf16[128,768]{1,0:T(8,128)(2,1)S(1)}, bf16[128,768]{1,0:T(8,128)(2,1)S(1)}, u32[]{:S(2)}, u32[]{:S(2)}) collective-permute-start(bf16[128,768]{1,0:T(8,128)(2,1)S(1)} %get-tuple-element.18), channel_id=1, source_target_pairs={{0,20},{1,21},{2,22},{3,23},{4,16},{5,17},{6,18},{7,19},{8,28},{9,... | collective-permute-start | bytes 589832 | tf_op jit(solution)/shard_map/ppermute | solution.py:25
  19.8 11.7 %collective-permute-start.9 = (bf16[256,768]{1,0:T(8,128)(2,1)S(1)}, bf16[256,768]{1,0:T(8,128)(2,1)S(1)}, u32[]{:S(2)}, u32[]{:S(2)}) collective-permute-start(bf16[256,768]{1,0:T(8,128)(2,1)S(1)} %constant_dynamic-update-slice_fusion.2.refs_4_), channel_id=1, source_target_pairs={{0,4},{1,5},{2,6},{3,7},{4,0},{5,1},{6,2},{7,3},{8,12},{9,13},{10,... | collective-permute-start | bytes 1179656 | tf_op jit(solution)/shard_map/ppermute | solution.py:25
  19.9 7.8 %collective-permute-start.5 = (bf16[256,768]{1,0:T(8,128)(2,1)S(1)}, bf16[256,768]{1,0:T(8,128)(2,1)S(1)}, u32[]{:S(2)}, u32[]{:S(2)}) collective-permute-start(bf16[256,768]{1,0:T(8,128)(2,1)S(1)} %constant_dynamic-update-slice_fusion.2.refs_4_), channel_id=1, source_target_pairs={{0,2},{1,3},{2,0},{3,1},{4,6},{5,7},{6,4},{7,5},{8,10},{9,11},{10,... | collective-permute-start | bytes 1179656 | tf_op jit(solution)/shard_map/ppermute | solution.py:25
  21.9 9.7 %collective-permute-start.8 = (bf16[256,768]{1,0:T(8,128)(2,1)S(1)}, bf16[256,768]{1,0:T(8,128)(2,1)S(1)}, u32[]{:S(2)}, u32[]{:S(2)}) collective-permute-start(bf16[256,768]{1,0:T(8,128)(2,1)S(1)} %collective-permute-done.7.refs_2_.refs_3_), channel_id=1, source_target_pairs={{0,1},{1,0},{2,3},{3,2},{4,5},{5,4},{6,7},{7,6},{8,9},{9,8},{10,11... | collective-permute-start | bytes 1179656 | tf_op jit(solution)/shard_map/ppermute | solution.py:25
  25.4 10.8 %collective-permute-start.2 = (bf16[256,768]{1,0:T(8,128)(2,1)S(1)}, bf16[256,768]{1,0:T(8,128)(2,1)S(1)}, u32[]{:S(2)}, u32[]{:S(2)}) collective-permute-start(bf16[256,768]{1,0:T(8,128)(2,1)S(1)} %constant_dynamic-update-slice_fusion.refs_6_), channel_id=1, source_target_pairs={{0,2},{1,3},{2,0},{3,1},{4,6},{5,7},{6,4},{7,5},{8,10},{9,11},{10,... | collective-permute-start | bytes 1179656 | tf_op jit(solution)/shard_map/ppermute | solution.py:25
  27.7 11.8 %collective-permute-start.10 = (bf16[256,768]{1,0:T(8,128)(2,1)S(1)}, bf16[256,768]{1,0:T(8,128)(2,1)}, u32[]{:S(2)}, u32[]{:S(2)}) collective-permute-start(bf16[256,768]{1,0:T(8,128)(2,1)S(1)} %collective-permute-done.5.refs_7_), channel_id=1, source_target_pairs={{0,4},{1,5},{2,6},{3,7},{4,0},{5,1},{6,2},{7,3},{8,12},{9,13},{10,... | collective-permute-start | bytes 1179656 | tf_op jit(solution)/shard_map/ppermute | solution.py:25
  36.3 11.5 %all-to-all-start = ((f32[32,8,128]{2,1,0:T(8,128)}), f32[32,8,128]{2,1,0:T(8,128)S(1)}, u32[]{:S(2)}, u32[]{:S(2)}) async-start(f32[32,8,128]{2,1,0:T(8,128)} %shard_map.58), calls=%async_computation | async-start | bytes 262144 | tf_op jit(solution)/shard_map/all_to_all | solution.py:199
  52.5 2.4 %collective-permute-start.11 = (f32[2,128,768]{2,1,0:T(8,128)S(1)}, f32[2,128,768]{2,1,0:T(8,128)S(1)}, u32[]{:S(2)}, u32[]{:S(2)}) collective-permute-start(f32[2,128,768]{2,1,0:T(8,128)S(1)} %get-tuple-element.27), channel_id=1, source_target_pairs={{0,1},{1,0},{2,3},{3,2},{4,5},{5,4},{6,7},{7,6},{8,9},{9,8},{10,11... | collective-permute-start | bytes 2359304 | tf_op jit(solution)/shard_map/ppermute | solution.py:25

commit v6 on v5

--- a/solution.py
+++ b/solution.py
@@ -59,7 +59,7 @@
     return pl.pallas_call(
         kernel,
         out_shape=out_shape,
-        in_specs=[pl.BlockSpec(memory_space=pltpu.HBM) if i in remote else whole for i in range(len(args))],
+        in_specs=[pl.BlockSpec(memory_space=pl.ANY) if i in remote else whole for i in range(len(args))],
         out_specs=jax.tree.map(lambda _: whole, out_shape),
         scratch_shapes=scratch,
         compiler_params=pltpu.CompilerParams(vmem_limit_bytes=VMEM_LIMIT),
@@ -89,7 +89,8 @@
     at = slice(place * n, (place + 1) * n)
     for side in range(2):
         for slot, ref in enumerate((own, ab, b)):
-            cols[side, slot, at] = ref[side * n : (side + 1) * n]
+            if ref is not None:
+                cols[side, slot, at] = ref[side * n : (side + 1) * n]
     cols[1 - odd, 3, at] = pc[:n]
     cols[odd, 3, at] = pc[n:]
 
@@ -121,47 +122,54 @@
 
 def grad_kernel(count, *refs):
     got, own, core, x, ab, b2, pc, abx, bx2, pcx = refs[:10]
-    image_lse, text_lse, kept, sent, got_in, rows, cols, sem = refs[10:]
-    load = pltpu.make_async_copy(got, got_in, sem)
-    load.start()
+    image_lse, text_lse, kept, sent, rows, cols, weights, sems = refs[10:]
     n = own.shape[0] // 2
     b = lax.axis_index("batch")
     odd = lax.rem(b, 2)
+    loads = [
+        pltpu.make_async_copy(bx2.at[pl.ds(side * n, n)], cols.at[side, 2, pl.ds(n, n)], sems.at[side])
+        for side in range(2)
+    ]
+    for load in loads:
+        load.start()
 
     def lse_of(block):
         at = lax.rem(block + count, count) * SPANS
-        v = [got_in[at + s] for s in range(SPANS)]
+        v = [got[at + s] for s in range(SPANS)]
         top = jnp.maximum(jnp.maximum(v[0], v[1]), jnp.maximum(v[2], v[3]))
         return top + jnp.log(sum(jnp.exp(a - top) for a in v))
 
     fill_columns(cols, 0, odd, own, ab, b2, pc)
-    fill_columns(cols, 1, odd, x, abx, bx2, pcx)
-    load.wait()
+    fill_columns(cols, 1, odd, x, abx, None, pcx)
     mine = lse_of(b)
     image_lse[...] = mine[0]
-    text_lse[...] = mine[4]
+    text_lse[...] = mine[SPANS]
     turned = mine.T
     for side in range(2):
         half = slice(n, 2 * n) if side == 0 else slice(0, n)
         rows[side, :n] = own[half]
         rows[side, n:] = core[half]
-        row_lse = jnp.concatenate([turned[:, 4 * side : 4 * side + 1], turned[:, 4 * side + 1 : 4 * side + 2]])
-        total = jnp.zeros((2 * n, rows.shape[-1]), F32)
+        at = SPANS * side
+        row_lse = jnp.concatenate([turned[:, at : at + 1], turned[:, at + 1 : at + 2]])
         steps = (0, -2, -1 - 2 * odd, -3 + 2 * odd) if side == 0 else (0, 2, 3 - 2 * odd, 1 + 2 * odd)
-        for k, step in enumerate(steps):
-            l = mine if k == 0 else lse_of(b + step)
-            at = 4 if side == 0 else 0
+        at = SPANS * (1 - side)
+        for k in (0, 1, 3, 2):
+            if k == 2:
+                loads[side].wait()
+            l = mine if k == 0 else lse_of(b + steps[k])
             col_lse = jnp.concatenate([l[at : at + 1], l[at + 2 : at + 3]], axis=1)
-            c = cols[side, k]
-            s = dot_t(rows[side], c) * LOGIT_SCALE
-            w = 0.5 * jnp.exp(s - row_lse) + 0.5 * jnp.exp(s - col_lse)
+            s = dot_t(rows[side], cols[side, k]) * LOGIT_SCALE
+            w = 0.5 * (jnp.exp(s - row_lse) + jnp.exp(s - col_lse))
             if k == 0:
                 i = lax.broadcasted_iota(jnp.int32, s.shape, 0)
                 j = lax.broadcasted_iota(jnp.int32, s.shape, 1)
                 w = w - ((i == j) & (i < n)).astype(F32)
-            total = total + jnp.dot(w.astype(BF16), c, preferred_element_type=F32)
-        kept[side] = LOGIT_SCALE * total[:n]
-        sent[side] = LOGIT_SCALE * total[n:]
+            weights[side, :, k * 2 * n : (k + 1) * 2 * n] = w.astype(BF16)
+        total = LOGIT_SCALE * jnp.dot(
+            weights[side], cols[side].reshape(STEPS * 2 * n, cols.shape[-1]), preferred_element_type=F32
+        )
+        kept[side] = total[:n]
+        sent[side] = total[n:]
 
 
 def add_kernel(kept, got, image_grad, text_grad):
@@ -203,13 +211,13 @@
         functools.partial(grad_kernel, count),
         (row, row, both, both),
         [
-            pltpu.VMEM(got.shape, F32),
             pltpu.VMEM((2, 2 * n, width), BF16),
             pltpu.VMEM((2, STEPS, 2 * n, width), BF16),
-            pltpu.SemaphoreType.DMA,
+            pltpu.VMEM((2, 2 * n, STEPS * 2 * n), BF16),
+            pltpu.SemaphoreType.DMA((2,)),
         ],
         8 * 2 * n * STEPS * 2 * n * width,
-        got, own, core, x, ab, b2, pc, far_ab, far_b, far_pc, remote=(0,),
+        got, own, core, x, ab, b2, pc, far_ab, far_b, far_pc, remote=(8,),
     )
     grad = jax.ShapeDtypeStruct((n, width), F32)
     image_grad, text_grad = call(add_kernel, (grad, grad), [], 0, kept, over_core(sent))

time: 56.1 us -> 54.2 us (0.966)
  Pallas kernels: 7.98 us -> 6.19 us
    pallas_call x4, Pallas kernels: 7.98 us -> 6.19 us  [call(): pl.pallas_call(kernel, out_shape=out_shape, in_specs=[pl.BlockSpec(memory...]
where the time goes in v6:
time: 54.2 us; the launch traced here: 54 us
  starting transfers between devices  26.6 us (49%)
  waiting for transfers between devices  19.4 us (36%)
  Pallas kernels  6.19 us (11%)
  other arithmetic  1.09 us (2%)
  between operations  0.75 us (1%)
    ppermute x12, starting transfers between devices, moved(): return lax.ppermute(value, AXES, pairs)  23.3 us
    ppermute x12, waiting for transfers between devices, moved(): return lax.ppermute(value, AXES, pairs)  11.2 us
    all_to_all x1, waiting for transfers between devices, body(): got = lax.all_to_all(send, AXES, 0, 0, tiled=True)  8.22 us
    pallas_call x4, Pallas kernels, call(): pl.pallas_call(kernel, out_shape=out_shape, in_specs=[pl.BlockSpec(memory...  6.19 us
    all_to_all x1, starting transfers between devices, body(): got = lax.all_to_all(send, AXES, 0, 0, tiled=True)  3.24 us
    convert_element_type x2, other arithmetic, body(): i0, t0 = (image_embeds.astype(BF16), text_embeds.astype(BF16))  1.09 us
  transfers between devices with their start and end apart: 13, of which 6 were waited for; matrix products, arithmetic and copies ran while one was open for 0% of the time, Pallas kernels for 4%

profile of v6, /device:TPU:0, one launch (start us, length us, event | category | flops | bytes accessed | tf_op | source)
XLA Modules:
  0.0 54.0 jit_solution(6172422604084755700)
XLA Ops:
  0.6 1.1 %convert_element_type.7.text = bf16[128,768]{1,0:T(8,128)(2,1)S(1)} convert(f32[128,768]{1,0:T(8,128)} %param.3) | non-fusion elementwise | flops 98304 | bytes 589824 | tf_op jit(solution)/shard_map/convert_element_type | solution.py:185
  1.7 3.1 %collective-permute-start.3 = (bf16[128,768]{1,0:T(8,128)(2,1)S(1)}, bf16[128,768]{1,0:T(8,128)(2,1)S(1)}, u32[]{:S(2)}, u32[]{:S(2)}) collective-permute-start(bf16[128,768]{1,0:T(8,128)(2,1)S(1)} %convert_element_type.7.text), channel_id=1, source_target_pairs={{0,8},{1,9},{2,10},{3,11},{4,12},{5,13},{6,14},{7,15},{8,16},{9,17... | collective-permute-start | bytes 589832 | tf_op jit(solution)/shard_map/ppermute | solution.py:25
  4.8 2.1 %collective-permute-start.4 = (bf16[128,768]{1,0:T(8,128)(2,1)S(1)}, bf16[128,768]{1,0:T(8,128)(2,1)S(1)}, u32[]{:S(2)}, u32[]{:S(2)}) collective-permute-start(bf16[128,768]{1,0:T(8,128)(2,1)S(1)} %convert_element_type.6.image), channel_id=1, source_target_pairs={{0,24},{1,25},{2,26},{3,27},{4,28},{5,29},{6,30},{7,31},{8,0},{9,1... | collective-permute-start | bytes 589832 | tf_op jit(solution)/shard_map/ppermute | solution.py:25
  6.9 0.1 shard_map.57
  7.0 1.8 %collective-permute-start.7 = (bf16[256,768]{1,0:T(8,128)(2,1)S(1)}, bf16[256,768]{1,0:T(8,128)(2,1)S(1)}, u32[]{:S(2)}, u32[]{:S(2)}) collective-permute-start(bf16[256,768]{1,0:T(8,128)(2,1)S(1)} %get-tuple-element.19.refs_0_.refs_1_), channel_id=1, source_target_pairs={{0,2},{1,3},{2,0},{3,1},{4,6},{5,7},{6,4},{7,5},{8,10},{9,11},{10,... | collective-permute-start | bytes 1179656 | tf_op jit(solution)/shard_map/ppermute | solution.py:25
  8.7 0.0 collective-permute-start.6
  8.7 1.5 %collective-permute-start = (bf16[128,768]{1,0:T(8,128)(2,1)S(1)}, bf16[128,768]{1,0:T(8,128)(2,1)S(1)}, u32[]{:S(2)}, u32[]{:S(2)}) collective-permute-start(bf16[128,768]{1,0:T(8,128)(2,1)S(1)} %get-tuple-element.17), channel_id=1, source_target_pairs={{0,4},{1,5},{2,6},{3,7},{4,0},{5,1},{6,2},{7,3},{8,12},{9,13},{10,... | collective-permute-start | bytes 589832 | tf_op jit(solution)/shard_map/ppermute | solution.py:25
  10.3 2.3 %collective-permute-done.3 = bf16[128,768]{1,0:T(8,128)(2,1)S(1)} collective-permute-done((bf16[128,768]{1,0:T(8,128)(2,1)S(1)}, bf16[128,768]{1,0:T(8,128)(2,1)S(1)}, u32[]{:S(2)}, u32[]{:S(2)}) %collective-permute-start.3) | collective-permute-done | bytes 196640 | tf_op jit(solution)/shard_map/ppermute | solution.py:25
  12.6 7.1 %collective-permute-start.1 = (bf16[128,768]{1,0:T(8,128)(2,1)S(1)}, bf16[128,768]{1,0:T(8,128)(2,1)S(1)}, u32[]{:S(2)}, u32[]{:S(2)}) collective-permute-start(bf16[128,768]{1,0:T(8,128)(2,1)S(1)} %get-tuple-element.18), channel_id=1, source_target_pairs={{0,20},{1,21},{2,22},{3,23},{4,16},{5,17},{6,18},{7,19},{8,28},{9,... | collective-permute-start | bytes 589832 | tf_op jit(solution)/shard_map/ppermute | solution.py:25
  19.8 0.1 collective-permute-start.9
  19.9 2.0 %collective-permute-start.5 = (bf16[256,768]{1,0:T(8,128)(2,1)S(1)}, bf16[256,768]{1,0:T(8,128)(2,1)S(1)}, u32[]{:S(2)}, u32[]{:S(2)}) collective-permute-start(bf16[256,768]{1,0:T(8,128)(2,1)S(1)} %constant_dynamic-update-slice_fusion.2.refs_4_), channel_id=1, source_target_pairs={{0,2},{1,3},{2,0},{3,1},{4,6},{5,7},{6,4},{7,5},{8,10},{9,11},{10,... | collective-permute-start | bytes 1179656 | tf_op jit(solution)/shard_map/ppermute | solution.py:25
  21.9 0.1 collective-permute-start.8
  21.9 3.5 %collective-permute-done.1 = bf16[128,768]{1,0:T(8,128)(2,1)S(1)} collective-permute-done((bf16[128,768]{1,0:T(8,128)(2,1)S(1)}, bf16[128,768]{1,0:T(8,128)(2,1)S(1)}, u32[]{:S(2)}, u32[]{:S(2)}) %collective-permute-start.1) | collective-permute-done | bytes 196640 | tf_op jit(solution)/shard_map/ppermute | solution.py:25
  25.4 1.6 %collective-permute-start.2 = (bf16[256,768]{1,0:T(8,128)(2,1)S(1)}, bf16[256,768]{1,0:T(8,128)(2,1)S(1)}, u32[]{:S(2)}, u32[]{:S(2)}) collective-permute-start(bf16[256,768]{1,0:T(8,128)(2,1)S(1)} %constant_dynamic-update-slice_fusion.refs_6_), channel_id=1, source_target_pairs={{0,2},{1,3},{2,0},{3,1},{4,6},{5,7},{6,4},{7,5},{8,10},{9,11},{10,... | collective-permute-start | bytes 1179656 | tf_op jit(solution)/shard_map/ppermute | solution.py:25
  27.0 0.7 %collective-permute-done.5.refs_7_ = bf16[256,768]{1,0:T(8,128)(2,1)S(1)} collective-permute-done((bf16[256,768]{1,0:T(8,128)(2,1)S(1)}, bf16[256,768]{1,0:T(8,128)(2,1)S(1)}, u32[]{:S(2)}, u32[]{:S(2)}) %collective-permute-start.5) | collective-permute-done | bytes 393248 | tf_op jit(solution)/shard_map/ppermute | solution.py:25
  27.7 3.8 %collective-permute-start.10 = (bf16[256,768]{1,0:T(8,128)(2,1)S(1)}, bf16[256,768]{1,0:T(8,128)(2,1)}, u32[]{:S(2)}, u32[]{:S(2)}) collective-permute-start(bf16[256,768]{1,0:T(8,128)(2,1)S(1)} %collective-permute-done.5.refs_7_), channel_id=1, source_target_pairs={{0,4},{1,5},{2,6},{3,7},{4,0},{5,1},{6,2},{7,3},{8,12},{9,13},{10,... | collective-permute-start | bytes 1179656 | tf_op jit(solution)/shard_map/ppermute | solution.py:25
  31.5 2.2 %shard_map.58 = f32[32,8,128]{2,1,0:T(8,128)} custom-call(bf16[256,768]{1,0:T(8,128)(2,1)S(1)} %get-tuple-element.19.refs_0_.refs_1_, bf16[256,768]{1,0:T(8,128)(2,1)S(1)} %collective-permute-done.6.refs_1_.refs_2_, bf16[256,768]{1,0:T(8,128)(2,1)S(1)} %collective-permute-done.7.refs_2_.refs_3_, bf16[256,768]{1,0:T(8,128)(2,1)S(1)} %collective-permute-done.8.refs_3_, ...), custom_call_target="tpu_custom_call" | custom-call | flops 805306368 | bytes 2752512 | tf_op jit(solution)/shard_map/pallas_call | solution.py:59
  33.7 2.5 %collective-permute-done.2.refs_9_ = bf16[256,768]{1,0:T(8,128)(2,1)S(1)} collective-permute-done((bf16[256,768]{1,0:T(8,128)(2,1)S(1)}, bf16[256,768]{1,0:T(8,128)(2,1)S(1)}, u32[]{:S(2)}, u32[]{:S(2)}) %collective-permute-start.2) | collective-permute-done | bytes 393248 | tf_op jit(solution)/shard_map/ppermute | solution.py:25
  36.3 3.2 %all-to-all-start = ((f32[32,8,128]{2,1,0:T(8,128)}), f32[32,8,128]{2,1,0:T(8,128)S(1)}, u32[]{:S(2)}, u32[]{:S(2)}) async-start(f32[32,8,128]{2,1,0:T(8,128)} %shard_map.58), calls=%async_computation | async-start | bytes 262144 | tf_op jit(solution)/shard_map/all_to_all | solution.py:207
  39.5 8.2 %all-to-all-done.refs_0_ = f32[32,8,128]{2,1,0:T(8,128)S(1)} async-done(((f32[32,8,128]{2,1,0:T(8,128)}), f32[32,8,128]{2,1,0:T(8,128)S(1)}, u32[]{:S(2)}, u32[]{:S(2)}) %all-to-all-start) | async-done | bytes 131104 | tf_op jit(solution)/shard_map/all_to_all | solution.py:207
  47.7 3.0 %shard_map.59 = (f32[128]{0:T(128)}, f32[128]{0:T(128)}, f32[2,128,768]{2,1,0:T(8,128)S(1)}, f32[2,128,768]{2,1,0:T(8,128)S(1)}) custom-call(f32[32,8,128]{2,1,0:T(8,128)S(1)} %all-to-all-done.refs_0_, bf16[256,768]{1,0:T(8,128)(2,1)S(1)} %get-tuple-element.19.refs_0_.refs_1_, bf16[256,768]{1,0:T(8,128)(2,1)S(1)} %collective-permute-done.6.refs_1_.refs_2_, ...), custom_call_target="tpu_custom_call" | custom-call | flops 1610612736 | bytes 3670016 | tf_op jit(solution)/shard_map/pallas_call | solution.py:59
  50.7 0.3 collective-permute-start.11
  51.0 2.1 %collective-permute-done.11.got = f32[2,128,768]{2,1,0:T(8,128)S(1)} collective-permute-done((f32[2,128,768]{2,1,0:T(8,128)S(1)}, f32[2,128,768]{2,1,0:T(8,128)S(1)}, u32[]{:S(2)}, u32[]{:S(2)}) %collective-permute-start.11) | collective-permute-done | bytes 786464 | tf_op jit(solution)/shard_map/ppermute | solution.py:25
  53.1 1.0 %shard_map.60 = (f32[128,768]{1,0:T(8,128)}, f32[128,768]{1,0:T(8,128)}) custom-call(f32[2,128,768]{2,1,0:T(8,128)S(1)} %get-tuple-element.26.kept, f32[2,128,768]{2,1,0:T(8,128)S(1)} %collective-permute-done.11.got), custom_call_target="tpu_custom_call" | custom-call | bytes 1572864 | tf_op jit(solution)/shard_map/pallas_call | solution.py:59
  (14 shorter events, 0.1 us)
Async XLA Ops:
  0.6 4.2 %copy-start = (f32[128,768]{1,0:T(8,128)S(1)}, f32[128,768]{1,0:T(8,128)}, u32[]{:S(2)}) copy-start(f32[128,768]{1,0:T(8,128)} %param.2) | copy-start | bytes 1179652
  1.7 10.9 %collective-permute-start.3 = (bf16[128,768]{1,0:T(8,128)(2,1)S(1)}, bf16[128,768]{1,0:T(8,128)(2,1)S(1)}, u32[]{:S(2)}, u32[]{:S(2)}) collective-permute-start(bf16[128,768]{1,0:T(8,128)(2,1)S(1)} %convert_element_type.7.text), channel_id=1, source_target_pairs={{0,8},{1,9},{2,10},{3,11},{4,12},{5,13},{6,14},{7,15},{8,16},{9,17... | collective-permute-start | bytes 589832 | tf_op jit(solution)/shard_map/ppermute | solution.py:25
  4.8 14.9 %collective-permute-start.4 = (bf16[128,768]{1,0:T(8,128)(2,1)S(1)}, bf16[128,768]{1,0:T(8,128)(2,1)S(1)}, u32[]{:S(2)}, u32[]{:S(2)}) collective-permute-start(bf16[128,768]{1,0:T(8,128)(2,1)S(1)} %convert_element_type.6.image), channel_id=1, source_target_pairs={{0,24},{1,25},{2,26},{3,27},{4,28},{5,29},{6,30},{7,31},{8,0},{9,1... | collective-permute-start | bytes 589832 | tf_op jit(solution)/shard_map/ppermute | solution.py:25
  7.0 14.9 %collective-permute-start.7 = (bf16[256,768]{1,0:T(8,128)(2,1)S(1)}, bf16[256,768]{1,0:T(8,128)(2,1)S(1)}, u32[]{:S(2)}, u32[]{:S(2)}) collective-permute-start(bf16[256,768]{1,0:T(8,128)(2,1)S(1)} %get-tuple-element.19.refs_0_.refs_1_), channel_id=1, source_target_pairs={{0,2},{1,3},{2,0},{3,1},{4,6},{5,7},{6,4},{7,5},{8,10},{9,11},{10,... | collective-permute-start | bytes 1179656 | tf_op jit(solution)/shard_map/ppermute | solution.py:25
  8.7 22.8 %collective-permute-start.6 = (bf16[256,768]{1,0:T(8,128)(2,1)S(1)}, bf16[256,768]{1,0:T(8,128)(2,1)S(1)}, u32[]{:S(2)}, u32[]{:S(2)}) collective-permute-start(bf16[256,768]{1,0:T(8,128)(2,1)S(1)} %get-tuple-element.19.refs_0_.refs_1_), channel_id=1, source_target_pairs={{0,1},{1,0},{2,3},{3,2},{4,5},{5,4},{6,7},{7,6},{8,9},{9,8},{10,11... | collective-permute-start | bytes 1179656 | tf_op jit(solution)/shard_map/ppermute | solution.py:25
  8.7 11.1 %collective-permute-start = (bf16[128,768]{1,0:T(8,128)(2,1)S(1)}, bf16[128,768]{1,0:T(8,128)(2,1)S(1)}, u32[]{:S(2)}, u32[]{:S(2)}) collective-permute-start(bf16[128,768]{1,0:T(8,128)(2,1)S(1)} %get-tuple-element.17), channel_id=1, source_target_pairs={{0,4},{1,5},{2,6},{3,7},{4,0},{5,1},{6,2},{7,3},{8,12},{9,13},{10,... | collective-permute-start | bytes 589832 | tf_op jit(solution)/shard_map/ppermute | solution.py:25
  12.6 12.8 %collective-permute-start.1 = (bf16[128,768]{1,0:T(8,128)(2,1)S(1)}, bf16[128,768]{1,0:T(8,128)(2,1)S(1)}, u32[]{:S(2)}, u32[]{:S(2)}) collective-permute-start(bf16[128,768]{1,0:T(8,128)(2,1)S(1)} %get-tuple-element.18), channel_id=1, source_target_pairs={{0,20},{1,21},{2,22},{3,23},{4,16},{5,17},{6,18},{7,19},{8,28},{9,... | collective-permute-start | bytes 589832 | tf_op jit(solution)/shard_map/ppermute | solution.py:25
  19.8 11.7 %collective-permute-start.9 = (bf16[256,768]{1,0:T(8,128)(2,1)S(1)}, bf16[256,768]{1,0:T(8,128)(2,1)S(1)}, u32[]{:S(2)}, u32[]{:S(2)}) collective-permute-start(bf16[256,768]{1,0:T(8,128)(2,1)S(1)} %constant_dynamic-update-slice_fusion.2.refs_4_), channel_id=1, source_target_pairs={{0,4},{1,5},{2,6},{3,7},{4,0},{5,1},{6,2},{7,3},{8,12},{9,13},{10,... | collective-permute-start | bytes 1179656 | tf_op jit(solution)/shard_map/ppermute | solution.py:25
  19.9 7.8 %collective-permute-start.5 = (bf16[256,768]{1,0:T(8,128)(2,1)S(1)}, bf16[256,768]{1,0:T(8,128)(2,1)S(1)}, u32[]{:S(2)}, u32[]{:S(2)}) collective-permute-start(bf16[256,768]{1,0:T(8,128)(2,1)S(1)} %constant_dynamic-update-slice_fusion.2.refs_4_), channel_id=1, source_target_pairs={{0,2},{1,3},{2,0},{3,1},{4,6},{5,7},{6,4},{7,5},{8,10},{9,11},{10,... | collective-permute-start | bytes 1179656 | tf_op jit(solution)/shard_map/ppermute | solution.py:25
  21.9 9.7 %collective-permute-start.8 = (bf16[256,768]{1,0:T(8,128)(2,1)S(1)}, bf16[256,768]{1,0:T(8,128)(2,1)S(1)}, u32[]{:S(2)}, u32[]{:S(2)}) collective-permute-start(bf16[256,768]{1,0:T(8,128)(2,1)S(1)} %collective-permute-done.7.refs_2_.refs_3_), channel_id=1, source_target_pairs={{0,1},{1,0},{2,3},{3,2},{4,5},{5,4},{6,7},{7,6},{8,9},{9,8},{10,11... | collective-permute-start | bytes 1179656 | tf_op jit(solution)/shard_map/ppermute | solution.py:25
  25.4 10.8 %collective-permute-start.2 = (bf16[256,768]{1,0:T(8,128)(2,1)S(1)}, bf16[256,768]{1,0:T(8,128)(2,1)S(1)}, u32[]{:S(2)}, u32[]{:S(2)}) collective-permute-start(bf16[256,768]{1,0:T(8,128)(2,1)S(1)} %constant_dynamic-update-slice_fusion.refs_6_), channel_id=1, source_target_pairs={{0,2},{1,3},{2,0},{3,1},{4,6},{5,7},{6,4},{7,5},{8,10},{9,11},{10,... | collective-permute-start | bytes 1179656 | tf_op jit(solution)/shard_map/ppermute | solution.py:25
  27.7 11.8 %collective-permute-start.10 = (bf16[256,768]{1,0:T(8,128)(2,1)S(1)}, bf16[256,768]{1,0:T(8,128)(2,1)}, u32[]{:S(2)}, u32[]{:S(2)}) collective-permute-start(bf16[256,768]{1,0:T(8,128)(2,1)S(1)} %collective-permute-done.5.refs_7_), channel_id=1, source_target_pairs={{0,4},{1,5},{2,6},{3,7},{4,0},{5,1},{6,2},{7,3},{8,12},{9,13},{10,... | collective-permute-start | bytes 1179656 | tf_op jit(solution)/shard_map/ppermute | solution.py:25
  36.3 11.5 %all-to-all-start = ((f32[32,8,128]{2,1,0:T(8,128)}), f32[32,8,128]{2,1,0:T(8,128)S(1)}, u32[]{:S(2)}, u32[]{:S(2)}) async-start(f32[32,8,128]{2,1,0:T(8,128)} %shard_map.58), calls=%async_computation | async-start | bytes 262144 | tf_op jit(solution)/shard_map/all_to_all | solution.py:207
  50.7 2.4 %collective-permute-start.11 = (f32[2,128,768]{2,1,0:T(8,128)S(1)}, f32[2,128,768]{2,1,0:T(8,128)S(1)}, u32[]{:S(2)}, u32[]{:S(2)}) collective-permute-start(f32[2,128,768]{2,1,0:T(8,128)S(1)} %get-tuple-element.27), channel_id=1, source_target_pairs={{0,1},{1,0},{2,3},{3,2},{4,5},{5,4},{6,7},{7,6},{8,9},{9,8},{10,11... | collective-permute-start | bytes 2359304 | tf_op jit(solution)/shard_map/ppermute | solution.py:25

commit v7 on v6

--- a/solution.py
+++ b/solution.py
@@ -95,22 +95,36 @@
     cols[odd, 3, at] = pc[n:]
 
 
-def stats_kernel(count, *refs):
-    own, core, x, corex, ab, b2, pc, out, rows, cols = refs
-    n = own.shape[0] // 2
-    pos = lax.axis_index("span")
+def stats_kernel(own, core, x, corex, ab, pc, part, rows, cols):
+    n = own.shape[0] // 2
     odd = lax.rem(lax.axis_index("batch"), 2)
-    fill_columns(cols, 0, odd, own, ab, b2, pc)
-    part = []
     for side in range(2):
         for q, ref in enumerate((own, core, x, corex)):
             rows[side, q * n : (q + 1) * n] = ref[n:] if side == 0 else ref[:n]
-        s = dot_t(cols[side].reshape(STEPS * n, cols.shape[-1]), rows[side]) * LOGIT_SCALE
+        for slot, ref in enumerate((own, ab)):
+            cols[side, slot] = ref[side * n : (side + 1) * n]
+    cols[1 - odd, 2] = pc[:n]
+    cols[odd, 2] = pc[n:]
+    for side in range(2):
+        s = dot_t(cols[side].reshape((STEPS - 1) * n, cols.shape[-1]), rows[side]) * LOGIT_SCALE
         top = jnp.max(s, axis=0, keepdims=True)
-        lse = top + jnp.log(jnp.sum(jnp.exp(s - top), axis=0, keepdims=True))
-        part += [lse[:, q * n : (q + 1) * n] for q in range(SPANS)]
+        part[side] = (top + jnp.log(jnp.sum(jnp.exp(s - top), axis=0, keepdims=True)))[0]
+
+
+def finish_kernel(count, part, own, core, x, corex, b2, _, out, rows):
+    n = own.shape[0] // 2
+    pos = lax.axis_index("span")
+    done = []
+    for side in range(2):
+        for q, ref in enumerate((own, core, x, corex)):
+            rows[side, q * n : (q + 1) * n] = ref[n:] if side == 0 else ref[:n]
+        s = dot_t(b2[side * n : (side + 1) * n], rows[side]) * LOGIT_SCALE
+        before = part[side : side + 1]
+        top = jnp.maximum(before, jnp.max(s, axis=0, keepdims=True))
+        lse = top + jnp.log(jnp.exp(before - top) + jnp.sum(jnp.exp(s - top), axis=0, keepdims=True))
+        done += [lse[:, q * n : (q + 1) * n] for q in range(SPANS)]
     for sigma in range(SPANS):
-        v = jnp.concatenate([part[4 * (r // 4) + ((r % 4) ^ sigma)] for r in range(2 * SPANS)])
+        v = jnp.concatenate([done[4 * (r // 4) + ((r % 4) ^ sigma)] for r in range(2 * SPANS)])
         to = pos ^ sigma
 
         def store(b, _):
@@ -195,15 +209,22 @@
     corex = over_core(x)
     far_ab, far_pc = over_x(ab), over_x(pc)
     far_b = in_pair(far_ab)
-    far_ab, core, _ = lax.optimization_barrier((far_ab, core, over_core(pc)))
+    part = call(
+        stats_kernel,
+        jax.ShapeDtypeStruct((2, SPANS * n), F32),
+        [pltpu.VMEM((2, SPANS * n, width), BF16), pltpu.VMEM((2, STEPS - 1, n, width), BF16)],
+        4 * SPANS * n * (STEPS - 1) * n * width,
+        own, core, x, corex, ab, pc,
+    )
+    seen = over_core(pc)
+    far_ab, part = lax.optimization_barrier((far_ab, part))
     send = call(
-        functools.partial(stats_kernel, count),
+        functools.partial(finish_kernel, count),
         jax.ShapeDtypeStruct((count * SPANS, 2 * SPANS, n), F32),
-        [pltpu.VMEM((2, SPANS * n, width), BF16), pltpu.VMEM((2, STEPS, n, width), BF16)],
-        4 * SPANS * n * STEPS * n * width,
-        own, core, x, corex, ab, b2, pc,
-    )
-    far_pc, send = lax.optimization_barrier((far_pc, send))
+        [pltpu.VMEM((2, SPANS * n, width), BF16)],
+        4 * SPANS * n * n * width,
+        part, own, core, x, corex, b2, seen, remote=(6,),
+    )
     got = lax.all_to_all(send, AXES, 0, 0, tiled=True)
     row = jax.ShapeDtypeStruct((n,), F32)
     both = jax.ShapeDtypeStruct((2, n, width), F32)

time: 54.2 us -> 51.6 us (0.952)
  waiting for transfers between devices: 19.4 us -> 16.7 us
    all_to_all x1, waiting for transfers between devices: 8.22 us -> 6.34 us  [body(): got = lax.all_to_all(send, AXES, 0, 0, tiled=True)]
    ppermute x12 -> x13, starting transfers between devices: 23.3 us -> 22 us  [moved(): return lax.ppermute(value, AXES, pairs)]
    all_to_all x1, starting transfers between devices: 3.24 us -> 4.1 us  [body(): got = lax.all_to_all(send, AXES, 0, 0, tiled=True)]
    ppermute x12 -> x13, waiting for transfers between devices: 11.2 us -> 10.4 us  [moved(): return lax.ppermute(value, AXES, pairs)]
    pallas_call x4 -> x5, Pallas kernels: 6.19 us -> 6.64 us  [call(): pl.pallas_call(kernel, out_shape=out_shape, in_specs=[pl.BlockSpec(memory...]
  transfers between devices with their start and end apart: 13 -> 14, of which waited for: 6 -> 7; matrix products, arithmetic and copies ran while one was open for 0% -> 0% of each run, Pallas kernels for 4% -> 5%
where the time goes in v7:
time: 51.6 us; the launch traced here: 51.4 us
  starting transfers between devices  26.1 us (51%)
  waiting for transfers between devices  16.7 us (32%)
  Pallas kernels  6.64 us (13%)
  other arithmetic  1.09 us (2%)
  between operations  0.77 us (1%)
    ppermute x13, starting transfers between devices, moved(): return lax.ppermute(value, AXES, pairs)  22 us
    ppermute x13, waiting for transfers between devices, moved(): return lax.ppermute(value, AXES, pairs)  10.4 us
    pallas_call x5, Pallas kernels, call(): pl.pallas_call(kernel, out_shape=out_shape, in_specs=[pl.BlockSpec(memory...  6.64 us
    all_to_all x1, waiting for transfers between devices, body(): got = lax.all_to_all(send, AXES, 0, 0, tiled=True)  6.34 us
    all_to_all x1, starting transfers between devices, body(): got = lax.all_to_all(send, AXES, 0, 0, tiled=True)  4.1 us
    convert_element_type x2, other arithmetic, body(): i0, t0 = (image_embeds.astype(BF16), text_embeds.astype(BF16))  1.09 us
  transfers between devices with their start and end apart: 14, of which 7 were waited for; matrix products, arithmetic and copies ran while one was open for 0% of the time, Pallas kernels for 5%

profile of v7, /device:TPU:0, one launch (start us, length us, event | category | flops | bytes accessed | tf_op | source)
XLA Modules:
  0.0 51.4 jit_solution(10805771220240954890)
XLA Ops:
  0.6 1.1 %convert_element_type.6.text = bf16[128,768]{1,0:T(8,128)(2,1)S(1)} convert(f32[128,768]{1,0:T(8,128)} %param.3) | non-fusion elementwise | flops 98304 | bytes 589824 | tf_op jit(solution)/shard_map/convert_element_type | solution.py:199
  1.7 3.1 %collective-permute-start = (bf16[128,768]{1,0:T(8,128)(2,1)S(1)}, bf16[128,768]{1,0:T(8,128)(2,1)S(1)}, u32[]{:S(2)}, u32[]{:S(2)}) collective-permute-start(bf16[128,768]{1,0:T(8,128)(2,1)S(1)} %convert_element_type.6.text), channel_id=1, source_target_pairs={{0,8},{1,9},{2,10},{3,11},{4,12},{5,13},{6,14},{7,15},{8,16},{9,17... | collective-permute-start | bytes 589832 | tf_op jit(solution)/shard_map/ppermute | solution.py:25
  4.8 2.1 %collective-permute-start.1 = (bf16[128,768]{1,0:T(8,128)(2,1)S(1)}, bf16[128,768]{1,0:T(8,128)(2,1)S(1)}, u32[]{:S(2)}, u32[]{:S(2)}) collective-permute-start(bf16[128,768]{1,0:T(8,128)(2,1)S(1)} %convert_element_type.7.image), channel_id=1, source_target_pairs={{0,24},{1,25},{2,26},{3,27},{4,28},{5,29},{6,30},{7,31},{8,0},{9,1... | collective-permute-start | bytes 589832 | tf_op jit(solution)/shard_map/ppermute | solution.py:25
  7.0 1.8 %collective-permute-start.4 = (bf16[256,768]{1,0:T(8,128)(2,1)S(1)}, bf16[256,768]{1,0:T(8,128)(2,1)S(1)}, u32[]{:S(2)}, u32[]{:S(2)}) collective-permute-start(bf16[256,768]{1,0:T(8,128)(2,1)S(1)} %get-tuple-element.15.own.refs_1_), channel_id=1, source_target_pairs={{0,2},{1,3},{2,0},{3,1},{4,6},{5,7},{6,4},{7,5},{8,10},{9,11},{10,... | collective-permute-start | bytes 1179656 | tf_op jit(solution)/shard_map/ppermute | solution.py:25
  8.7 1.5 %collective-permute-start.6 = (bf16[128,768]{1,0:T(8,128)(2,1)S(1)}, bf16[128,768]{1,0:T(8,128)(2,1)S(1)}, u32[]{:S(2)}, u32[]{:S(2)}) collective-permute-start(bf16[128,768]{1,0:T(8,128)(2,1)S(1)} %get-tuple-element.16), channel_id=1, source_target_pairs={{0,4},{1,5},{2,6},{3,7},{4,0},{5,1},{6,2},{7,3},{8,12},{9,13},{10,... | collective-permute-start | bytes 589832 | tf_op jit(solution)/shard_map/ppermute | solution.py:25
  10.3 2.3 %collective-permute-done = bf16[128,768]{1,0:T(8,128)(2,1)S(1)} collective-permute-done((bf16[128,768]{1,0:T(8,128)(2,1)S(1)}, bf16[128,768]{1,0:T(8,128)(2,1)S(1)}, u32[]{:S(2)}, u32[]{:S(2)}) %collective-permute-start) | collective-permute-done | bytes 196640 | tf_op jit(solution)/shard_map/ppermute | solution.py:25
  12.6 7.1 %collective-permute-start.7 = (bf16[128,768]{1,0:T(8,128)(2,1)S(1)}, bf16[128,768]{1,0:T(8,128)(2,1)S(1)}, u32[]{:S(2)}, u32[]{:S(2)}) collective-permute-start(bf16[128,768]{1,0:T(8,128)(2,1)S(1)} %get-tuple-element.17), channel_id=1, source_target_pairs={{0,20},{1,21},{2,22},{3,23},{4,16},{5,17},{6,18},{7,19},{8,28},{9,... | collective-permute-start | bytes 589832 | tf_op jit(solution)/shard_map/ppermute | solution.py:25
  19.8 0.1 collective-permute-start.8
  19.9 2.0 %collective-permute-start.2 = (bf16[256,768]{1,0:T(8,128)(2,1)S(1)}, bf16[256,768]{1,0:T(8,128)(2,1)S(1)}, u32[]{:S(2)}, u32[]{:S(2)}) collective-permute-start(bf16[256,768]{1,0:T(8,128)(2,1)S(1)} %constant_dynamic-update-slice_fusion.ab.refs_4_), channel_id=1, source_target_pairs={{0,2},{1,3},{2,0},{3,1},{4,6},{5,7},{6,4},{7,5},{8,10},{9,11},{10,... | collective-permute-start | bytes 1179656 | tf_op jit(solution)/shard_map/ppermute | solution.py:25
  21.9 3.5 %collective-permute-done.7 = bf16[128,768]{1,0:T(8,128)(2,1)S(1)} collective-permute-done((bf16[128,768]{1,0:T(8,128)(2,1)S(1)}, bf16[128,768]{1,0:T(8,128)(2,1)S(1)}, u32[]{:S(2)}, u32[]{:S(2)}) %collective-permute-start.7) | collective-permute-done | bytes 196640 | tf_op jit(solution)/shard_map/ppermute | solution.py:25
  25.4 0.1 collective-permute-start.9
  25.5 1.6 %collective-permute-start.11 = (bf16[256,768]{1,0:T(8,128)(2,1)S(1)}, bf16[256,768]{1,0:T(8,128)(2,1)S(1)}, u32[]{:S(2)}, u32[]{:S(2)}) collective-permute-start(bf16[256,768]{1,0:T(8,128)(2,1)S(1)} %constant_dynamic-update-slice_fusion.2.pc.refs_6_), channel_id=1, source_target_pairs={{0,2},{1,3},{2,0},{3,1},{4,6},{5,7},{6,4},{7,5},{8,10},{9,11},{10,... | collective-permute-start | bytes 1179656 | tf_op jit(solution)/shard_map/ppermute | solution.py:25
  27.1 0.6 %collective-permute-done.2.refs_7_ = bf16[256,768]{1,0:T(8,128)(2,1)S(1)} collective-permute-done((bf16[256,768]{1,0:T(8,128)(2,1)S(1)}, bf16[256,768]{1,0:T(8,128)(2,1)S(1)}, u32[]{:S(2)}, u32[]{:S(2)}) %collective-permute-start.2) | collective-permute-done | bytes 393248 | tf_op jit(solution)/shard_map/ppermute | solution.py:25
  27.7 2.4 %collective-permute-start.10 = (bf16[256,768]{1,0:T(8,128)(2,1)S(1)}, bf16[256,768]{1,0:T(8,128)(2,1)}, u32[]{:S(2)}, u32[]{:S(2)}) collective-permute-start(bf16[256,768]{1,0:T(8,128)(2,1)S(1)} %collective-permute-done.2.refs_7_), channel_id=1, source_target_pairs={{0,4},{1,5},{2,6},{3,7},{4,0},{5,1},{6,2},{7,3},{8,12},{9,13},{10,... | collective-permute-start | bytes 1179656 | tf_op jit(solution)/shard_map/ppermute | solution.py:25
  30.1 1.1 %shard_map.58.part = f32[2,512]{1,0:T(2,128)S(1)} custom-call(bf16[256,768]{1,0:T(8,128)(2,1)S(1)} %get-tuple-element.15.own.refs_1_, bf16[256,768]{1,0:T(8,128)(2,1)S(1)} %collective-permute-done.3.core.refs_2_, bf16[256,768]{1,0:T(8,128)(2,1)S(1)} %collective-permute-done.4.x.refs_3_, bf16[256,768]{1,0:T(8,128)(2,1)S(1)} %collective-permute-done.5.corex, ...), custom_call_target="tpu_custom_call" | custom-call | flops 603979776 | bytes 2359296 | tf_op jit(solution)/shard_map/pallas_call | solution.py:59
  31.2 1.5 %shard_map.59 = f32[32,8,128]{2,1,0:T(8,128)} custom-call(f32[2,512]{1,0:T(2,128)S(1)} %shard_map.58.part, bf16[256,768]{1,0:T(8,128)(2,1)S(1)} %get-tuple-element.15.own.refs_1_, bf16[256,768]{1,0:T(8,128)(2,1)S(1)} %collective-permute-done.3.core.refs_2_, bf16[256,768]{1,0:T(8,128)(2,1)S(1)} %collective-permute-done.4.x.refs_3_, ...), custom_call_target="tpu_custom_call" | custom-call | flops 201326592 | bytes 2363392 | tf_op jit(solution)/shard_map/pallas_call | solution.py:59
  32.8 4.1 %all-to-all-start = ((f32[32,8,128]{2,1,0:T(8,128)}), f32[32,8,128]{2,1,0:T(8,128)S(1)}, u32[]{:S(2)}, u32[]{:S(2)}) async-start(f32[32,8,128]{2,1,0:T(8,128)} %shard_map.59), calls=%async_computation | async-start | bytes 262144 | tf_op jit(solution)/shard_map/all_to_all | solution.py:228
  36.9 0.2 collective-permute-done.11.refs_9_
  37.0 1.7 %collective-permute-done.10.refs_8_ = bf16[256,768]{1,0:T(8,128)(2,1)} collective-permute-done((bf16[256,768]{1,0:T(8,128)(2,1)S(1)}, bf16[256,768]{1,0:T(8,128)(2,1)}, u32[]{:S(2)}, u32[]{:S(2)}) %collective-permute-start.10) | collective-permute-done | bytes 393248 | tf_op jit(solution)/shard_map/ppermute | solution.py:25
  38.8 6.3 %all-to-all-done.refs_0_ = f32[32,8,128]{2,1,0:T(8,128)S(1)} async-done(((f32[32,8,128]{2,1,0:T(8,128)}), f32[32,8,128]{2,1,0:T(8,128)S(1)}, u32[]{:S(2)}, u32[]{:S(2)}) %all-to-all-start) | async-done | bytes 131104 | tf_op jit(solution)/shard_map/all_to_all | solution.py:228
  45.1 3.0 %shard_map.60 = (f32[128]{0:T(128)}, f32[128]{0:T(128)}, f32[2,128,768]{2,1,0:T(8,128)S(1)}, f32[2,128,768]{2,1,0:T(8,128)S(1)}) custom-call(f32[32,8,128]{2,1,0:T(8,128)S(1)} %all-to-all-done.refs_0_, bf16[256,768]{1,0:T(8,128)(2,1)S(1)} %get-tuple-element.15.own.refs_1_, bf16[256,768]{1,0:T(8,128)(2,1)S(1)} %collective-permute-done.3.core.refs_2_, ...), custom_call_target="tpu_custom_call" | custom-call | flops 1610612736 | bytes 3670016 | tf_op jit(solution)/shard_map/pallas_call | solution.py:59
  48.1 0.3 collective-permute-start.12
  48.4 2.1 %collective-permute-done.12.got = f32[2,128,768]{2,1,0:T(8,128)S(1)} collective-permute-done((f32[2,128,768]{2,1,0:T(8,128)S(1)}, f32[2,128,768]{2,1,0:T(8,128)S(1)}, u32[]{:S(2)}, u32[]{:S(2)}) %collective-permute-start.12) | collective-permute-done | bytes 786464 | tf_op jit(solution)/shard_map/ppermute | solution.py:25
  50.4 1.0 %shard_map.61 = (f32[128,768]{1,0:T(8,128)}, f32[128,768]{1,0:T(8,128)}) custom-call(f32[2,128,768]{2,1,0:T(8,128)S(1)} %get-tuple-element.22.kept, f32[2,128,768]{2,1,0:T(8,128)S(1)} %collective-permute-done.12.got), custom_call_target="tpu_custom_call" | custom-call | bytes 1572864 | tf_op jit(solution)/shard_map/pallas_call | solution.py:59
  (17 shorter events, 0.2 us)
Async XLA Ops:
  0.6 4.2 %copy-start = (f32[128,768]{1,0:T(8,128)S(1)}, f32[128,768]{1,0:T(8,128)}, u32[]{:S(2)}) copy-start(f32[128,768]{1,0:T(8,128)} %param.2) | copy-start | bytes 1179652
  1.7 10.9 %collective-permute-start = (bf16[128,768]{1,0:T(8,128)(2,1)S(1)}, bf16[128,768]{1,0:T(8,128)(2,1)S(1)}, u32[]{:S(2)}, u32[]{:S(2)}) collective-permute-start(bf16[128,768]{1,0:T(8,128)(2,1)S(1)} %convert_element_type.6.text), channel_id=1, source_target_pairs={{0,8},{1,9},{2,10},{3,11},{4,12},{5,13},{6,14},{7,15},{8,16},{9,17... | collective-permute-start | bytes 589832 | tf_op jit(solution)/shard_map/ppermute | solution.py:25
  4.8 14.9 %collective-permute-start.1 = (bf16[128,768]{1,0:T(8,128)(2,1)S(1)}, bf16[128,768]{1,0:T(8,128)(2,1)S(1)}, u32[]{:S(2)}, u32[]{:S(2)}) collective-permute-start(bf16[128,768]{1,0:T(8,128)(2,1)S(1)} %convert_element_type.7.image), channel_id=1, source_target_pairs={{0,24},{1,25},{2,26},{3,27},{4,28},{5,29},{6,30},{7,31},{8,0},{9,1... | collective-permute-start | bytes 589832 | tf_op jit(solution)/shard_map/ppermute | solution.py:25
  7.0 14.9 %collective-permute-start.4 = (bf16[256,768]{1,0:T(8,128)(2,1)S(1)}, bf16[256,768]{1,0:T(8,128)(2,1)S(1)}, u32[]{:S(2)}, u32[]{:S(2)}) collective-permute-start(bf16[256,768]{1,0:T(8,128)(2,1)S(1)} %get-tuple-element.15.own.refs_1_), channel_id=1, source_target_pairs={{0,2},{1,3},{2,0},{3,1},{4,6},{5,7},{6,4},{7,5},{8,10},{9,11},{10,... | collective-permute-start | bytes 1179656 | tf_op jit(solution)/shard_map/ppermute | solution.py:25
  8.7 16.8 %collective-permute-start.3 = (bf16[256,768]{1,0:T(8,128)(2,1)S(1)}, bf16[256,768]{1,0:T(8,128)(2,1)S(1)}, u32[]{:S(2)}, u32[]{:S(2)}) collective-permute-start(bf16[256,768]{1,0:T(8,128)(2,1)S(1)} %get-tuple-element.15.own.refs_1_), channel_id=1, source_target_pairs={{0,1},{1,0},{2,3},{3,2},{4,5},{5,4},{6,7},{7,6},{8,9},{9,8},{10,11... | collective-permute-start | bytes 1179656 | tf_op jit(solution)/shard_map/ppermute | solution.py:25
  8.7 11.1 %collective-permute-start.6 = (bf16[128,768]{1,0:T(8,128)(2,1)S(1)}, bf16[128,768]{1,0:T(8,128)(2,1)S(1)}, u32[]{:S(2)}, u32[]{:S(2)}) collective-permute-start(bf16[128,768]{1,0:T(8,128)(2,1)S(1)} %get-tuple-element.16), channel_id=1, source_target_pairs={{0,4},{1,5},{2,6},{3,7},{4,0},{5,1},{6,2},{7,3},{8,12},{9,13},{10,... | collective-permute-start | bytes 589832 | tf_op jit(solution)/shard_map/ppermute | solution.py:25
  12.6 12.8 %collective-permute-start.7 = (bf16[128,768]{1,0:T(8,128)(2,1)S(1)}, bf16[128,768]{1,0:T(8,128)(2,1)S(1)}, u32[]{:S(2)}, u32[]{:S(2)}) collective-permute-start(bf16[128,768]{1,0:T(8,128)(2,1)S(1)} %get-tuple-element.17), channel_id=1, source_target_pairs={{0,20},{1,21},{2,22},{3,23},{4,16},{5,17},{6,18},{7,19},{8,28},{9,... | collective-permute-start | bytes 589832 | tf_op jit(solution)/shard_map/ppermute | solution.py:25
  19.8 11.4 %collective-permute-start.8 = (bf16[256,768]{1,0:T(8,128)(2,1)S(1)}, bf16[256,768]{1,0:T(8,128)(2,1)S(1)}, u32[]{:S(2)}, u32[]{:S(2)}) collective-permute-start(bf16[256,768]{1,0:T(8,128)(2,1)S(1)} %constant_dynamic-update-slice_fusion.ab.refs_4_), channel_id=1, source_target_pairs={{0,4},{1,5},{2,6},{3,7},{4,0},{5,1},{6,2},{7,3},{8,12},{9,13},{10,... | collective-permute-start | bytes 1179656 | tf_op jit(solution)/shard_map/ppermute | solution.py:25
  19.9 7.8 %collective-permute-start.2 = (bf16[256,768]{1,0:T(8,128)(2,1)S(1)}, bf16[256,768]{1,0:T(8,128)(2,1)S(1)}, u32[]{:S(2)}, u32[]{:S(2)}) collective-permute-start(bf16[256,768]{1,0:T(8,128)(2,1)S(1)} %constant_dynamic-update-slice_fusion.ab.refs_4_), channel_id=1, source_target_pairs={{0,2},{1,3},{2,0},{3,1},{4,6},{5,7},{6,4},{7,5},{8,10},{9,11},{10,... | collective-permute-start | bytes 1179656 | tf_op jit(solution)/shard_map/ppermute | solution.py:25
  21.9 8.2 %collective-permute-start.5 = (bf16[256,768]{1,0:T(8,128)(2,1)S(1)}, bf16[256,768]{1,0:T(8,128)(2,1)S(1)}, u32[]{:S(2)}, u32[]{:S(2)}) collective-permute-start(bf16[256,768]{1,0:T(8,128)(2,1)S(1)} %collective-permute-done.4.x.refs_3_), channel_id=1, source_target_pairs={{0,1},{1,0},{2,3},{3,2},{4,5},{5,4},{6,7},{7,6},{8,9},{9,8},{10,11... | collective-permute-start | bytes 1179656 | tf_op jit(solution)/shard_map/ppermute | solution.py:25
  25.4 5.8 %collective-permute-start.9 = (bf16[256,768]{1,0:T(8,128)(2,1)S(1)}, bf16[256,768]{1,0:T(8,128)(2,1)S(1)}, u32[]{:S(2)}, u32[]{:S(2)}) collective-permute-start(bf16[256,768]{1,0:T(8,128)(2,1)S(1)} %constant_dynamic-update-slice_fusion.2.pc.refs_6_), channel_id=1, source_target_pairs={{0,1},{1,0},{2,3},{3,2},{4,5},{5,4},{6,7},{7,6},{8,9},{9,8},{10,11... | collective-permute-start | bytes 1179656 | tf_op jit(solution)/shard_map/ppermute | solution.py:25
  25.5 11.5 %collective-permute-start.11 = (bf16[256,768]{1,0:T(8,128)(2,1)S(1)}, bf16[256,768]{1,0:T(8,128)(2,1)S(1)}, u32[]{:S(2)}, u32[]{:S(2)}) collective-permute-start(bf16[256,768]{1,0:T(8,128)(2,1)S(1)} %constant_dynamic-update-slice_fusion.2.pc.refs_6_), channel_id=1, source_target_pairs={{0,2},{1,3},{2,0},{3,1},{4,6},{5,7},{6,4},{7,5},{8,10},{9,11},{10,... | collective-permute-start | bytes 1179656 | tf_op jit(solution)/shard_map/ppermute | solution.py:25
  27.7 11.1 %collective-permute-start.10 = (bf16[256,768]{1,0:T(8,128)(2,1)S(1)}, bf16[256,768]{1,0:T(8,128)(2,1)}, u32[]{:S(2)}, u32[]{:S(2)}) collective-permute-start(bf16[256,768]{1,0:T(8,128)(2,1)S(1)} %collective-permute-done.2.refs_7_), channel_id=1, source_target_pairs={{0,4},{1,5},{2,6},{3,7},{4,0},{5,1},{6,2},{7,3},{8,12},{9,13},{10,... | collective-permute-start | bytes 1179656 | tf_op jit(solution)/shard_map/ppermute | solution.py:25
  32.8 12.3 %all-to-all-start = ((f32[32,8,128]{2,1,0:T(8,128)}), f32[32,8,128]{2,1,0:T(8,128)S(1)}, u32[]{:S(2)}, u32[]{:S(2)}) async-start(f32[32,8,128]{2,1,0:T(8,128)} %shard_map.59), calls=%async_computation | async-start | bytes 262144 | tf_op jit(solution)/shard_map/all_to_all | solution.py:228
  48.1 2.4 %collective-permute-start.12 = (f32[2,128,768]{2,1,0:T(8,128)S(1)}, f32[2,128,768]{2,1,0:T(8,128)S(1)}, u32[]{:S(2)}, u32[]{:S(2)}) collective-permute-start(f32[2,128,768]{2,1,0:T(8,128)S(1)} %get-tuple-element.23), channel_id=1, source_target_pairs={{0,1},{1,0},{2,3},{3,2},{4,5},{5,4},{6,7},{7,6},{8,9},{9,8},{10,11... | collective-permute-start | bytes 2359304 | tf_op jit(solution)/shard_map/ppermute | solution.py:25

commit v8 on v7

--- a/solution.py
+++ b/solution.py
@@ -208,7 +208,6 @@
     x = over_x(own)
     corex = over_core(x)
     far_ab, far_pc = over_x(ab), over_x(pc)
-    far_b = in_pair(far_ab)
     part = call(
         stats_kernel,
         jax.ShapeDtypeStruct((2, SPANS * n), F32),
@@ -225,6 +224,7 @@
         4 * SPANS * n * n * width,
         part, own, core, x, corex, b2, seen, remote=(6,),
     )
+    far_b = in_pair(after(far_ab, send))
     got = lax.all_to_all(send, AXES, 0, 0, tiled=True)
     row = jax.ShapeDtypeStruct((n,), F32)
     both = jax.ShapeDtypeStruct((2, n, width), F32)

time: 51.6 us -> 50.9 us (0.986)
  starting transfers between devices: 26.1 us -> 24 us
  waiting for transfers between devices: 16.7 us -> 18.2 us
    all_to_all x1, starting transfers between devices: 4.1 us -> 2.96 us  [body(): got = lax.all_to_all(send, AXES, 0, 0, tiled=True)]
    ppermute x13, starting transfers between devices: 22 us -> 21 us  [moved(): return lax.ppermute(value, AXES, pairs)]
    all_to_all x1, waiting for transfers between devices: 6.34 us -> 7.32 us  [body(): got = lax.all_to_all(send, AXES, 0, 0, tiled=True)]
  transfers between devices with their start and end apart: 14 -> 14, of which waited for: 7 -> 6; matrix products, arithmetic and copies ran while one was open for 0% -> 0% of each run, Pallas kernels for 5% -> 5%
where the time goes in v8:
time: 50.9 us; the launch traced here: 50.7 us
  starting transfers between devices  24 us (47%)
  waiting for transfers between devices  18.2 us (36%)
  Pallas kernels  6.65 us (13%)
  other arithmetic  1.09 us (2%)
  between operations  0.76 us (1%)
    ppermute x13, starting transfers between devices, moved(): return lax.ppermute(value, AXES, pairs)  21 us
    ppermute x13, waiting for transfers between devices, moved(): return lax.ppermute(value, AXES, pairs)  10.8 us
    all_to_all x1, waiting for transfers between devices, body(): got = lax.all_to_all(send, AXES, 0, 0, tiled=True)  7.32 us
    pallas_call x5, Pallas kernels, call(): pl.pallas_call(kernel, out_shape=out_shape, in_specs=[pl.BlockSpec(memory...  6.65 us
    all_to_all x1, starting transfers between devices, body(): got = lax.all_to_all(send, AXES, 0, 0, tiled=True)  2.96 us
    convert_element_type x2, other arithmetic, body(): i0, t0 = (image_embeds.astype(BF16), text_embeds.astype(BF16))  1.09 us
  transfers between devices with their start and end apart: 14, of which 6 were waited for; matrix products, arithmetic and copies ran while one was open for 0% of the time, Pallas kernels for 5%

profile of v8, /device:TPU:0, one launch (start us, length us, event | category | flops | bytes accessed | tf_op | source)
XLA Modules:
  0.0 50.7 jit_solution(11557752340835672862)
XLA Ops:
  0.6 1.1 %convert_element_type.6.text = bf16[128,768]{1,0:T(8,128)(2,1)S(1)} convert(f32[128,768]{1,0:T(8,128)} %param.3) | non-fusion elementwise | flops 98304 | bytes 589824 | tf_op jit(solution)/shard_map/convert_element_type | solution.py:199
  1.7 3.1 %collective-permute-start = (bf16[128,768]{1,0:T(8,128)(2,1)S(1)}, bf16[128,768]{1,0:T(8,128)(2,1)S(1)}, u32[]{:S(2)}, u32[]{:S(2)}) collective-permute-start(bf16[128,768]{1,0:T(8,128)(2,1)S(1)} %convert_element_type.6.text), channel_id=1, source_target_pairs={{0,8},{1,9},{2,10},{3,11},{4,12},{5,13},{6,14},{7,15},{8,16},{9,17... | collective-permute-start | bytes 589832 | tf_op jit(solution)/shard_map/ppermute | solution.py:25
  4.8 2.1 %collective-permute-start.1 = (bf16[128,768]{1,0:T(8,128)(2,1)S(1)}, bf16[128,768]{1,0:T(8,128)(2,1)S(1)}, u32[]{:S(2)}, u32[]{:S(2)}) collective-permute-start(bf16[128,768]{1,0:T(8,128)(2,1)S(1)} %convert_element_type.7.image), channel_id=1, source_target_pairs={{0,24},{1,25},{2,26},{3,27},{4,28},{5,29},{6,30},{7,31},{8,0},{9,1... | collective-permute-start | bytes 589832 | tf_op jit(solution)/shard_map/ppermute | solution.py:25
  7.0 1.8 %collective-permute-start.4 = (bf16[256,768]{1,0:T(8,128)(2,1)S(1)}, bf16[256,768]{1,0:T(8,128)(2,1)S(1)}, u32[]{:S(2)}, u32[]{:S(2)}) collective-permute-start(bf16[256,768]{1,0:T(8,128)(2,1)S(1)} %get-tuple-element.16.own.refs_1_), channel_id=1, source_target_pairs={{0,2},{1,3},{2,0},{3,1},{4,6},{5,7},{6,4},{7,5},{8,10},{9,11},{10,... | collective-permute-start | bytes 1179656 | tf_op jit(solution)/shard_map/ppermute | solution.py:25
  8.7 1.5 %collective-permute-start.6 = (bf16[128,768]{1,0:T(8,128)(2,1)S(1)}, bf16[128,768]{1,0:T(8,128)(2,1)S(1)}, u32[]{:S(2)}, u32[]{:S(2)}) collective-permute-start(bf16[128,768]{1,0:T(8,128)(2,1)S(1)} %get-tuple-element.17), channel_id=1, source_target_pairs={{0,4},{1,5},{2,6},{3,7},{4,0},{5,1},{6,2},{7,3},{8,12},{9,13},{10,... | collective-permute-start | bytes 589832 | tf_op jit(solution)/shard_map/ppermute | solution.py:25
  10.3 2.3 %collective-permute-done = bf16[128,768]{1,0:T(8,128)(2,1)S(1)} collective-permute-done((bf16[128,768]{1,0:T(8,128)(2,1)S(1)}, bf16[128,768]{1,0:T(8,128)(2,1)S(1)}, u32[]{:S(2)}, u32[]{:S(2)}) %collective-permute-start) | collective-permute-done | bytes 196640 | tf_op jit(solution)/shard_map/ppermute | solution.py:25
  12.6 7.1 %collective-permute-start.7 = (bf16[128,768]{1,0:T(8,128)(2,1)S(1)}, bf16[128,768]{1,0:T(8,128)(2,1)S(1)}, u32[]{:S(2)}, u32[]{:S(2)}) collective-permute-start(bf16[128,768]{1,0:T(8,128)(2,1)S(1)} %get-tuple-element.18), channel_id=1, source_target_pairs={{0,20},{1,21},{2,22},{3,23},{4,16},{5,17},{6,18},{7,19},{8,28},{9,... | collective-permute-start | bytes 589832 | tf_op jit(solution)/shard_map/ppermute | solution.py:25
  19.8 0.1 collective-permute-start.8
  19.9 2.0 %collective-permute-start.2 = (bf16[256,768]{1,0:T(8,128)(2,1)S(1)}, bf16[256,768]{1,0:T(8,128)(2,1)S(1)}, u32[]{:S(2)}, u32[]{:S(2)}) collective-permute-start(bf16[256,768]{1,0:T(8,128)(2,1)S(1)} %constant_dynamic-update-slice_fusion.ab.refs_4_), channel_id=1, source_target_pairs={{0,2},{1,3},{2,0},{3,1},{4,6},{5,7},{6,4},{7,5},{8,10},{9,11},{10,... | collective-permute-start | bytes 1179656 | tf_op jit(solution)/shard_map/ppermute | solution.py:25
  21.9 0.1 collective-permute-start.5
  21.9 3.5 %collective-permute-done.7 = bf16[128,768]{1,0:T(8,128)(2,1)S(1)} collective-permute-done((bf16[128,768]{1,0:T(8,128)(2,1)S(1)}, bf16[128,768]{1,0:T(8,128)(2,1)S(1)}, u32[]{:S(2)}, u32[]{:S(2)}) %collective-permute-start.7) | collective-permute-done | bytes 196640 | tf_op jit(solution)/shard_map/ppermute | solution.py:25
  25.4 0.1 collective-permute-start.9
  25.5 1.6 %collective-permute-start.11 = (bf16[256,768]{1,0:T(8,128)(2,1)S(1)}, bf16[256,768]{1,0:T(8,128)(2,1)S(1)}, u32[]{:S(2)}, u32[]{:S(2)}) collective-permute-start(bf16[256,768]{1,0:T(8,128)(2,1)S(1)} %constant_dynamic-update-slice_fusion.2.pc.refs_6_), channel_id=1, source_target_pairs={{0,2},{1,3},{2,0},{3,1},{4,6},{5,7},{6,4},{7,5},{8,10},{9,11},{10,... | collective-permute-start | bytes 1179656 | tf_op jit(solution)/shard_map/ppermute | solution.py:25
  27.1 1.1 %shard_map.58.part = f32[2,512]{1,0:T(2,128)S(1)} custom-call(bf16[256,768]{1,0:T(8,128)(2,1)S(1)} %get-tuple-element.16.own.refs_1_, bf16[256,768]{1,0:T(8,128)(2,1)S(1)} %collective-permute-done.3.core.refs_2_, bf16[256,768]{1,0:T(8,128)(2,1)S(1)} %collective-permute-done.4.x.refs_3_, bf16[256,768]{1,0:T(8,128)(2,1)S(1)} %collective-permute-done.5.corex, ...), custom_call_target="tpu_custom_call" | custom-call | flops 603979776 | bytes 2359296 | tf_op jit(solution)/shard_map/pallas_call | solution.py:59
  28.2 2.0 %collective-permute-done.8.b2.refs_5_ = bf16[256,768]{1,0:T(8,128)(2,1)S(1)} collective-permute-done((bf16[256,768]{1,0:T(8,128)(2,1)S(1)}, bf16[256,768]{1,0:T(8,128)(2,1)S(1)}, u32[]{:S(2)}, u32[]{:S(2)}) %collective-permute-start.8) | collective-permute-done | bytes 393248 | tf_op jit(solution)/shard_map/ppermute | solution.py:25
  30.2 1.5 %shard_map.59 = f32[32,8,128]{2,1,0:T(8,128)} custom-call(f32[2,512]{1,0:T(2,128)S(1)} %shard_map.58.part, bf16[256,768]{1,0:T(8,128)(2,1)S(1)} %get-tuple-element.16.own.refs_1_, bf16[256,768]{1,0:T(8,128)(2,1)S(1)} %collective-permute-done.3.core.refs_2_, bf16[256,768]{1,0:T(8,128)(2,1)S(1)} %collective-permute-done.4.x.refs_3_, ...), custom_call_target="tpu_custom_call" | custom-call | flops 201326592 | bytes 2363392 | tf_op jit(solution)/shard_map/pallas_call | solution.py:59
  31.8 1.4 %collective-permute-start.10 = (bf16[256,768]{1,0:T(8,128)(2,1)S(1)}, bf16[256,768]{1,0:T(8,128)(2,1)}, u32[]{:S(2)}, u32[]{:S(2)}) collective-permute-start(bf16[256,768]{1,0:T(8,128)(2,1)S(1)} %collective-permute-done.2.refs_7_), channel_id=1, source_target_pairs={{0,4},{1,5},{2,6},{3,7},{4,0},{5,1},{6,2},{7,3},{8,12},{9,13},{10,... | collective-permute-start | bytes 1179656 | tf_op jit(solution)/shard_map/ppermute | solution.py:25
  33.2 3.0 %all-to-all-start = ((f32[32,8,128]{2,1,0:T(8,128)}), f32[32,8,128]{2,1,0:T(8,128)S(1)}, u32[]{:S(2)}, u32[]{:S(2)}) async-start(f32[32,8,128]{2,1,0:T(8,128)} %shard_map.59), calls=%async_computation | async-start | bytes 262144 | tf_op jit(solution)/shard_map/all_to_all | solution.py:228
  36.1 0.9 %collective-permute-done.11.refs_9_ = bf16[256,768]{1,0:T(8,128)(2,1)S(1)} collective-permute-done((bf16[256,768]{1,0:T(8,128)(2,1)S(1)}, bf16[256,768]{1,0:T(8,128)(2,1)S(1)}, u32[]{:S(2)}, u32[]{:S(2)}) %collective-permute-start.11) | collective-permute-done | bytes 393248 | tf_op jit(solution)/shard_map/ppermute | solution.py:25
  37.0 7.3 %all-to-all-done.refs_0_ = f32[32,8,128]{2,1,0:T(8,128)S(1)} async-done(((f32[32,8,128]{2,1,0:T(8,128)}), f32[32,8,128]{2,1,0:T(8,128)S(1)}, u32[]{:S(2)}, u32[]{:S(2)}) %all-to-all-start) | async-done | bytes 131104 | tf_op jit(solution)/shard_map/all_to_all | solution.py:228
  44.4 3.0 %shard_map.60 = (f32[128]{0:T(128)}, f32[128]{0:T(128)}, f32[2,128,768]{2,1,0:T(8,128)S(1)}, f32[2,128,768]{2,1,0:T(8,128)S(1)}) custom-call(f32[32,8,128]{2,1,0:T(8,128)S(1)} %all-to-all-done.refs_0_, bf16[256,768]{1,0:T(8,128)(2,1)S(1)} %get-tuple-element.16.own.refs_1_, bf16[256,768]{1,0:T(8,128)(2,1)S(1)} %collective-permute-done.3.core.refs_2_, ...), custom_call_target="tpu_custom_call" | custom-call | flops 1610612736 | bytes 3670016 | tf_op jit(solution)/shard_map/pallas_call | solution.py:59
  47.4 0.3 collective-permute-start.12
  47.6 2.1 %collective-permute-done.12.got = f32[2,128,768]{2,1,0:T(8,128)S(1)} collective-permute-done((f32[2,128,768]{2,1,0:T(8,128)S(1)}, f32[2,128,768]{2,1,0:T(8,128)S(1)}, u32[]{:S(2)}, u32[]{:S(2)}) %collective-permute-start.12) | collective-permute-done | bytes 786464 | tf_op jit(solution)/shard_map/ppermute | solution.py:25
  49.7 1.0 %shard_map.61 = (f32[128,768]{1,0:T(8,128)}, f32[128,768]{1,0:T(8,128)}) custom-call(f32[2,128,768]{2,1,0:T(8,128)S(1)} %get-tuple-element.24.kept, f32[2,128,768]{2,1,0:T(8,128)S(1)} %collective-permute-done.12.got), custom_call_target="tpu_custom_call" | custom-call | bytes 1572864 | tf_op jit(solution)/shard_map/pallas_call | solution.py:59
  (17 shorter events, 0.2 us)
Async XLA Ops:
  0.6 4.2 %copy-start = (f32[128,768]{1,0:T(8,128)S(1)}, f32[128,768]{1,0:T(8,128)}, u32[]{:S(2)}) copy-start(f32[128,768]{1,0:T(8,128)} %param.2) | copy-start | bytes 1179652
  1.7 10.9 %collective-permute-start = (bf16[128,768]{1,0:T(8,128)(2,1)S(1)}, bf16[128,768]{1,0:T(8,128)(2,1)S(1)}, u32[]{:S(2)}, u32[]{:S(2)}) collective-permute-start(bf16[128,768]{1,0:T(8,128)(2,1)S(1)} %convert_element_type.6.text), channel_id=1, source_target_pairs={{0,8},{1,9},{2,10},{3,11},{4,12},{5,13},{6,14},{7,15},{8,16},{9,17... | collective-permute-start | bytes 589832 | tf_op jit(solution)/shard_map/ppermute | solution.py:25
  4.8 14.9 %collective-permute-start.1 = (bf16[128,768]{1,0:T(8,128)(2,1)S(1)}, bf16[128,768]{1,0:T(8,128)(2,1)S(1)}, u32[]{:S(2)}, u32[]{:S(2)}) collective-permute-start(bf16[128,768]{1,0:T(8,128)(2,1)S(1)} %convert_element_type.7.image), channel_id=1, source_target_pairs={{0,24},{1,25},{2,26},{3,27},{4,28},{5,29},{6,30},{7,31},{8,0},{9,1... | collective-permute-start | bytes 589832 | tf_op jit(solution)/shard_map/ppermute | solution.py:25
  7.0 14.9 %collective-permute-start.4 = (bf16[256,768]{1,0:T(8,128)(2,1)S(1)}, bf16[256,768]{1,0:T(8,128)(2,1)S(1)}, u32[]{:S(2)}, u32[]{:S(2)}) collective-permute-start(bf16[256,768]{1,0:T(8,128)(2,1)S(1)} %get-tuple-element.16.own.refs_1_), channel_id=1, source_target_pairs={{0,2},{1,3},{2,0},{3,1},{4,6},{5,7},{6,4},{7,5},{8,10},{9,11},{10,... | collective-permute-start | bytes 1179656 | tf_op jit(solution)/shard_map/ppermute | solution.py:25
  8.7 16.8 %collective-permute-start.3 = (bf16[256,768]{1,0:T(8,128)(2,1)S(1)}, bf16[256,768]{1,0:T(8,128)(2,1)S(1)}, u32[]{:S(2)}, u32[]{:S(2)}) collective-permute-start(bf16[256,768]{1,0:T(8,128)(2,1)S(1)} %get-tuple-element.16.own.refs_1_), channel_id=1, source_target_pairs={{0,1},{1,0},{2,3},{3,2},{4,5},{5,4},{6,7},{7,6},{8,9},{9,8},{10,11... | collective-permute-start | bytes 1179656 | tf_op jit(solution)/shard_map/ppermute | solution.py:25
  8.7 11.1 %collective-permute-start.6 = (bf16[128,768]{1,0:T(8,128)(2,1)S(1)}, bf16[128,768]{1,0:T(8,128)(2,1)S(1)}, u32[]{:S(2)}, u32[]{:S(2)}) collective-permute-start(bf16[128,768]{1,0:T(8,128)(2,1)S(1)} %get-tuple-element.17), channel_id=1, source_target_pairs={{0,4},{1,5},{2,6},{3,7},{4,0},{5,1},{6,2},{7,3},{8,12},{9,13},{10,... | collective-permute-start | bytes 589832 | tf_op jit(solution)/shard_map/ppermute | solution.py:25
  12.6 12.8 %collective-permute-start.7 = (bf16[128,768]{1,0:T(8,128)(2,1)S(1)}, bf16[128,768]{1,0:T(8,128)(2,1)S(1)}, u32[]{:S(2)}, u32[]{:S(2)}) collective-permute-start(bf16[128,768]{1,0:T(8,128)(2,1)S(1)} %get-tuple-element.18), channel_id=1, source_target_pairs={{0,20},{1,21},{2,22},{3,23},{4,16},{5,17},{6,18},{7,19},{8,28},{9,... | collective-permute-start | bytes 589832 | tf_op jit(solution)/shard_map/ppermute | solution.py:25
  19.8 10.5 %collective-permute-start.8 = (bf16[256,768]{1,0:T(8,128)(2,1)S(1)}, bf16[256,768]{1,0:T(8,128)(2,1)S(1)}, u32[]{:S(2)}, u32[]{:S(2)}) collective-permute-start(bf16[256,768]{1,0:T(8,128)(2,1)S(1)} %constant_dynamic-update-slice_fusion.ab.refs_4_), channel_id=1, source_target_pairs={{0,4},{1,5},{2,6},{3,7},{4,0},{5,1},{6,2},{7,3},{8,12},{9,13},{10,... | collective-permute-start | bytes 1179656 | tf_op jit(solution)/shard_map/ppermute | solution.py:25
  19.9 8.3 %collective-permute-start.2 = (bf16[256,768]{1,0:T(8,128)(2,1)S(1)}, bf16[256,768]{1,0:T(8,128)(2,1)S(1)}, u32[]{:S(2)}, u32[]{:S(2)}) collective-permute-start(bf16[256,768]{1,0:T(8,128)(2,1)S(1)} %constant_dynamic-update-slice_fusion.ab.refs_4_), channel_id=1, source_target_pairs={{0,2},{1,3},{2,0},{3,1},{4,6},{5,7},{6,4},{7,5},{8,10},{9,11},{10,... | collective-permute-start | bytes 1179656 | tf_op jit(solution)/shard_map/ppermute | solution.py:25
  21.9 5.2 %collective-permute-start.5 = (bf16[256,768]{1,0:T(8,128)(2,1)S(1)}, bf16[256,768]{1,0:T(8,128)(2,1)S(1)}, u32[]{:S(2)}, u32[]{:S(2)}) collective-permute-start(bf16[256,768]{1,0:T(8,128)(2,1)S(1)} %collective-permute-done.4.x.refs_3_), channel_id=1, source_target_pairs={{0,1},{1,0},{2,3},{3,2},{4,5},{5,4},{6,7},{7,6},{8,9},{9,8},{10,11... | collective-permute-start | bytes 1179656 | tf_op jit(solution)/shard_map/ppermute | solution.py:25
  25.4 4.8 %collective-permute-start.9 = (bf16[256,768]{1,0:T(8,128)(2,1)S(1)}, bf16[256,768]{1,0:T(8,128)(2,1)S(1)}, u32[]{:S(2)}, u32[]{:S(2)}) collective-permute-start(bf16[256,768]{1,0:T(8,128)(2,1)S(1)} %constant_dynamic-update-slice_fusion.2.pc.refs_6_), channel_id=1, source_target_pairs={{0,1},{1,0},{2,3},{3,2},{4,5},{5,4},{6,7},{7,6},{8,9},{9,8},{10,11... | collective-permute-start | bytes 1179656 | tf_op jit(solution)/shard_map/ppermute | solution.py:25
  25.5 11.5 %collective-permute-start.11 = (bf16[256,768]{1,0:T(8,128)(2,1)S(1)}, bf16[256,768]{1,0:T(8,128)(2,1)S(1)}, u32[]{:S(2)}, u32[]{:S(2)}) collective-permute-start(bf16[256,768]{1,0:T(8,128)(2,1)S(1)} %constant_dynamic-update-slice_fusion.2.pc.refs_6_), channel_id=1, source_target_pairs={{0,2},{1,3},{2,0},{3,1},{4,6},{5,7},{6,4},{7,5},{8,10},{9,11},{10,... | collective-permute-start | bytes 1179656 | tf_op jit(solution)/shard_map/ppermute | solution.py:25
  31.8 12.6 %collective-permute-start.10 = (bf16[256,768]{1,0:T(8,128)(2,1)S(1)}, bf16[256,768]{1,0:T(8,128)(2,1)}, u32[]{:S(2)}, u32[]{:S(2)}) collective-permute-start(bf16[256,768]{1,0:T(8,128)(2,1)S(1)} %collective-permute-done.2.refs_7_), channel_id=1, source_target_pairs={{0,4},{1,5},{2,6},{3,7},{4,0},{5,1},{6,2},{7,3},{8,12},{9,13},{10,... | collective-permute-start | bytes 1179656 | tf_op jit(solution)/shard_map/ppermute | solution.py:25
  33.2 11.2 %all-to-all-start = ((f32[32,8,128]{2,1,0:T(8,128)}), f32[32,8,128]{2,1,0:T(8,128)S(1)}, u32[]{:S(2)}, u32[]{:S(2)}) async-start(f32[32,8,128]{2,1,0:T(8,128)} %shard_map.59), calls=%async_computation | async-start | bytes 262144 | tf_op jit(solution)/shard_map/all_to_all | solution.py:228
  47.4 2.4 %collective-permute-start.12 = (f32[2,128,768]{2,1,0:T(8,128)S(1)}, f32[2,128,768]{2,1,0:T(8,128)S(1)}, u32[]{:S(2)}, u32[]{:S(2)}) collective-permute-start(f32[2,128,768]{2,1,0:T(8,128)S(1)} %get-tuple-element.25), channel_id=1, source_target_pairs={{0,1},{1,0},{2,3},{3,2},{4,5},{5,4},{6,7},{7,6},{8,9},{9,8},{10,11... | collective-permute-start | bytes 2359304 | tf_op jit(solution)/shard_map/ppermute | solution.py:25

commit v9 on v8

--- a/solution.py
+++ b/solution.py
@@ -183,12 +183,12 @@
             weights[side], cols[side].reshape(STEPS * 2 * n, cols.shape[-1]), preferred_element_type=F32
         )
         kept[side] = total[:n]
-        sent[side] = total[n:]
+        sent[side] = total[n:].astype(BF16)
 
 
 def add_kernel(kept, got, image_grad, text_grad):
-    image_grad[...] = kept[0] + got[0]
-    text_grad[...] = kept[1] + got[1]
+    image_grad[...] = kept[0] + got[0].astype(F32)
+    text_grad[...] = kept[1] + got[1].astype(F32)
 
 
 def body(image_embeds, text_embeds):
@@ -230,7 +230,7 @@
     both = jax.ShapeDtypeStruct((2, n, width), F32)
     image_lse, text_lse, kept, sent = call(
         functools.partial(grad_kernel, count),
-        (row, row, both, both),
+        (row, row, both, jax.ShapeDtypeStruct((2, n, width), BF16)),
         [
             pltpu.VMEM((2, 2 * n, width), BF16),
             pltpu.VMEM((2, STEPS, 2 * n, width), BF16),

time: 50.9 us -> 50.3 us (0.988)
  waiting for transfers between devices: 18.2 us -> 17.6 us
    ppermute x13, waiting for transfers between devices: 10.8 us -> 10.3 us  [moved(): return lax.ppermute(value, AXES, pairs)]
where the time goes in v9:
time: 50.3 us; the launch traced here: 50.1 us
  starting transfers between devices  24 us (48%)
  waiting for transfers between devices  17.6 us (35%)
  Pallas kernels  6.63 us (13%)
  other arithmetic  1.09 us (2%)
  between operations  0.76 us (2%)
    ppermute x13, starting transfers between devices, moved(): return lax.ppermute(value, AXES, pairs)  21 us
    ppermute x13, waiting for transfers between devices, moved(): return lax.ppermute(value, AXES, pairs)  10.3 us
    all_to_all x1, waiting for transfers between devices, body(): got = lax.all_to_all(send, AXES, 0, 0, tiled=True)  7.32 us
    pallas_call x5, Pallas kernels, call(): pl.pallas_call(kernel, out_shape=out_shape, in_specs=[pl.BlockSpec(memory...  6.63 us
    all_to_all x1, starting transfers between devices, body(): got = lax.all_to_all(send, AXES, 0, 0, tiled=True)  2.96 us
    convert_element_type x2, other arithmetic, body(): i0, t0 = (image_embeds.astype(BF16), text_embeds.astype(BF16))  1.09 us
  transfers between devices with their start and end apart: 14, of which 6 were waited for; matrix products, arithmetic and copies ran while one was open for 0% of the time, Pallas kernels for 5%

profile of v9, /device:TPU:0, one launch (start us, length us, event | category | flops | bytes accessed | tf_op | source)
XLA Modules:
  0.0 50.1 jit_solution(7079528232693143144)
XLA Ops:
  0.6 1.1 %convert_element_type.6.text = bf16[128,768]{1,0:T(8,128)(2,1)S(1)} convert(f32[128,768]{1,0:T(8,128)} %param.3) | non-fusion elementwise | flops 98304 | bytes 589824 | tf_op jit(solution)/shard_map/convert_element_type | solution.py:199
  1.7 3.1 %collective-permute-start = (bf16[128,768]{1,0:T(8,128)(2,1)S(1)}, bf16[128,768]{1,0:T(8,128)(2,1)S(1)}, u32[]{:S(2)}, u32[]{:S(2)}) collective-permute-start(bf16[128,768]{1,0:T(8,128)(2,1)S(1)} %convert_element_type.6.text), channel_id=1, source_target_pairs={{0,8},{1,9},{2,10},{3,11},{4,12},{5,13},{6,14},{7,15},{8,16},{9,17... | collective-permute-start | bytes 589832 | tf_op jit(solution)/shard_map/ppermute | solution.py:25
  4.8 2.1 %collective-permute-start.1 = (bf16[128,768]{1,0:T(8,128)(2,1)S(1)}, bf16[128,768]{1,0:T(8,128)(2,1)S(1)}, u32[]{:S(2)}, u32[]{:S(2)}) collective-permute-start(bf16[128,768]{1,0:T(8,128)(2,1)S(1)} %convert_element_type.7.image), channel_id=1, source_target_pairs={{0,24},{1,25},{2,26},{3,27},{4,28},{5,29},{6,30},{7,31},{8,0},{9,1... | collective-permute-start | bytes 589832 | tf_op jit(solution)/shard_map/ppermute | solution.py:25
  7.0 1.8 %collective-permute-start.4 = (bf16[256,768]{1,0:T(8,128)(2,1)S(1)}, bf16[256,768]{1,0:T(8,128)(2,1)S(1)}, u32[]{:S(2)}, u32[]{:S(2)}) collective-permute-start(bf16[256,768]{1,0:T(8,128)(2,1)S(1)} %get-tuple-element.16.own.refs_1_), channel_id=1, source_target_pairs={{0,2},{1,3},{2,0},{3,1},{4,6},{5,7},{6,4},{7,5},{8,10},{9,11},{10,... | collective-permute-start | bytes 1179656 | tf_op jit(solution)/shard_map/ppermute | solution.py:25
  8.7 1.5 %collective-permute-start.6 = (bf16[128,768]{1,0:T(8,128)(2,1)S(1)}, bf16[128,768]{1,0:T(8,128)(2,1)S(1)}, u32[]{:S(2)}, u32[]{:S(2)}) collective-permute-start(bf16[128,768]{1,0:T(8,128)(2,1)S(1)} %get-tuple-element.17), channel_id=1, source_target_pairs={{0,4},{1,5},{2,6},{3,7},{4,0},{5,1},{6,2},{7,3},{8,12},{9,13},{10,... | collective-permute-start | bytes 589832 | tf_op jit(solution)/shard_map/ppermute | solution.py:25
  10.3 2.3 %collective-permute-done = bf16[128,768]{1,0:T(8,128)(2,1)S(1)} collective-permute-done((bf16[128,768]{1,0:T(8,128)(2,1)S(1)}, bf16[128,768]{1,0:T(8,128)(2,1)S(1)}, u32[]{:S(2)}, u32[]{:S(2)}) %collective-permute-start) | collective-permute-done | bytes 196640 | tf_op jit(solution)/shard_map/ppermute | solution.py:25
  12.6 7.1 %collective-permute-start.7 = (bf16[128,768]{1,0:T(8,128)(2,1)S(1)}, bf16[128,768]{1,0:T(8,128)(2,1)S(1)}, u32[]{:S(2)}, u32[]{:S(2)}) collective-permute-start(bf16[128,768]{1,0:T(8,128)(2,1)S(1)} %get-tuple-element.18), channel_id=1, source_target_pairs={{0,20},{1,21},{2,22},{3,23},{4,16},{5,17},{6,18},{7,19},{8,28},{9,... | collective-permute-start | bytes 589832 | tf_op jit(solution)/shard_map/ppermute | solution.py:25
  19.8 0.1 collective-permute-start.8
  19.9 2.0 %collective-permute-start.2 = (bf16[256,768]{1,0:T(8,128)(2,1)S(1)}, bf16[256,768]{1,0:T(8,128)(2,1)S(1)}, u32[]{:S(2)}, u32[]{:S(2)}) collective-permute-start(bf16[256,768]{1,0:T(8,128)(2,1)S(1)} %constant_dynamic-update-slice_fusion.ab.refs_4_), channel_id=1, source_target_pairs={{0,2},{1,3},{2,0},{3,1},{4,6},{5,7},{6,4},{7,5},{8,10},{9,11},{10,... | collective-permute-start | bytes 1179656 | tf_op jit(solution)/shard_map/ppermute | solution.py:25
  21.9 0.1 collective-permute-start.5
  21.9 3.5 %collective-permute-done.7 = bf16[128,768]{1,0:T(8,128)(2,1)S(1)} collective-permute-done((bf16[128,768]{1,0:T(8,128)(2,1)S(1)}, bf16[128,768]{1,0:T(8,128)(2,1)S(1)}, u32[]{:S(2)}, u32[]{:S(2)}) %collective-permute-start.7) | collective-permute-done | bytes 196640 | tf_op jit(solution)/shard_map/ppermute | solution.py:25
  25.4 0.1 collective-permute-start.9
  25.5 1.6 %collective-permute-start.11 = (bf16[256,768]{1,0:T(8,128)(2,1)S(1)}, bf16[256,768]{1,0:T(8,128)(2,1)S(1)}, u32[]{:S(2)}, u32[]{:S(2)}) collective-permute-start(bf16[256,768]{1,0:T(8,128)(2,1)S(1)} %constant_dynamic-update-slice_fusion.2.pc.refs_6_), channel_id=1, source_target_pairs={{0,2},{1,3},{2,0},{3,1},{4,6},{5,7},{6,4},{7,5},{8,10},{9,11},{10,... | collective-permute-start | bytes 1179656 | tf_op jit(solution)/shard_map/ppermute | solution.py:25
  27.1 1.1 %shard_map.58.part = f32[2,512]{1,0:T(2,128)S(1)} custom-call(bf16[256,768]{1,0:T(8,128)(2,1)S(1)} %get-tuple-element.16.own.refs_1_, bf16[256,768]{1,0:T(8,128)(2,1)S(1)} %collective-permute-done.3.core.refs_2_, bf16[256,768]{1,0:T(8,128)(2,1)S(1)} %collective-permute-done.4.x.refs_3_, bf16[256,768]{1,0:T(8,128)(2,1)S(1)} %collective-permute-done.5.corex, ...), custom_call_target="tpu_custom_call" | custom-call | flops 603979776 | bytes 2359296 | tf_op jit(solution)/shard_map/pallas_call | solution.py:59
  28.2 2.0 %collective-permute-done.8.b2.refs_5_ = bf16[256,768]{1,0:T(8,128)(2,1)S(1)} collective-permute-done((bf16[256,768]{1,0:T(8,128)(2,1)S(1)}, bf16[256,768]{1,0:T(8,128)(2,1)S(1)}, u32[]{:S(2)}, u32[]{:S(2)}) %collective-permute-start.8) | collective-permute-done | bytes 393248 | tf_op jit(solution)/shard_map/ppermute | solution.py:25
  30.2 1.5 %shard_map.59 = f32[32,8,128]{2,1,0:T(8,128)} custom-call(f32[2,512]{1,0:T(2,128)S(1)} %shard_map.58.part, bf16[256,768]{1,0:T(8,128)(2,1)S(1)} %get-tuple-element.16.own.refs_1_, bf16[256,768]{1,0:T(8,128)(2,1)S(1)} %collective-permute-done.3.core.refs_2_, bf16[256,768]{1,0:T(8,128)(2,1)S(1)} %collective-permute-done.4.x.refs_3_, ...), custom_call_target="tpu_custom_call" | custom-call | flops 201326592 | bytes 2363392 | tf_op jit(solution)/shard_map/pallas_call | solution.py:59
  31.8 1.4 %collective-permute-start.10 = (bf16[256,768]{1,0:T(8,128)(2,1)S(1)}, bf16[256,768]{1,0:T(8,128)(2,1)}, u32[]{:S(2)}, u32[]{:S(2)}) collective-permute-start(bf16[256,768]{1,0:T(8,128)(2,1)S(1)} %collective-permute-done.2.refs_7_), channel_id=1, source_target_pairs={{0,4},{1,5},{2,6},{3,7},{4,0},{5,1},{6,2},{7,3},{8,12},{9,13},{10,... | collective-permute-start | bytes 1179656 | tf_op jit(solution)/shard_map/ppermute | solution.py:25
  33.2 3.0 %all-to-all-start = ((f32[32,8,128]{2,1,0:T(8,128)}), f32[32,8,128]{2,1,0:T(8,128)S(1)}, u32[]{:S(2)}, u32[]{:S(2)}) async-start(f32[32,8,128]{2,1,0:T(8,128)} %shard_map.59), calls=%async_computation | async-start | bytes 262144 | tf_op jit(solution)/shard_map/all_to_all | solution.py:228
  36.1 0.9 %collective-permute-done.11.refs_9_ = bf16[256,768]{1,0:T(8,128)(2,1)S(1)} collective-permute-done((bf16[256,768]{1,0:T(8,128)(2,1)S(1)}, bf16[256,768]{1,0:T(8,128)(2,1)S(1)}, u32[]{:S(2)}, u32[]{:S(2)}) %collective-permute-start.11) | collective-permute-done | bytes 393248 | tf_op jit(solution)/shard_map/ppermute | solution.py:25
  37.0 7.3 %all-to-all-done.refs_0_ = f32[32,8,128]{2,1,0:T(8,128)S(1)} async-done(((f32[32,8,128]{2,1,0:T(8,128)}), f32[32,8,128]{2,1,0:T(8,128)S(1)}, u32[]{:S(2)}, u32[]{:S(2)}) %all-to-all-start) | async-done | bytes 131104 | tf_op jit(solution)/shard_map/all_to_all | solution.py:228
  44.4 3.0 %shard_map.60 = (f32[128]{0:T(128)}, f32[128]{0:T(128)}, f32[2,128,768]{2,1,0:T(8,128)S(1)}, bf16[2,128,768]{2,1,0:T(8,128)(2,1)S(1)}) custom-call(f32[32,8,128]{2,1,0:T(8,128)S(1)} %all-to-all-done.refs_0_, bf16[256,768]{1,0:T(8,128)(2,1)S(1)} %get-tuple-element.16.own.refs_1_, bf16[256,768]{1,0:T(8,128)(2,1)S(1)} %collective-permute-done.3.core.refs_2_, ...), custom_call_target="tpu_custom_call" | custom-call | flops 1610612736 | bytes 3670016 | tf_op jit(solution)/shard_map/pallas_call | solution.py:59
  47.4 0.3 collective-permute-start.12
  47.6 1.5 %collective-permute-done.12.got = bf16[2,128,768]{2,1,0:T(8,128)(2,1)S(1)} collective-permute-done((bf16[2,128,768]{2,1,0:T(8,128)(2,1)S(1)}, bf16[2,128,768]{2,1,0:T(8,128)(2,1)S(1)}, u32[]{:S(2)}, u32[]{:S(2)}) %collective-permute-start.12) | collective-permute-done | bytes 393248 | tf_op jit(solution)/shard_map/ppermute | solution.py:25
  49.2 0.9 %shard_map.61 = (f32[128,768]{1,0:T(8,128)}, f32[128,768]{1,0:T(8,128)}) custom-call(f32[2,128,768]{2,1,0:T(8,128)S(1)} %get-tuple-element.24.kept, bf16[2,128,768]{2,1,0:T(8,128)(2,1)S(1)} %collective-permute-done.12.got), custom_call_target="tpu_custom_call" | custom-call | bytes 1179648 | tf_op jit(solution)/shard_map/pallas_call | solution.py:59
  (17 shorter events, 0.2 us)
Async XLA Ops:
  0.6 4.2 %copy-start = (f32[128,768]{1,0:T(8,128)S(1)}, f32[128,768]{1,0:T(8,128)}, u32[]{:S(2)}) copy-start(f32[128,768]{1,0:T(8,128)} %param.2) | copy-start | bytes 1179652
  1.7 10.9 %collective-permute-start = (bf16[128,768]{1,0:T(8,128)(2,1)S(1)}, bf16[128,768]{1,0:T(8,128)(2,1)S(1)}, u32[]{:S(2)}, u32[]{:S(2)}) collective-permute-start(bf16[128,768]{1,0:T(8,128)(2,1)S(1)} %convert_element_type.6.text), channel_id=1, source_target_pairs={{0,8},{1,9},{2,10},{3,11},{4,12},{5,13},{6,14},{7,15},{8,16},{9,17... | collective-permute-start | bytes 589832 | tf_op jit(solution)/shard_map/ppermute | solution.py:25
  4.8 14.9 %collective-permute-start.1 = (bf16[128,768]{1,0:T(8,128)(2,1)S(1)}, bf16[128,768]{1,0:T(8,128)(2,1)S(1)}, u32[]{:S(2)}, u32[]{:S(2)}) collective-permute-start(bf16[128,768]{1,0:T(8,128)(2,1)S(1)} %convert_element_type.7.image), channel_id=1, source_target_pairs={{0,24},{1,25},{2,26},{3,27},{4,28},{5,29},{6,30},{7,31},{8,0},{9,1... | collective-permute-start | bytes 589832 | tf_op jit(solution)/shard_map/ppermute | solution.py:25
  7.0 14.9 %collective-permute-start.4 = (bf16[256,768]{1,0:T(8,128)(2,1)S(1)}, bf16[256,768]{1,0:T(8,128)(2,1)S(1)}, u32[]{:S(2)}, u32[]{:S(2)}) collective-permute-start(bf16[256,768]{1,0:T(8,128)(2,1)S(1)} %get-tuple-element.16.own.refs_1_), channel_id=1, source_target_pairs={{0,2},{1,3},{2,0},{3,1},{4,6},{5,7},{6,4},{7,5},{8,10},{9,11},{10,... | collective-permute-start | bytes 1179656 | tf_op jit(solution)/shard_map/ppermute | solution.py:25
  8.7 16.8 %collective-permute-start.3 = (bf16[256,768]{1,0:T(8,128)(2,1)S(1)}, bf16[256,768]{1,0:T(8,128)(2,1)S(1)}, u32[]{:S(2)}, u32[]{:S(2)}) collective-permute-start(bf16[256,768]{1,0:T(8,128)(2,1)S(1)} %get-tuple-element.16.own.refs_1_), channel_id=1, source_target_pairs={{0,1},{1,0},{2,3},{3,2},{4,5},{5,4},{6,7},{7,6},{8,9},{9,8},{10,11... | collective-permute-start | bytes 1179656 | tf_op jit(solution)/shard_map/ppermute | solution.py:25
  8.7 11.1 %collective-permute-start.6 = (bf16[128,768]{1,0:T(8,128)(2,1)S(1)}, bf16[128,768]{1,0:T(8,128)(2,1)S(1)}, u32[]{:S(2)}, u32[]{:S(2)}) collective-permute-start(bf16[128,768]{1,0:T(8,128)(2,1)S(1)} %get-tuple-element.17), channel_id=1, source_target_pairs={{0,4},{1,5},{2,6},{3,7},{4,0},{5,1},{6,2},{7,3},{8,12},{9,13},{10,... | collective-permute-start | bytes 589832 | tf_op jit(solution)/shard_map/ppermute | solution.py:25
  12.6 12.8 %collective-permute-start.7 = (bf16[128,768]{1,0:T(8,128)(2,1)S(1)}, bf16[128,768]{1,0:T(8,128)(2,1)S(1)}, u32[]{:S(2)}, u32[]{:S(2)}) collective-permute-start(bf16[128,768]{1,0:T(8,128)(2,1)S(1)} %get-tuple-element.18), channel_id=1, source_target_pairs={{0,20},{1,21},{2,22},{3,23},{4,16},{5,17},{6,18},{7,19},{8,28},{9,... | collective-permute-start | bytes 589832 | tf_op jit(solution)/shard_map/ppermute | solution.py:25
  19.8 10.5 %collective-permute-start.8 = (bf16[256,768]{1,0:T(8,128)(2,1)S(1)}, bf16[256,768]{1,0:T(8,128)(2,1)S(1)}, u32[]{:S(2)}, u32[]{:S(2)}) collective-permute-start(bf16[256,768]{1,0:T(8,128)(2,1)S(1)} %constant_dynamic-update-slice_fusion.ab.refs_4_), channel_id=1, source_target_pairs={{0,4},{1,5},{2,6},{3,7},{4,0},{5,1},{6,2},{7,3},{8,12},{9,13},{10,... | collective-permute-start | bytes 1179656 | tf_op jit(solution)/shard_map/ppermute | solution.py:25
  19.9 8.3 %collective-permute-start.2 = (bf16[256,768]{1,0:T(8,128)(2,1)S(1)}, bf16[256,768]{1,0:T(8,128)(2,1)S(1)}, u32[]{:S(2)}, u32[]{:S(2)}) collective-permute-start(bf16[256,768]{1,0:T(8,128)(2,1)S(1)} %constant_dynamic-update-slice_fusion.ab.refs_4_), channel_id=1, source_target_pairs={{0,2},{1,3},{2,0},{3,1},{4,6},{5,7},{6,4},{7,5},{8,10},{9,11},{10,... | collective-permute-start | bytes 1179656 | tf_op jit(solution)/shard_map/ppermute | solution.py:25
  21.9 5.2 %collective-permute-start.5 = (bf16[256,768]{1,0:T(8,128)(2,1)S(1)}, bf16[256,768]{1,0:T(8,128)(2,1)S(1)}, u32[]{:S(2)}, u32[]{:S(2)}) collective-permute-start(bf16[256,768]{1,0:T(8,128)(2,1)S(1)} %collective-permute-done.4.x.refs_3_), channel_id=1, source_target_pairs={{0,1},{1,0},{2,3},{3,2},{4,5},{5,4},{6,7},{7,6},{8,9},{9,8},{10,11... | collective-permute-start | bytes 1179656 | tf_op jit(solution)/shard_map/ppermute | solution.py:25
  25.4 4.8 %collective-permute-start.9 = (bf16[256,768]{1,0:T(8,128)(2,1)S(1)}, bf16[256,768]{1,0:T(8,128)(2,1)S(1)}, u32[]{:S(2)}, u32[]{:S(2)}) collective-permute-start(bf16[256,768]{1,0:T(8,128)(2,1)S(1)} %constant_dynamic-update-slice_fusion.2.pc.refs_6_), channel_id=1, source_target_pairs={{0,1},{1,0},{2,3},{3,2},{4,5},{5,4},{6,7},{7,6},{8,9},{9,8},{10,11... | collective-permute-start | bytes 1179656 | tf_op jit(solution)/shard_map/ppermute | solution.py:25
  25.5 11.5 %collective-permute-start.11 = (bf16[256,768]{1,0:T(8,128)(2,1)S(1)}, bf16[256,768]{1,0:T(8,128)(2,1)S(1)}, u32[]{:S(2)}, u32[]{:S(2)}) collective-permute-start(bf16[256,768]{1,0:T(8,128)(2,1)S(1)} %constant_dynamic-update-slice_fusion.2.pc.refs_6_), channel_id=1, source_target_pairs={{0,2},{1,3},{2,0},{3,1},{4,6},{5,7},{6,4},{7,5},{8,10},{9,11},{10,... | collective-permute-start | bytes 1179656 | tf_op jit(solution)/shard_map/ppermute | solution.py:25
  31.8 12.6 %collective-permute-start.10 = (bf16[256,768]{1,0:T(8,128)(2,1)S(1)}, bf16[256,768]{1,0:T(8,128)(2,1)}, u32[]{:S(2)}, u32[]{:S(2)}) collective-permute-start(bf16[256,768]{1,0:T(8,128)(2,1)S(1)} %collective-permute-done.2.refs_7_), channel_id=1, source_target_pairs={{0,4},{1,5},{2,6},{3,7},{4,0},{5,1},{6,2},{7,3},{8,12},{9,13},{10,... | collective-permute-start | bytes 1179656 | tf_op jit(solution)/shard_map/ppermute | solution.py:25
  33.2 11.2 %all-to-all-start = ((f32[32,8,128]{2,1,0:T(8,128)}), f32[32,8,128]{2,1,0:T(8,128)S(1)}, u32[]{:S(2)}, u32[]{:S(2)}) async-start(f32[32,8,128]{2,1,0:T(8,128)} %shard_map.59), calls=%async_computation | async-start | bytes 262144 | tf_op jit(solution)/shard_map/all_to_all | solution.py:228
  47.4 1.8 %collective-permute-start.12 = (bf16[2,128,768]{2,1,0:T(8,128)(2,1)S(1)}, bf16[2,128,768]{2,1,0:T(8,128)(2,1)S(1)}, u32[]{:S(2)}, u32[]{:S(2)}) collective-permute-start(bf16[2,128,768]{2,1,0:T(8,128)(2,1)S(1)} %get-tuple-element.25), channel_id=1, source_target_pairs={{0,1},{1,0},{2,3},{3,2},{4,5},{5,4},{6,7},{7,6},{8,9},{9,8},{10,11... | collective-permute-start | bytes 1179656 | tf_op jit(solution)/shard_map/ppermute | solution.py:25

commit v10 on v9

--- a/solution.py
+++ b/solution.py
@@ -111,14 +111,14 @@
         part[side] = (top + jnp.log(jnp.sum(jnp.exp(s - top), axis=0, keepdims=True)))[0]
 
 
-def finish_kernel(count, part, own, core, x, corex, b2, _, out, rows):
+def finish_kernel(count, part, own, core, x, corex, b2, _, out):
     n = own.shape[0] // 2
     pos = lax.axis_index("span")
     done = []
     for side in range(2):
-        for q, ref in enumerate((own, core, x, corex)):
-            rows[side, q * n : (q + 1) * n] = ref[n:] if side == 0 else ref[:n]
-        s = dot_t(b2[side * n : (side + 1) * n], rows[side]) * LOGIT_SCALE
+        half = slice(n, 2 * n) if side == 0 else slice(0, n)
+        rows = jnp.concatenate([ref[half] for ref in (own, core, x, corex)])
+        s = dot_t(b2[side * n : (side + 1) * n], rows) * LOGIT_SCALE
         before = part[side : side + 1]
         top = jnp.maximum(before, jnp.max(s, axis=0, keepdims=True))
         lse = top + jnp.log(jnp.exp(before - top) + jnp.sum(jnp.exp(s - top), axis=0, keepdims=True))
@@ -131,7 +131,7 @@
             out[b * SPANS + to] = v
             return 0
 
-        lax.fori_loop(0, count, store, 0)
+        lax.fori_loop(0, count, store, 0, unroll=count <= 16)
 
 
 def grad_kernel(count, *refs):
@@ -179,6 +179,7 @@
                 j = lax.broadcasted_iota(jnp.int32, s.shape, 1)
                 w = w - ((i == j) & (i < n)).astype(F32)
             weights[side, :, k * 2 * n : (k + 1) * 2 * n] = w.astype(BF16)
+    for side in range(2):
         total = LOGIT_SCALE * jnp.dot(
             weights[side], cols[side].reshape(STEPS * 2 * n, cols.shape[-1]), preferred_element_type=F32
         )
@@ -220,7 +221,7 @@
     send = call(
         functools.partial(finish_kernel, count),
         jax.ShapeDtypeStruct((count * SPANS, 2 * SPANS, n), F32),
-        [pltpu.VMEM((2, SPANS * n, width), BF16)],
+        [],
         4 * SPANS * n * n * width,
         part, own, core, x, corex, b2, seen, remote=(6,),
     )

time: 50.3 us -> 50.1 us (level)
  no operation moved by 1% of the time
where the time goes in v10:
time: 50.1 us; the launch traced here: 49.8 us
  starting transfers between devices  24 us (48%)
  waiting for transfers between devices  17.6 us (35%)
  Pallas kernels  6.39 us (13%)
  other arithmetic  1.09 us (2%)
  between operations  0.76 us (2%)
    ppermute x13, starting transfers between devices, moved(): return lax.ppermute(value, AXES, pairs)  21 us
    ppermute x13, waiting for transfers between devices, moved(): return lax.ppermute(value, AXES, pairs)  10.4 us
    all_to_all x1, waiting for transfers between devices, body(): got = lax.all_to_all(send, AXES, 0, 0, tiled=True)  7.16 us
    pallas_call x5, Pallas kernels, call(): pl.pallas_call(kernel, out_shape=out_shape, in_specs=[pl.BlockSpec(memory...  6.39 us
    all_to_all x1, starting transfers between devices, body(): got = lax.all_to_all(send, AXES, 0, 0, tiled=True)  2.96 us
    convert_element_type x2, other arithmetic, body(): i0, t0 = (image_embeds.astype(BF16), text_embeds.astype(BF16))  1.09 us
  transfers between devices with their start and end apart: 14, of which 6 were waited for; matrix products, arithmetic and copies ran while one was open for 0% of the time, Pallas kernels for 5%

profile of v10, /device:TPU:0, one launch (start us, length us, event | category | flops | bytes accessed | tf_op | source)
XLA Modules:
  0.0 49.8 jit_solution(2470135569051784282)
XLA Ops:
  0.6 1.1 %convert_element_type.6.text = bf16[128,768]{1,0:T(8,128)(2,1)S(1)} convert(f32[128,768]{1,0:T(8,128)} %param.3) | non-fusion elementwise | flops 98304 | bytes 589824 | tf_op jit(solution)/shard_map/convert_element_type | solution.py:200
  1.7 3.1 %collective-permute-start = (bf16[128,768]{1,0:T(8,128)(2,1)S(1)}, bf16[128,768]{1,0:T(8,128)(2,1)S(1)}, u32[]{:S(2)}, u32[]{:S(2)}) collective-permute-start(bf16[128,768]{1,0:T(8,128)(2,1)S(1)} %convert_element_type.6.text), channel_id=1, source_target_pairs={{0,8},{1,9},{2,10},{3,11},{4,12},{5,13},{6,14},{7,15},{8,16},{9,17... | collective-permute-start | bytes 589832 | tf_op jit(solution)/shard_map/ppermute | solution.py:25
  4.8 2.1 %collective-permute-start.1 = (bf16[128,768]{1,0:T(8,128)(2,1)S(1)}, bf16[128,768]{1,0:T(8,128)(2,1)S(1)}, u32[]{:S(2)}, u32[]{:S(2)}) collective-permute-start(bf16[128,768]{1,0:T(8,128)(2,1)S(1)} %convert_element_type.7.image), channel_id=1, source_target_pairs={{0,24},{1,25},{2,26},{3,27},{4,28},{5,29},{6,30},{7,31},{8,0},{9,1... | collective-permute-start | bytes 589832 | tf_op jit(solution)/shard_map/ppermute | solution.py:25
  7.0 1.8 %collective-permute-start.4 = (bf16[256,768]{1,0:T(8,128)(2,1)S(1)}, bf16[256,768]{1,0:T(8,128)(2,1)S(1)}, u32[]{:S(2)}, u32[]{:S(2)}) collective-permute-start(bf16[256,768]{1,0:T(8,128)(2,1)S(1)} %get-tuple-element.16.own.refs_1_), channel_id=1, source_target_pairs={{0,2},{1,3},{2,0},{3,1},{4,6},{5,7},{6,4},{7,5},{8,10},{9,11},{10,... | collective-permute-start | bytes 1179656 | tf_op jit(solution)/shard_map/ppermute | solution.py:25
  8.7 1.5 %collective-permute-start.6 = (bf16[128,768]{1,0:T(8,128)(2,1)S(1)}, bf16[128,768]{1,0:T(8,128)(2,1)S(1)}, u32[]{:S(2)}, u32[]{:S(2)}) collective-permute-start(bf16[128,768]{1,0:T(8,128)(2,1)S(1)} %get-tuple-element.17), channel_id=1, source_target_pairs={{0,4},{1,5},{2,6},{3,7},{4,0},{5,1},{6,2},{7,3},{8,12},{9,13},{10,... | collective-permute-start | bytes 589832 | tf_op jit(solution)/shard_map/ppermute | solution.py:25
  10.3 2.3 %collective-permute-done = bf16[128,768]{1,0:T(8,128)(2,1)S(1)} collective-permute-done((bf16[128,768]{1,0:T(8,128)(2,1)S(1)}, bf16[128,768]{1,0:T(8,128)(2,1)S(1)}, u32[]{:S(2)}, u32[]{:S(2)}) %collective-permute-start) | collective-permute-done | bytes 196640 | tf_op jit(solution)/shard_map/ppermute | solution.py:25
  12.6 7.1 %collective-permute-start.7 = (bf16[128,768]{1,0:T(8,128)(2,1)S(1)}, bf16[128,768]{1,0:T(8,128)(2,1)S(1)}, u32[]{:S(2)}, u32[]{:S(2)}) collective-permute-start(bf16[128,768]{1,0:T(8,128)(2,1)S(1)} %get-tuple-element.18), channel_id=1, source_target_pairs={{0,20},{1,21},{2,22},{3,23},{4,16},{5,17},{6,18},{7,19},{8,28},{9,... | collective-permute-start | bytes 589832 | tf_op jit(solution)/shard_map/ppermute | solution.py:25
  19.8 0.1 collective-permute-start.8
  19.9 2.0 %collective-permute-start.2 = (bf16[256,768]{1,0:T(8,128)(2,1)S(1)}, bf16[256,768]{1,0:T(8,128)(2,1)S(1)}, u32[]{:S(2)}, u32[]{:S(2)}) collective-permute-start(bf16[256,768]{1,0:T(8,128)(2,1)S(1)} %constant_dynamic-update-slice_fusion.ab.refs_4_), channel_id=1, source_target_pairs={{0,2},{1,3},{2,0},{3,1},{4,6},{5,7},{6,4},{7,5},{8,10},{9,11},{10,... | collective-permute-start | bytes 1179656 | tf_op jit(solution)/shard_map/ppermute | solution.py:25
  21.9 0.1 collective-permute-start.5
  21.9 3.5 %collective-permute-done.7 = bf16[128,768]{1,0:T(8,128)(2,1)S(1)} collective-permute-done((bf16[128,768]{1,0:T(8,128)(2,1)S(1)}, bf16[128,768]{1,0:T(8,128)(2,1)S(1)}, u32[]{:S(2)}, u32[]{:S(2)}) %collective-permute-start.7) | collective-permute-done | bytes 196640 | tf_op jit(solution)/shard_map/ppermute | solution.py:25
  25.4 0.1 collective-permute-start.9
  25.5 1.6 %collective-permute-start.11 = (bf16[256,768]{1,0:T(8,128)(2,1)S(1)}, bf16[256,768]{1,0:T(8,128)(2,1)S(1)}, u32[]{:S(2)}, u32[]{:S(2)}) collective-permute-start(bf16[256,768]{1,0:T(8,128)(2,1)S(1)} %constant_dynamic-update-slice_fusion.2.pc.refs_6_), channel_id=1, source_target_pairs={{0,2},{1,3},{2,0},{3,1},{4,6},{5,7},{6,4},{7,5},{8,10},{9,11},{10,... | collective-permute-start | bytes 1179656 | tf_op jit(solution)/shard_map/ppermute | solution.py:25
  27.1 1.1 %shard_map.58.part = f32[2,512]{1,0:T(2,128)S(1)} custom-call(bf16[256,768]{1,0:T(8,128)(2,1)S(1)} %get-tuple-element.16.own.refs_1_, bf16[256,768]{1,0:T(8,128)(2,1)S(1)} %collective-permute-done.3.core.refs_2_, bf16[256,768]{1,0:T(8,128)(2,1)S(1)} %collective-permute-done.4.x.refs_3_, bf16[256,768]{1,0:T(8,128)(2,1)S(1)} %collective-permute-done.5.corex, ...), custom_call_target="tpu_custom_call" | custom-call | flops 603979776 | bytes 2359296 | tf_op jit(solution)/shard_map/pallas_call | solution.py:59
  28.2 2.0 %collective-permute-done.8.b2.refs_5_ = bf16[256,768]{1,0:T(8,128)(2,1)S(1)} collective-permute-done((bf16[256,768]{1,0:T(8,128)(2,1)S(1)}, bf16[256,768]{1,0:T(8,128)(2,1)S(1)}, u32[]{:S(2)}, u32[]{:S(2)}) %collective-permute-start.8) | collective-permute-done | bytes 393248 | tf_op jit(solution)/shard_map/ppermute | solution.py:25
  30.2 1.4 %shard_map.59 = f32[32,8,128]{2,1,0:T(8,128)} custom-call(f32[2,512]{1,0:T(2,128)S(1)} %shard_map.58.part, bf16[256,768]{1,0:T(8,128)(2,1)S(1)} %get-tuple-element.16.own.refs_1_, bf16[256,768]{1,0:T(8,128)(2,1)S(1)} %collective-permute-done.3.core.refs_2_, bf16[256,768]{1,0:T(8,128)(2,1)S(1)} %collective-permute-done.4.x.refs_3_, ...), custom_call_target="tpu_custom_call" | custom-call | flops 201326592 | bytes 2363392 | tf_op jit(solution)/shard_map/pallas_call | solution.py:59
  31.6 1.4 %collective-permute-start.10 = (bf16[256,768]{1,0:T(8,128)(2,1)S(1)}, bf16[256,768]{1,0:T(8,128)(2,1)}, u32[]{:S(2)}, u32[]{:S(2)}) collective-permute-start(bf16[256,768]{1,0:T(8,128)(2,1)S(1)} %collective-permute-done.2.refs_7_), channel_id=1, source_target_pairs={{0,4},{1,5},{2,6},{3,7},{4,0},{5,1},{6,2},{7,3},{8,12},{9,13},{10,... | collective-permute-start | bytes 1179656 | tf_op jit(solution)/shard_map/ppermute | solution.py:25
  33.0 3.0 %all-to-all-start = ((f32[32,8,128]{2,1,0:T(8,128)}), f32[32,8,128]{2,1,0:T(8,128)S(1)}, u32[]{:S(2)}, u32[]{:S(2)}) async-start(f32[32,8,128]{2,1,0:T(8,128)} %shard_map.59), calls=%async_computation | async-start | bytes 262144 | tf_op jit(solution)/shard_map/all_to_all | solution.py:229
  36.0 1.1 %collective-permute-done.11.refs_9_ = bf16[256,768]{1,0:T(8,128)(2,1)S(1)} collective-permute-done((bf16[256,768]{1,0:T(8,128)(2,1)S(1)}, bf16[256,768]{1,0:T(8,128)(2,1)S(1)}, u32[]{:S(2)}, u32[]{:S(2)}) %collective-permute-start.11) | collective-permute-done | bytes 393248 | tf_op jit(solution)/shard_map/ppermute | solution.py:25
  37.0 7.2 %all-to-all-done.refs_0_ = f32[32,8,128]{2,1,0:T(8,128)S(1)} async-done(((f32[32,8,128]{2,1,0:T(8,128)}), f32[32,8,128]{2,1,0:T(8,128)S(1)}, u32[]{:S(2)}, u32[]{:S(2)}) %all-to-all-start) | async-done | bytes 131104 | tf_op jit(solution)/shard_map/all_to_all | solution.py:229
  44.2 2.9 %shard_map.60 = (f32[128]{0:T(128)}, f32[128]{0:T(128)}, f32[2,128,768]{2,1,0:T(8,128)S(1)}, bf16[2,128,768]{2,1,0:T(8,128)(2,1)S(1)}) custom-call(f32[32,8,128]{2,1,0:T(8,128)S(1)} %all-to-all-done.refs_0_, bf16[256,768]{1,0:T(8,128)(2,1)S(1)} %get-tuple-element.16.own.refs_1_, bf16[256,768]{1,0:T(8,128)(2,1)S(1)} %collective-permute-done.3.core.refs_2_, ...), custom_call_target="tpu_custom_call" | custom-call | flops 1610612736 | bytes 3670016 | tf_op jit(solution)/shard_map/pallas_call | solution.py:59
  47.1 0.3 collective-permute-start.12
  47.4 1.5 %collective-permute-done.12.got = bf16[2,128,768]{2,1,0:T(8,128)(2,1)S(1)} collective-permute-done((bf16[2,128,768]{2,1,0:T(8,128)(2,1)S(1)}, bf16[2,128,768]{2,1,0:T(8,128)(2,1)S(1)}, u32[]{:S(2)}, u32[]{:S(2)}) %collective-permute-start.12) | collective-permute-done | bytes 393248 | tf_op jit(solution)/shard_map/ppermute | solution.py:25
  48.9 0.9 %shard_map.61 = (f32[128,768]{1,0:T(8,128)}, f32[128,768]{1,0:T(8,128)}) custom-call(f32[2,128,768]{2,1,0:T(8,128)S(1)} %get-tuple-element.24.kept, bf16[2,128,768]{2,1,0:T(8,128)(2,1)S(1)} %collective-permute-done.12.got), custom_call_target="tpu_custom_call" | custom-call | bytes 1179648 | tf_op jit(solution)/shard_map/pallas_call | solution.py:59
  (17 shorter events, 0.2 us)
Async XLA Ops:
  0.6 4.2 %copy-start = (f32[128,768]{1,0:T(8,128)S(1)}, f32[128,768]{1,0:T(8,128)}, u32[]{:S(2)}) copy-start(f32[128,768]{1,0:T(8,128)} %param.2) | copy-start | bytes 1179652
  1.7 10.9 %collective-permute-start = (bf16[128,768]{1,0:T(8,128)(2,1)S(1)}, bf16[128,768]{1,0:T(8,128)(2,1)S(1)}, u32[]{:S(2)}, u32[]{:S(2)}) collective-permute-start(bf16[128,768]{1,0:T(8,128)(2,1)S(1)} %convert_element_type.6.text), channel_id=1, source_target_pairs={{0,8},{1,9},{2,10},{3,11},{4,12},{5,13},{6,14},{7,15},{8,16},{9,17... | collective-permute-start | bytes 589832 | tf_op jit(solution)/shard_map/ppermute | solution.py:25
  4.8 14.9 %collective-permute-start.1 = (bf16[128,768]{1,0:T(8,128)(2,1)S(1)}, bf16[128,768]{1,0:T(8,128)(2,1)S(1)}, u32[]{:S(2)}, u32[]{:S(2)}) collective-permute-start(bf16[128,768]{1,0:T(8,128)(2,1)S(1)} %convert_element_type.7.image), channel_id=1, source_target_pairs={{0,24},{1,25},{2,26},{3,27},{4,28},{5,29},{6,30},{7,31},{8,0},{9,1... | collective-permute-start | bytes 589832 | tf_op jit(solution)/shard_map/ppermute | solution.py:25
  7.0 14.9 %collective-permute-start.4 = (bf16[256,768]{1,0:T(8,128)(2,1)S(1)}, bf16[256,768]{1,0:T(8,128)(2,1)S(1)}, u32[]{:S(2)}, u32[]{:S(2)}) collective-permute-start(bf16[256,768]{1,0:T(8,128)(2,1)S(1)} %get-tuple-element.16.own.refs_1_), channel_id=1, source_target_pairs={{0,2},{1,3},{2,0},{3,1},{4,6},{5,7},{6,4},{7,5},{8,10},{9,11},{10,... | collective-permute-start | bytes 1179656 | tf_op jit(solution)/shard_map/ppermute | solution.py:25
  8.7 16.8 %collective-permute-start.3 = (bf16[256,768]{1,0:T(8,128)(2,1)S(1)}, bf16[256,768]{1,0:T(8,128)(2,1)S(1)}, u32[]{:S(2)}, u32[]{:S(2)}) collective-permute-start(bf16[256,768]{1,0:T(8,128)(2,1)S(1)} %get-tuple-element.16.own.refs_1_), channel_id=1, source_target_pairs={{0,1},{1,0},{2,3},{3,2},{4,5},{5,4},{6,7},{7,6},{8,9},{9,8},{10,11... | collective-permute-start | bytes 1179656 | tf_op jit(solution)/shard_map/ppermute | solution.py:25
  8.7 11.1 %collective-permute-start.6 = (bf16[128,768]{1,0:T(8,128)(2,1)S(1)}, bf16[128,768]{1,0:T(8,128)(2,1)S(1)}, u32[]{:S(2)}, u32[]{:S(2)}) collective-permute-start(bf16[128,768]{1,0:T(8,128)(2,1)S(1)} %get-tuple-element.17), channel_id=1, source_target_pairs={{0,4},{1,5},{2,6},{3,7},{4,0},{5,1},{6,2},{7,3},{8,12},{9,13},{10,... | collective-permute-start | bytes 589832 | tf_op jit(solution)/shard_map/ppermute | solution.py:25
  12.6 12.8 %collective-permute-start.7 = (bf16[128,768]{1,0:T(8,128)(2,1)S(1)}, bf16[128,768]{1,0:T(8,128)(2,1)S(1)}, u32[]{:S(2)}, u32[]{:S(2)}) collective-permute-start(bf16[128,768]{1,0:T(8,128)(2,1)S(1)} %get-tuple-element.18), channel_id=1, source_target_pairs={{0,20},{1,21},{2,22},{3,23},{4,16},{5,17},{6,18},{7,19},{8,28},{9,... | collective-permute-start | bytes 589832 | tf_op jit(solution)/shard_map/ppermute | solution.py:25
  19.8 10.5 %collective-permute-start.8 = (bf16[256,768]{1,0:T(8,128)(2,1)S(1)}, bf16[256,768]{1,0:T(8,128)(2,1)S(1)}, u32[]{:S(2)}, u32[]{:S(2)}) collective-permute-start(bf16[256,768]{1,0:T(8,128)(2,1)S(1)} %constant_dynamic-update-slice_fusion.ab.refs_4_), channel_id=1, source_target_pairs={{0,4},{1,5},{2,6},{3,7},{4,0},{5,1},{6,2},{7,3},{8,12},{9,13},{10,... | collective-permute-start | bytes 1179656 | tf_op jit(solution)/shard_map/ppermute | solution.py:25
  19.9 8.3 %collective-permute-start.2 = (bf16[256,768]{1,0:T(8,128)(2,1)S(1)}, bf16[256,768]{1,0:T(8,128)(2,1)S(1)}, u32[]{:S(2)}, u32[]{:S(2)}) collective-permute-start(bf16[256,768]{1,0:T(8,128)(2,1)S(1)} %constant_dynamic-update-slice_fusion.ab.refs_4_), channel_id=1, source_target_pairs={{0,2},{1,3},{2,0},{3,1},{4,6},{5,7},{6,4},{7,5},{8,10},{9,11},{10,... | collective-permute-start | bytes 1179656 | tf_op jit(solution)/shard_map/ppermute | solution.py:25
  21.9 5.2 %collective-permute-start.5 = (bf16[256,768]{1,0:T(8,128)(2,1)S(1)}, bf16[256,768]{1,0:T(8,128)(2,1)S(1)}, u32[]{:S(2)}, u32[]{:S(2)}) collective-permute-start(bf16[256,768]{1,0:T(8,128)(2,1)S(1)} %collective-permute-done.4.x.refs_3_), channel_id=1, source_target_pairs={{0,1},{1,0},{2,3},{3,2},{4,5},{5,4},{6,7},{7,6},{8,9},{9,8},{10,11... | collective-permute-start | bytes 1179656 | tf_op jit(solution)/shard_map/ppermute | solution.py:25
  25.4 4.8 %collective-permute-start.9 = (bf16[256,768]{1,0:T(8,128)(2,1)S(1)}, bf16[256,768]{1,0:T(8,128)(2,1)S(1)}, u32[]{:S(2)}, u32[]{:S(2)}) collective-permute-start(bf16[256,768]{1,0:T(8,128)(2,1)S(1)} %constant_dynamic-update-slice_fusion.2.pc.refs_6_), channel_id=1, source_target_pairs={{0,1},{1,0},{2,3},{3,2},{4,5},{5,4},{6,7},{7,6},{8,9},{9,8},{10,11... | collective-permute-start | bytes 1179656 | tf_op jit(solution)/shard_map/ppermute | solution.py:25
  25.5 11.5 %collective-permute-start.11 = (bf16[256,768]{1,0:T(8,128)(2,1)S(1)}, bf16[256,768]{1,0:T(8,128)(2,1)S(1)}, u32[]{:S(2)}, u32[]{:S(2)}) collective-permute-start(bf16[256,768]{1,0:T(8,128)(2,1)S(1)} %constant_dynamic-update-slice_fusion.2.pc.refs_6_), channel_id=1, source_target_pairs={{0,2},{1,3},{2,0},{3,1},{4,6},{5,7},{6,4},{7,5},{8,10},{9,11},{10,... | collective-permute-start | bytes 1179656 | tf_op jit(solution)/shard_map/ppermute | solution.py:25
  31.6 12.6 %collective-permute-start.10 = (bf16[256,768]{1,0:T(8,128)(2,1)S(1)}, bf16[256,768]{1,0:T(8,128)(2,1)}, u32[]{:S(2)}, u32[]{:S(2)}) collective-permute-start(bf16[256,768]{1,0:T(8,128)(2,1)S(1)} %collective-permute-done.2.refs_7_), channel_id=1, source_target_pairs={{0,4},{1,5},{2,6},{3,7},{4,0},{5,1},{6,2},{7,3},{8,12},{9,13},{10,... | collective-permute-start | bytes 1179656 | tf_op jit(solution)/shard_map/ppermute | solution.py:25
  33.0 11.2 %all-to-all-start = ((f32[32,8,128]{2,1,0:T(8,128)}), f32[32,8,128]{2,1,0:T(8,128)S(1)}, u32[]{:S(2)}, u32[]{:S(2)}) async-start(f32[32,8,128]{2,1,0:T(8,128)} %shard_map.59), calls=%async_computation | async-start | bytes 262144 | tf_op jit(solution)/shard_map/all_to_all | solution.py:229
  47.1 1.8 %collective-permute-start.12 = (bf16[2,128,768]{2,1,0:T(8,128)(2,1)S(1)}, bf16[2,128,768]{2,1,0:T(8,128)(2,1)S(1)}, u32[]{:S(2)}, u32[]{:S(2)}) collective-permute-start(bf16[2,128,768]{2,1,0:T(8,128)(2,1)S(1)} %get-tuple-element.25), channel_id=1, source_target_pairs={{0,1},{1,0},{2,3},{3,2},{4,5},{5,4},{6,7},{7,6},{8,9},{9,8},{10,11... | collective-permute-start | bytes 1179656 | tf_op jit(solution)/shard_map/ppermute | solution.py:25
